TPU v7x, 32 devices: a whole 2x2x4 slice. The times are simulated.
32 devices in a mesh: dp: 8 (over y, x, core), expert: 4 (over z).
Axes of the slice: x: 2, y: 2, z: 4, core: 2. Of those that a mesh axis runs over, the one named last changes fastest.
Arguments:
- tokens: bfloat16 [2, 8192, 1536], P(None, ('dp', 'expert')), may hold values from -6 to 6
- out_grad: bfloat16 [2, 8192, 1536], P(None, ('dp', 'expert')), may hold values from -6 to 6
- routes: int32 [2, 8192, 8], P(None, ('dp', 'expert')), may hold values from 0 to 39, all different within a row; in each aligned block of 256 rows (0 to 255, 256 to 511, ..., all dimensions but the last counted through in order) at most 64 rows name the same one
- attn_gain: bfloat16 [1536], P('dp'), may hold values from 0.5 to 1.5
- w_query: bfloat16 [1536, 1536], P('dp'), may hold values from -0.21875 to 0.21875
- w_key: bfloat16 [1536, 512], P('dp'), may hold values from -0.21875 to 0.21875
- w_value: bfloat16 [1536, 512], P('dp'), may hold values from -0.15625 to 0.15625
- w_out: bfloat16 [1536, 1536], P('dp'), may hold values from -1.25 to 1.25
- moe_gain: bfloat16 [1536], P('dp'), may hold values from 0.5 to 1.5
- w_router: bfloat16 [1536, 40], P('dp'), may hold values from -0.078125 to 0.078125
- w_gate: bfloat16 [40, 1536, 512], P('expert'), may hold values from -0.15625 to 0.15625
- w_up: bfloat16 [40, 1536, 512], P('expert'), may hold values from -0.15625 to 0.15625
- w_down: bfloat16 [40, 512, 1536], P('expert'), may hold values from -1 to 1
Outputs:
- mixed: bfloat16 [2, 8192, 1536], P(None, ('dp', 'expert'))
- grad_tokens: float32 [2, 8192, 1536], P(None, ('dp', 'expert'))
- grad_attn_gain: float32 [1536], P('dp')
- grad_query: float32 [1536, 1536], P('dp')
- grad_key: float32 [1536, 512], P('dp')
- grad_value: float32 [1536, 512], P('dp')
- grad_out: float32 [1536, 1536], P('dp')
- grad_moe_gain: float32 [1536], P('dp')
- grad_router: float32 [1536, 40], P('dp')
- grad_gate: float32 [40, 1536, 512], P('expert', 'dp')
- grad_up: float32 [40, 1536, 512], P('expert', 'dp')
- grad_down: float32 [40, 512, 1536], P('expert', 'dp')
Inputs may be any that keep to these rules, and one draw needn't show every extreme that they name: `routes`: each row names 8 different experts; in each aligned block of 256 rows (one device's tokens of one micro-batch) no expert is named by more than 64 rows, a bound that some block reaches.
All inputs are finite; a program needn't handle non-finite values.
Results may differ from a plain program's by a relative error of at most 0.024.
Values may be sent and summed in bfloat16 or wider, within the bound.
No kernel may reach another device: no remote copies, remote signals or barrier semaphores. Data moves between devices by JAX's collectives and lax.ppermute only.
A program may use at most 576 MiB of HBM per device.

v0:
```python
from functools import partial

import jax
import jax.numpy as jnp
from jax import lax
from jax.sharding import PartitionSpec as P

HEADS = 24
KV_HEADS = 8
HEAD = 64
FF = 512
EXPERTS = 40
TOP = 8
BLOCK = 256
SEQ = 1024
CAP = 64
QD = 1536
KD = 512


EPSILON = 1e-06
ROPE_BASE = 10000.0
NEGATIVE = -1e30


def dense_dot(left, right):
    return jnp.dot(left, right, preferred_element_type=jnp.float32)


def left_dot(left, right):
    return lax.dot_general(
        left, right, (((0,), (0,)), ((), ())), preferred_element_type=jnp.float32
    )


def right_dot(left, right):
    return lax.dot_general(
        left, right, (((1,), (1,)), ((), ())), preferred_element_type=jnp.float32
    )


def rotary_tables(positions):
    half_size = HEAD // 2
    frequency = ROPE_BASE ** (-jnp.arange(half_size, dtype=jnp.float32) / half_size)
    angle = positions.astype(jnp.float32)[:, None] * frequency[None, :]
    return (jnp.cos(angle)[:, None, :], jnp.sin(angle)[:, None, :])


def rotate(values, cosine, sine):
    half_size = values.shape[-1] // 2
    first, second = (values[..., :half_size], values[..., half_size:])
    return jnp.concatenate(
        [first * cosine - second * sine, second * cosine + first * sine], axis=-1
    )


def unrotate(grads, cosine, sine):
    half_size = grads.shape[-1] // 2
    first, second = (grads[..., :half_size], grads[..., half_size:])
    return jnp.concatenate(
        [first * cosine + second * sine, second * cosine - first * sine], axis=-1
    )


def online_step(carried, query_rows, key_rows, value_rows, score_scale):
    running_max, running_sum, running_out = carried
    scores = (
        jnp.einsum("qgrd,kgd->grqk", query_rows, key_rows, preferred_element_type=jnp.float32)
        * score_scale
    )
    new_max = jnp.maximum(running_max, jnp.max(scores, axis=-1))
    factor = jnp.exp(running_max - new_max)
    weights = jnp.exp(scores - new_max[..., None])
    running_sum = running_sum * factor + jnp.sum(weights, axis=-1)
    running_out = running_out * factor[..., None] + jnp.einsum(
        "grqk,kgd->grqd",
        weights.astype(jnp.bfloat16),
        value_rows,
        preferred_element_type=jnp.float32,
    )
    return (new_max, running_sum, running_out)


def keep_state(carried):
    return carried


def local(
    tokens,
    out_grad,
    routes,
    attn_gain,
    w_query,
    w_key,
    w_value,
    w_out,
    moe_gain,
    w_router,
    w_gate,
    w_up,
    w_down,
):
    features = tokens.shape[2]
    expert_count = lax.axis_size("expert")
    own_rank = lax.axis_index("expert")
    exp_dev = w_gate.shape[0]
    repeat = HEADS // KV_HEADS
    score_scale = HEAD ** (-0.5)
    seq_blocks = SEQ // BLOCK
    place_in_seq = own_rank % seq_blocks
    first_block = own_rank - place_in_seq
    cosine, sine = rotary_tables(place_in_seq * BLOCK + jnp.arange(BLOCK, dtype=jnp.int32))

    def micro_step(carried, inputs):
        dense_acc, expert_acc = carried
        x_block, dy_block, route_block = inputs
        whole = (
            lax.all_gather(w_query, "dp", axis=0, tiled=True),
            lax.all_gather(w_key, "dp", axis=0, tiled=True),
            lax.all_gather(w_value, "dp", axis=0, tiled=True),
            lax.all_gather(w_out, "dp", axis=0, tiled=True),
            lax.all_gather(w_router, "dp", axis=0, tiled=True),
            lax.all_gather(attn_gain, "dp", axis=0, tiled=True),
            lax.all_gather(moe_gain, "dp", axis=0, tiled=True),
        )
        query_w, key_w, value_w, out_w, router_w, gain_one, gain_two = whole
        gain_one = gain_one.astype(jnp.float32)
        gain_two = gain_two.astype(jnp.float32)
        x_rows = x_block.astype(jnp.float32)
        inverse_one = lax.rsqrt(jnp.mean(x_rows * x_rows, axis=-1, keepdims=True) + EPSILON)
        normed = (x_rows * inverse_one * gain_one).astype(jnp.bfloat16)
        query_f = dense_dot(normed, query_w).reshape(BLOCK, HEADS, HEAD)
        key_f = dense_dot(normed, key_w).reshape(BLOCK, KV_HEADS, HEAD)
        value_b = dense_dot(normed, value_w).astype(jnp.bfloat16)
        query_b = (
            rotate(query_f, cosine, sine)
            .astype(jnp.bfloat16)
            .reshape(BLOCK, KV_HEADS, repeat, HEAD)
        )
        key_b = rotate(key_f, cosine, sine).astype(jnp.bfloat16).reshape(BLOCK, KD)
        start_state = (
            jnp.full((KV_HEADS, repeat, BLOCK), NEGATIVE, jnp.float32),
            jnp.zeros((KV_HEADS, repeat, BLOCK), jnp.float32),
            jnp.zeros((KV_HEADS, repeat, BLOCK, HEAD), jnp.float32),
        )
        state = start_state
        start = jnp.int32(0)
        key_piece = lax.all_gather(key_b, "expert", axis=0, tiled=True)
        value_piece = lax.all_gather(value_b, "expert", axis=0, tiled=True)
        for piece_index in range(key_piece.shape[0] // BLOCK):
            key_rows = key_piece[piece_index * BLOCK : (piece_index + 1) * BLOCK].reshape(
                BLOCK, KV_HEADS, HEAD
            )
            value_rows = value_piece[piece_index * BLOCK : (piece_index + 1) * BLOCK].reshape(
                BLOCK, KV_HEADS, HEAD
            )
            key_block = start // BLOCK + piece_index
            seen = jnp.logical_and(key_block >= first_block, key_block <= own_rank)
            update = partial(
                online_step,
                query_rows=query_b,
                key_rows=key_rows,
                value_rows=value_rows,
                score_scale=score_scale,
            )
            state = lax.cond(seen, update, keep_state, state)
        running_max, running_sum, running_out = state
        out_four = running_out / running_sum[..., None]
        log_total = running_max + jnp.log(running_sum)
        out_b = jnp.transpose(out_four, (2, 0, 1, 3)).reshape(BLOCK, QD).astype(jnp.bfloat16)
        mid = x_rows + dense_dot(out_b, out_w)
        inverse_two = lax.rsqrt(jnp.mean(mid * mid, axis=-1, keepdims=True) + EPSILON)
        normed_two = (mid * inverse_two * gain_two).astype(jnp.bfloat16)
        logits = dense_dot(normed_two, router_w)
        route_table = route_block[:, :, None] == jnp.arange(EXPERTS, dtype=jnp.int32)[None, None, :]
        table_float = route_table.astype(jnp.float32)
        chosen = jnp.sum(table_float * logits[:, None, :], axis=-1)
        gate_weights = jax.nn.softmax(chosen, axis=-1)
        onehot = route_table.reshape(BLOCK * TOP, EXPERTS).astype(jnp.int32)
        earlier = jnp.cumsum(onehot, axis=0) - onehot
        slot_index = jnp.sum(earlier * onehot, axis=-1)
        target = route_block.reshape(-1) * CAP + slot_index
        outgoing = (
            jnp.zeros((EXPERTS * CAP, features), jnp.bfloat16)
            .at[target]
            .set(jnp.repeat(normed_two, TOP, axis=0))
        )
        arrived = lax.all_to_all(
            outgoing.reshape(expert_count, exp_dev, CAP, features),
            "expert",
            split_axis=0,
            concat_axis=2,
            tiled=True,
        )
        inbound = arrived.reshape(exp_dev, expert_count * CAP, features)
        gate_pre = jnp.einsum("erd,edf->erf", inbound, w_gate, preferred_element_type=jnp.float32)
        up_pre = jnp.einsum("erd,edf->erf", inbound, w_up, preferred_element_type=jnp.float32)
        active = (jax.nn.silu(gate_pre) * up_pre).astype(jnp.bfloat16)
        result = jnp.einsum(
            "erf,efd->erd", active, w_down, preferred_element_type=jnp.float32
        ).astype(jnp.bfloat16)
        returned = lax.all_to_all(
            result.reshape(1, exp_dev, expert_count * CAP, features),
            "expert",
            split_axis=2,
            concat_axis=0,
            tiled=True,
        )
        back_rows = returned.reshape(EXPERTS * CAP, features)[target].reshape(BLOCK, TOP, features)
        mixture = jnp.sum(gate_weights[:, :, None] * back_rows, axis=1)
        output = (mid + mixture).astype(jnp.bfloat16)
        grad_y = dy_block.astype(jnp.float32)
        grad_gates = jnp.sum(grad_y[:, None, :] * back_rows, axis=-1)
        grad_rows = (
            (gate_weights[:, :, None] * grad_y[:, None, :])
            .astype(jnp.bfloat16)
            .reshape(BLOCK * TOP, features)
        )
        grad_outgoing = jnp.zeros((EXPERTS * CAP, features), jnp.bfloat16).at[target].set(grad_rows)
        grad_in = lax.all_to_all(
            grad_outgoing.reshape(expert_count, exp_dev, CAP, features),
            "expert",
            split_axis=0,
            concat_axis=2,
            tiled=True,
        ).reshape(exp_dev, expert_count * CAP, features)
        grad_active = jnp.einsum(
            "erd,efd->erf", grad_in, w_down, preferred_element_type=jnp.float32
        )
        sigmoid_gate = jax.nn.sigmoid(gate_pre)
        grad_gate_pre = (
            grad_active * up_pre * sigmoid_gate * (1.0 + gate_pre * (1.0 - sigmoid_gate))
        ).astype(jnp.bfloat16)
        grad_up_pre = (grad_active * gate_pre * sigmoid_gate).astype(jnp.bfloat16)
        new_down = jnp.einsum("erf,erd->efd", active, grad_in, preferred_element_type=jnp.float32)
        new_gate = jnp.einsum(
            "erd,erf->edf", inbound, grad_gate_pre, preferred_element_type=jnp.float32
        )
        new_up = jnp.einsum(
            "erd,erf->edf", inbound, grad_up_pre, preferred_element_type=jnp.float32
        )
        grad_inbound = (
            jnp.einsum("erf,edf->erd", grad_gate_pre, w_gate, preferred_element_type=jnp.float32)
            + jnp.einsum("erf,edf->erd", grad_up_pre, w_up, preferred_element_type=jnp.float32)
        ).astype(jnp.bfloat16)
        grad_back = lax.all_to_all(
            grad_inbound.reshape(1, exp_dev, expert_count * CAP, features),
            "expert",
            split_axis=2,
            concat_axis=0,
            tiled=True,
        )
        grad_pairs = grad_back.reshape(EXPERTS * CAP, features)[target].reshape(
            BLOCK, TOP, features
        )
        grad_normed_two = jnp.sum(grad_pairs, axis=1, dtype=jnp.float32)
        grad_chosen = gate_weights * (
            grad_gates - jnp.sum(gate_weights * grad_gates, axis=-1, keepdims=True)
        )
        grad_logits = jnp.sum(table_float * grad_chosen[:, :, None], axis=1).astype(jnp.bfloat16)
        new_router = left_dot(normed_two, grad_logits)
        grad_normed_two = grad_normed_two + right_dot(grad_logits, router_w)
        new_gain_two = jnp.sum(grad_normed_two * mid * inverse_two, axis=0)
        scaled_two = grad_normed_two * gain_two
        grad_mid = (
            grad_y
            + inverse_two * scaled_two
            - mid * inverse_two**3 * jnp.mean(scaled_two * mid, axis=-1, keepdims=True)
        )
        grad_branch = grad_mid.astype(jnp.bfloat16)
        new_out = left_dot(out_b, grad_branch)
        grad_attn = (
            right_dot(grad_branch, out_w)
            .astype(jnp.bfloat16)
            .reshape(BLOCK, KV_HEADS, repeat, HEAD)
        )
        row_delta = jnp.sum(jnp.transpose(grad_attn, (1, 2, 0, 3)) * out_four, axis=-1)
        keys_whole, values_whole = (
            lax.all_gather(key_b, "expert", axis=0, tiled=True),
            lax.all_gather(value_b, "expert", axis=0, tiled=True),
        )

        def back_block(grad_query, block_index):
            key_rows = lax.dynamic_slice_in_dim(keys_whole, block_index * BLOCK, BLOCK, 0).reshape(
                BLOCK, KV_HEADS, HEAD
            )
            value_rows = lax.dynamic_slice_in_dim(
                values_whole, block_index * BLOCK, BLOCK, 0
            ).reshape(BLOCK, KV_HEADS, HEAD)

            def visible_block(grad_query):
                scores = (
                    jnp.einsum(
                        "qgrd,kgd->grqk", query_b, key_rows, preferred_element_type=jnp.float32
                    )
                    * score_scale
                )
                probabilities = jnp.exp(scores - log_total[..., None])
                grad_probs = jnp.einsum(
                    "qgrd,kgd->grqk", grad_attn, value_rows, preferred_element_type=jnp.float32
                )
                grad_scores = (probabilities * (grad_probs - row_delta[..., None])).astype(
                    jnp.bfloat16
                )
                grad_query = grad_query + score_scale * jnp.einsum(
                    "grqk,kgd->qgrd", grad_scores, key_rows, preferred_element_type=jnp.float32
                )
                grad_keys = score_scale * jnp.einsum(
                    "grqk,qgrd->kgd", grad_scores, query_b, preferred_element_type=jnp.float32
                )
                grad_values = jnp.einsum(
                    "grqk,qgrd->kgd",
                    probabilities.astype(jnp.bfloat16),
                    grad_attn,
                    preferred_element_type=jnp.float32,
                )
                return (grad_query, grad_keys.reshape(BLOCK, KD), grad_values.reshape(BLOCK, KD))

            def skipped_block(grad_query):
                zero_rows = jnp.zeros((BLOCK, KD), jnp.float32)
                return (grad_query, zero_rows, zero_rows)

            seen = jnp.logical_and(block_index >= first_block, block_index <= own_rank)
            grad_query, grad_keys, grad_values = lax.cond(
                seen, visible_block, skipped_block, grad_query
            )
            return (grad_query, (grad_keys, grad_values))

        grad_query, (key_parts, value_parts) = lax.scan(
            back_block,
            jnp.zeros((BLOCK, KV_HEADS, repeat, HEAD), jnp.float32),
            jnp.arange(expert_count, dtype=jnp.int32),
        )
        own_keys, own_values = (
            lax.psum_scatter(
                key_parts.reshape(expert_count * BLOCK, KD).astype(jnp.bfloat16),
                "expert",
                scatter_dimension=0,
                tiled=True,
            ).astype(jnp.float32),
            lax.psum_scatter(
                value_parts.reshape(expert_count * BLOCK, KD).astype(jnp.bfloat16),
                "expert",
                scatter_dimension=0,
                tiled=True,
            ).astype(jnp.float32),
        )
        grad_key_b = (
            unrotate(own_keys.reshape(BLOCK, KV_HEADS, HEAD), cosine, sine)
            .astype(jnp.bfloat16)
            .reshape(BLOCK, KD)
        )
        grad_value_b = own_values.astype(jnp.bfloat16)
        grad_query_b = (
            unrotate(grad_query.reshape(BLOCK, HEADS, HEAD), cosine, sine)
            .astype(jnp.bfloat16)
            .reshape(BLOCK, QD)
        )
        new_query = left_dot(normed, grad_query_b)
        new_key = left_dot(normed, grad_key_b)
        new_value = left_dot(normed, grad_value_b)
        grad_normed = (
            right_dot(grad_query_b, query_w)
            + right_dot(grad_key_b, key_w)
            + right_dot(grad_value_b, value_w)
        )
        new_gain_one = jnp.sum(grad_normed * x_rows * inverse_one, axis=0)
        scaled_one = grad_normed * gain_one
        grad_x = (
            grad_mid
            + inverse_one * scaled_one
            - x_rows * inverse_one**3 * jnp.mean(scaled_one * x_rows, axis=-1, keepdims=True)
        )
        dense_new = (new_query, new_key, new_value, new_out, new_router, new_gain_one, new_gain_two)
        dense_acc = tuple((running + fresh for running, fresh in zip(dense_acc, dense_new)))
        expert_new = (new_gate, new_up, new_down)
        expert_acc = tuple((running + fresh for running, fresh in zip(expert_acc, expert_new)))
        return ((dense_acc, expert_acc), (output, grad_x))

    dense_init = (
        jnp.zeros((features, QD), jnp.float32),
        jnp.zeros((features, KD), jnp.float32),
        jnp.zeros((features, KD), jnp.float32),
        jnp.zeros((QD, features), jnp.float32),
        jnp.zeros((features, EXPERTS), jnp.float32),
        jnp.zeros((features,), jnp.float32),
        jnp.zeros((features,), jnp.float32),
    )
    expert_init = (
        jnp.zeros((exp_dev, features, FF), jnp.float32),
        jnp.zeros((exp_dev, features, FF), jnp.float32),
        jnp.zeros((exp_dev, FF, features), jnp.float32),
    )
    (dense_acc, expert_acc), (mixed, grad_tokens) = lax.scan(
        micro_step, (dense_init, expert_init), (tokens, out_grad, routes)
    )
    expert_acc = (
        lax.psum_scatter(
            expert_acc[0].astype(jnp.bfloat16), "dp", scatter_dimension=1, tiled=True
        ).astype(jnp.float32),
        lax.psum_scatter(
            expert_acc[1].astype(jnp.bfloat16), "dp", scatter_dimension=1, tiled=True
        ).astype(jnp.float32),
        lax.psum_scatter(
            expert_acc[2].astype(jnp.bfloat16), "dp", scatter_dimension=1, tiled=True
        ).astype(jnp.float32),
    )
    dense_shards = (
        lax.psum_scatter(
            dense_acc[0].astype(jnp.bfloat16), "dp", scatter_dimension=0, tiled=True
        ).astype(jnp.float32),
        lax.psum_scatter(
            dense_acc[1].astype(jnp.bfloat16), "dp", scatter_dimension=0, tiled=True
        ).astype(jnp.float32),
        lax.psum_scatter(
            dense_acc[2].astype(jnp.bfloat16), "dp", scatter_dimension=0, tiled=True
        ).astype(jnp.float32),
        lax.psum_scatter(
            dense_acc[3].astype(jnp.bfloat16), "dp", scatter_dimension=0, tiled=True
        ).astype(jnp.float32),
        lax.psum_scatter(
            dense_acc[4].astype(jnp.bfloat16), "dp", scatter_dimension=0, tiled=True
        ).astype(jnp.float32),
        lax.psum_scatter(
            dense_acc[5].astype(jnp.bfloat16), "dp", scatter_dimension=0, tiled=True
        ).astype(jnp.float32),
        lax.psum_scatter(
            dense_acc[6].astype(jnp.bfloat16), "dp", scatter_dimension=0, tiled=True
        ).astype(jnp.float32),
    )
    dense_sum = (
        lax.psum(dense_shards[0].astype(jnp.bfloat16), "expert").astype(jnp.float32),
        lax.psum(dense_shards[1].astype(jnp.bfloat16), "expert").astype(jnp.float32),
        lax.psum(dense_shards[2].astype(jnp.bfloat16), "expert").astype(jnp.float32),
        lax.psum(dense_shards[3].astype(jnp.bfloat16), "expert").astype(jnp.float32),
        lax.psum(dense_shards[4].astype(jnp.bfloat16), "expert").astype(jnp.float32),
        lax.psum(dense_shards[5].astype(jnp.bfloat16), "expert").astype(jnp.float32),
        lax.psum(dense_shards[6].astype(jnp.bfloat16), "expert").astype(jnp.float32),
    )
    return (
        mixed,
        grad_tokens,
        dense_sum[5],
        dense_sum[0],
        dense_sum[1],
        dense_sum[2],
        dense_sum[3],
        dense_sum[6],
        dense_sum[4],
        expert_acc[0],
        expert_acc[1],
        expert_acc[2],
    )


def solution(mesh):
    return jax.shard_map(
        local,
        mesh=mesh,
        in_specs=(
            P(None, ("dp", "expert"), None),
            P(None, ("dp", "expert"), None),
            P(None, ("dp", "expert"), None),
            P("dp"),
            P("dp", None),
            P("dp", None),
            P("dp", None),
            P("dp", None),
            P("dp"),
            P("dp", None),
            P("expert", None, None),
            P("expert", None, None),
            P("expert", None, None),
        ),
        out_specs=(
            P(None, ("dp", "expert"), None),
            P(None, ("dp", "expert"), None),
            P("dp"),
            P("dp", None),
            P("dp", None),
            P("dp", None),
            P("dp", None),
            P("dp"),
            P("dp", None),
            P("expert", "dp", None),
            P("expert", "dp", None),
            P("expert", "dp", None),
        ),
        check_vma=False,
    )
```

profile of v0, /device:TPU:0, one launch (start us, length us, event | category | flops | bytes accessed | tf_op | source)
XLA Modules:
  0.0 3462.5 jit_solution(4602122645446233349)
XLA Ops:
  8.2 2792.2 %while.68 = (s32[]{:T(128)}, f32[1536,1536]{1,0:T(8,128)}, f32[1536,512]{1,0:T(8,128)}, f32[1536,512]{1,0:T(8,128)}, f32[1536,1536]{1,0:T(8,128)}, /*index=5*/f3...) while((s32[]{:T(128)}, f32[1536,1536]{1,0:T(8,128)}, ...), condition=%wide.region_43.44_spmd.clone.clone.clone, body=%wide.region_0.43_spmd.clone.clone.clone.sunk | while | flops 48851050496 | bytes 1325343872 | solution.py:394
  43.1 24.2 all-gather.13.cloned.1.call-done
  86.2 19.8 reduce-window.22
  131.0 37.1 %all-gather.17.cloned.1.call-done = bf16[1536,1536]{1,0:T(8,128)(2,1)} async-done(((bf16[192,1536]{1,0:T(8,128)(2,1)}), bf16[1536,1536]{1,0:T(8,128)(2,1)}) %all-gather.17.cloned.1.call-update) | async-done | bytes 4718608 | tf_op jit(solution)/shard_map/while/body/eval_jaxpr/all_gather | solution.py:118
  254.4 157.6 %all-to-all-done.1 = bf16[4,10,64,1536]{3,2,1,0:T(8,128)(2,1)} async-done(((bf16[4,10,64,1536]{3,2,1,0:T(8,128)(2,1)}), bf16[4,10,64,1536]{3,2,1,0:T(8,128)(2,1)}, u32[]{:S(2)}, u32[]{:S(2)}) %all-to-all-start.1) | async-done | bytes 7864352 | tf_op jit(solution)/shard_map/while/body/eval_jaxpr/all_to_all | solution.py:220
  425.3 164.3 %all-to-all-done = bf16[4,10,64,1536]{3,2,1,0:T(8,128)(2,1)} async-done(((bf16[4,10,64,1536]{3,2,1,0:T(8,128)(2,1)}), bf16[4,10,64,1536]{3,2,1,0:T(8,128)(2,1)}, u32[]{:S(2)}, u32[]{:S(2)}) %all-to-all-start) | async-done | bytes 7864352 | tf_op jit(solution)/shard_map/while/body/eval_jaxpr/all_to_all | solution.py:188
  648.7 29.1 copy.299
  708.0 28.9 copy.297
  736.9 219.9 %all-to-all-done.3 = bf16[1,10,256,1536]{3,1,0,2:T(8,128)(2,1)} async-done(((bf16[1,10,256,1536]{3,1,0,2:T(8,128)(2,1)}), bf16[1,10,256,1536]{3,1,0,2:T(8,128)(2,1)}, u32[]{:S(2)}, u32[]{:S(2)}) %all-to-all-start.3) | async-done | bytes 7864352 | tf_op jit(solution)/shard_map/while/body/eval_jaxpr/all_to_all | solution.py:202
  1036.7 199.1 %all-to-all-done.2 = bf16[1,10,256,1536]{3,1,0,2:T(8,128)(2,1)} async-done(((bf16[1,10,256,1536]{3,1,0,2:T(8,128)(2,1)}), bf16[1,10,256,1536]{3,1,0,2:T(8,128)(2,1)}, u32[]{:S(2)}, u32[]{:S(2)}) %all-to-all-start.2) | async-done | bytes 7864352 | tf_op jit(solution)/shard_map/while/body/eval_jaxpr/all_to_all | solution.py:246
  1280.3 36.0 %while.69 = (s32[]{:T(128)}, f32[256,8,3,64]{0,3,2,1:T(8,128)S(1)}, bf16[4,256,512]{2,1,0:T(8,128)(2,1)}, bf16[4,256,512]{2,1,0:T(8,128)(2,1)}, s32[4]{0:T(128)S...) while((s32[]{:T(128)}, f32[256,8,3,64]{0,3,2,1:T(8,128)S(1)}, ...), condition=%wide.region_36.36_spmd, body=%wide.region_33.35_spmd.sunk | while | flops 1020264448 | bytes 39134000 | solution.py:329
  1370.7 22.1 reduce-scatter.31.cloned.1.call-done
  1435.2 24.1 all-gather.13.cloned.1.call-done
  1523.0 37.3 %all-gather.17.cloned.1.call-done = bf16[1536,1536]{1,0:T(8,128)(2,1)} async-done(((bf16[192,1536]{1,0:T(8,128)(2,1)}), bf16[1536,1536]{1,0:T(8,128)(2,1)}) %all-gather.17.cloned.1.call-update) | async-done | bytes 4718608 | tf_op jit(solution)/shard_map/while/body/eval_jaxpr/all_gather | solution.py:118
  1646.3 157.6 %all-to-all-done.1 = bf16[4,10,64,1536]{3,2,1,0:T(8,128)(2,1)} async-done(((bf16[4,10,64,1536]{3,2,1,0:T(8,128)(2,1)}), bf16[4,10,64,1536]{3,2,1,0:T(8,128)(2,1)}, u32[]{:S(2)}, u32[]{:S(2)}) %all-to-all-start.1) | async-done | bytes 7864352 | tf_op jit(solution)/shard_map/while/body/eval_jaxpr/all_to_all | solution.py:220
  1816.9 164.2 %all-to-all-done = bf16[4,10,64,1536]{3,2,1,0:T(8,128)(2,1)} async-done(((bf16[4,10,64,1536]{3,2,1,0:T(8,128)(2,1)}), bf16[4,10,64,1536]{3,2,1,0:T(8,128)(2,1)}, u32[]{:S(2)}, u32[]{:S(2)}) %all-to-all-start) | async-done | bytes 7864352 | tf_op jit(solution)/shard_map/while/body/eval_jaxpr/all_to_all | solution.py:188
  2040.3 29.1 copy.299
  2099.7 28.9 copy.297
  2128.6 219.9 %all-to-all-done.3 = bf16[1,10,256,1536]{3,1,0,2:T(8,128)(2,1)} async-done(((bf16[1,10,256,1536]{3,1,0,2:T(8,128)(2,1)}), bf16[1,10,256,1536]{3,1,0,2:T(8,128)(2,1)}, u32[]{:S(2)}, u32[]{:S(2)}) %all-to-all-start.3) | async-done | bytes 7864352 | tf_op jit(solution)/shard_map/while/body/eval_jaxpr/all_to_all | solution.py:202
  2357.5 26.4 select_add_fusion.14
  2383.9 23.5 select_add_fusion.12
  2446.9 180.5 %all-to-all-done.2 = bf16[1,10,256,1536]{3,1,0,2:T(8,128)(2,1)} async-done(((bf16[1,10,256,1536]{3,1,0,2:T(8,128)(2,1)}), bf16[1,10,256,1536]{3,1,0,2:T(8,128)(2,1)}, u32[]{:S(2)}, u32[]{:S(2)}) %all-to-all-start.2) | async-done | bytes 7864352 | tf_op jit(solution)/shard_map/while/body/eval_jaxpr/all_to_all | solution.py:246
  2671.9 36.0 %while.69 = (s32[]{:T(128)}, f32[256,8,3,64]{0,3,2,1:T(8,128)S(1)}, bf16[4,256,512]{2,1,0:T(8,128)(2,1)}, bf16[4,256,512]{2,1,0:T(8,128)(2,1)}, s32[4]{0:T(128)S...) while((s32[]{:T(128)}, f32[256,8,3,64]{0,3,2,1:T(8,128)S(1)}, ...), condition=%wide.region_36.36_spmd, body=%wide.region_33.35_spmd.sunk | while | flops 1020264448 | bytes 39134000 | solution.py:329
  2708.1 26.5 select_add_fusion.13
  2820.4 27.0 reduce-scatter.15.cloned.1.call-done
  2847.4 42.1 %reduce-scatter.17.cloned.1.call-done = bf16[192,512]{1,0:T(8,128)(2,1)} async-done(((bf16[1536,512]{1,0:T(8,128)(2,1)}), bf16[192,512]{1,0:T(8,128)(2,1)}) %reduce-scatter.17.cloned.1.call-update) | async-done | bytes 196624 | tf_op jit(solution)/shard_map/reduce_scatter | solution.py:415
  2889.5 57.1 %reduce-scatter.13.cloned.1.call-done = bf16[192,1536]{1,0:T(8,128)(2,1)} async-done(((bf16[1536,1536]{1,0:T(8,128)(2,1)}), bf16[192,1536]{1,0:T(8,128)(2,1)}) %reduce-scatter.13.cloned.1.call-update) | async-done | bytes 589840 | tf_op jit(solution)/shard_map/reduce_scatter | solution.py:409
  2946.6 57.6 %reduce-scatter.19.cloned.1.call-done = bf16[192,1536]{1,0:T(8,128)(2,1)} async-done(((bf16[1536,1536]{1,0:T(8,128)(2,1)}), bf16[192,1536]{1,0:T(8,128)(2,1)}) %reduce-scatter.19.cloned.1.call-update) | async-done | bytes 589840 | tf_op jit(solution)/shard_map/reduce_scatter | solution.py:418
  3092.1 22.8 all-reduce.18.cloned.1.call-done
  3121.0 105.3 %reduce-scatter.21.cloned.1.call-done = bf16[10,192,512]{2,1,0:T(8,128)(2,1)} async-done(((bf16[10,1536,512]{2,1,0:T(8,128)(2,1)}), bf16[10,192,512]{2,1,0:T(8,128)(2,1)}) %reduce-scatter.21.cloned.1.call-update) | async-done | bytes 1966096 | tf_op jit(solution)/shard_map/reduce_scatter | solution.py:398
  3230.3 108.3 %reduce-scatter.23.cloned.1.call-done = bf16[10,192,512]{2,1,0:T(8,128)(2,1)} async-done(((bf16[10,1536,512]{2,1,0:T(8,128)(2,1)}), bf16[10,192,512]{2,1,0:T(8,128)(2,1)}) %reduce-scatter.23.cloned.1.call-update) | async-done | bytes 1966096 | tf_op jit(solution)/shard_map/reduce_scatter | solution.py:401
  3342.6 108.3 %reduce-scatter.25.cloned.1.call-done = bf16[10,64,1536]{2,1,0:T(8,128)(2,1)} async-done(((bf16[10,512,1536]{2,1,0:T(8,128)(2,1)}), bf16[10,64,1536]{2,1,0:T(8,128)(2,1)}) %reduce-scatter.25.cloned.1.call-update) | async-done | bytes 1966096 | tf_op jit(solution)/shard_map/reduce_scatter | solution.py:404
  (729 shorter events, 1110.3 us)
Async XLA Ops:
  8.5 31.2 all-gather.19.cloned.1.call-start
  9.2 58.1 %all-gather.13.cloned.1.call-start = ((), (), s32[]{:S(2)}) async-start(), calls=%async_computation.23 | async-start | bytes 1769472 | tf_op jit(solution)/shard_map/while/body/eval_jaxpr/all_gather | solution.py:119
  9.9 107.2 %all-gather.21.cloned.1.call-start = ((), (), s32[]{:S(2)}) async-start(), calls=%async_computation.27 | async-start | bytes 1310720 | tf_op jit(solution)/shard_map/while/body/eval_jaxpr/all_gather | solution.py:280
  42.8 86.3 %all-gather.15.cloned.1.call-start = ((), (), s32[]{:S(2)}) async-start(), calls=%async_computation.24 | async-start | bytes 1310720 | tf_op jit(solution)/shard_map/while/body/eval_jaxpr/all_gather | solution.py:279
  70.6 97.5 %all-gather.17.cloned.1.call-start = ((), (), s32[]{:S(2)}) async-start(), calls=%async_computation.25 | async-start | bytes 5308416 | tf_op jit(solution)/shard_map/while/body/eval_jaxpr/all_gather | solution.py:118
  71.2 137.6 %all-gather.23.cloned.1.call-start = ((), (), s32[]{:S(2)}) async-start(), calls=%async_computation.28 | async-start | bytes 5308416 | tf_op jit(solution)/shard_map/while/body/eval_jaxpr/all_gather | solution.py:121
  231.1 180.9 %all-to-all-start.1 = ((bf16[4,10,64,1536]{3,2,1,0:T(8,128)(2,1)}), bf16[4,10,64,1536]{3,2,1,0:T(8,128)(2,1)}, u32[]{:S(2)}, u32[]{:S(2)}) async-start(bf16[4,10,64,1536]{3,2,1,0:T(8,128)(2,1)} %bitcast.567), calls=%async_computation.1 | async-start | bytes 15728640 | tf_op jit(solution)/shard_map/while/body/eval_jaxpr/all_to_all | solution.py:220
  412.0 177.5 %all-to-all-start = ((bf16[4,10,64,1536]{3,2,1,0:T(8,128)(2,1)}), bf16[4,10,64,1536]{3,2,1,0:T(8,128)(2,1)}, u32[]{:S(2)}, u32[]{:S(2)}) async-start(bf16[4,10,64,1536]{3,2,1,0:T(8,128)(2,1)} %bitcast.566), calls=%async_computation | async-start | bytes 15728640 | tf_op jit(solution)/shard_map/while/body/eval_jaxpr/all_to_all | solution.py:188
  677.8 279.0 %all-to-all-start.3 = ((bf16[1,10,256,1536]{3,1,0,2:T(8,128)(2,1)}), bf16[1,10,256,1536]{3,1,0,2:T(8,128)(2,1)}, u32[]{:S(2)}, u32[]{:S(2)}) async-start(bf16[1,10,256,1536]{3,1,0,2:T(8,128)(2,1)} %copy.299), calls=%async_computation.3 | async-start | bytes 25165824 | tf_op jit(solution)/shard_map/while/body/eval_jaxpr/all_to_all | solution.py:202
  956.8 278.9 %all-to-all-start.2 = ((bf16[1,10,256,1536]{3,1,0,2:T(8,128)(2,1)}), bf16[1,10,256,1536]{3,1,0,2:T(8,128)(2,1)}, u32[]{:S(2)}, u32[]{:S(2)}) async-start(bf16[1,10,256,1536]{3,1,0,2:T(8,128)(2,1)} %copy.297), calls=%async_computation.2 | async-start | bytes 25165824 | tf_op jit(solution)/shard_map/while/body/eval_jaxpr/all_to_all | solution.py:246
  963.3 400.7 %reduce-scatter.29.cloned.1.call-start = ((), (), s32[]{:S(2)}) async-start(), calls=%async_computation.29 | async-start | bytes 1310720 | tf_op jit(solution)/shard_map/while/body/eval_jaxpr/reduce_scatter | solution.py:335
  1316.3 76.5 %reduce-scatter.31.cloned.1.call-start = ((), (), s32[]{:S(2)}) async-start(), calls=%async_computation.30 | async-start | bytes 1310720 | tf_op jit(solution)/shard_map/while/body/eval_jaxpr/reduce_scatter | solution.py:341
  1405.4 53.9 %all-gather.13.cloned.1.call-start = ((), (), s32[]{:S(2)}) async-start(), calls=%async_computation.23 | async-start | bytes 1769472 | tf_op jit(solution)/shard_map/while/body/eval_jaxpr/all_gather | solution.py:119
  1406.0 103.3 %all-gather.21.cloned.1.call-start = ((), (), s32[]{:S(2)}) async-start(), calls=%async_computation.27 | async-start | bytes 1310720 | tf_op jit(solution)/shard_map/while/body/eval_jaxpr/all_gather | solution.py:280
  1435.0 86.2 %all-gather.15.cloned.1.call-start = ((), (), s32[]{:S(2)}) async-start(), calls=%async_computation.24 | async-start | bytes 1310720 | tf_op jit(solution)/shard_map/while/body/eval_jaxpr/all_gather | solution.py:279
  1462.6 97.7 %all-gather.17.cloned.1.call-start = ((), (), s32[]{:S(2)}) async-start(), calls=%async_computation.25 | async-start | bytes 5308416 | tf_op jit(solution)/shard_map/while/body/eval_jaxpr/all_gather | solution.py:118
  1463.4 137.6 %all-gather.23.cloned.1.call-start = ((), (), s32[]{:S(2)}) async-start(), calls=%async_computation.28 | async-start | bytes 5308416 | tf_op jit(solution)/shard_map/while/body/eval_jaxpr/all_gather | solution.py:121
  1623.3 180.6 %all-to-all-start.1 = ((bf16[4,10,64,1536]{3,2,1,0:T(8,128)(2,1)}), bf16[4,10,64,1536]{3,2,1,0:T(8,128)(2,1)}, u32[]{:S(2)}, u32[]{:S(2)}) async-start(bf16[4,10,64,1536]{3,2,1,0:T(8,128)(2,1)} %bitcast.567), calls=%async_computation.1 | async-start | bytes 15728640 | tf_op jit(solution)/shard_map/while/body/eval_jaxpr/all_to_all | solution.py:220
  1803.9 177.3 %all-to-all-start = ((bf16[4,10,64,1536]{3,2,1,0:T(8,128)(2,1)}), bf16[4,10,64,1536]{3,2,1,0:T(8,128)(2,1)}, u32[]{:S(2)}, u32[]{:S(2)}) async-start(bf16[4,10,64,1536]{3,2,1,0:T(8,128)(2,1)} %bitcast.566), calls=%async_computation | async-start | bytes 15728640 | tf_op jit(solution)/shard_map/while/body/eval_jaxpr/all_to_all | solution.py:188
  2069.4 279.0 %all-to-all-start.3 = ((bf16[1,10,256,1536]{3,1,0,2:T(8,128)(2,1)}), bf16[1,10,256,1536]{3,1,0,2:T(8,128)(2,1)}, u32[]{:S(2)}, u32[]{:S(2)}) async-start(bf16[1,10,256,1536]{3,1,0,2:T(8,128)(2,1)} %copy.299), calls=%async_computation.3 | async-start | bytes 25165824 | tf_op jit(solution)/shard_map/while/body/eval_jaxpr/all_to_all | solution.py:202
  2348.5 278.9 %all-to-all-start.2 = ((bf16[1,10,256,1536]{3,1,0,2:T(8,128)(2,1)}), bf16[1,10,256,1536]{3,1,0,2:T(8,128)(2,1)}, u32[]{:S(2)}, u32[]{:S(2)}) async-start(bf16[1,10,256,1536]{3,1,0,2:T(8,128)(2,1)} %copy.297), calls=%async_computation.2 | async-start | bytes 25165824 | tf_op jit(solution)/shard_map/while/body/eval_jaxpr/all_to_all | solution.py:246
  2354.9 406.7 %reduce-scatter.29.cloned.1.call-start = ((), (), s32[]{:S(2)}) async-start(), calls=%async_computation.29 | async-start | bytes 1310720 | tf_op jit(solution)/shard_map/while/body/eval_jaxpr/reduce_scatter | solution.py:335
  2708.0 76.7 %reduce-scatter.31.cloned.1.call-start = ((), (), s32[]{:S(2)}) async-start(), calls=%async_computation.30 | async-start | bytes 1310720 | tf_op jit(solution)/shard_map/while/body/eval_jaxpr/reduce_scatter | solution.py:341
  2800.4 47.0 %reduce-scatter.15.cloned.1.call-start = ((), (), s32[]{:S(2)}) async-start(), calls=%async_computation.15 | async-start | bytes 1769472 | tf_op jit(solution)/shard_map/reduce_scatter | solution.py:412
  2803.9 85.6 %reduce-scatter.17.cloned.1.call-start = ((), (), s32[]{:S(2)}) async-start(), calls=%async_computation.16 | async-start | bytes 1769472 | tf_op jit(solution)/shard_map/reduce_scatter | solution.py:415
  2805.3 141.3 %reduce-scatter.13.cloned.1.call-start = ((), (), s32[]{:S(2)}) async-start(), calls=%async_computation.14 | async-start | bytes 5308416 | tf_op jit(solution)/shard_map/reduce_scatter | solution.py:409
  2811.9 192.4 %reduce-scatter.19.cloned.1.call-start = ((), (), s32[]{:S(2)}) async-start(), calls=%async_computation.17 | async-start | bytes 5308416 | tf_op jit(solution)/shard_map/reduce_scatter | solution.py:418
  2818.5 251.9 %reduce-scatter.27.cloned.1.call-start = ((), (), s32[]{:S(2)}) async-start(), calls=%async_computation.21 | async-start | bytes 442368
  2820.3 294.6 %all-reduce.18.cloned.1.call-start = ((), (), s32[]{:S(2)}) async-start(), calls=%async_computation.22 | async-start | bytes 3145728 | tf_op jit(solution)/shard_map/psum | solution.py:432
  3004.2 222.0 %reduce-scatter.21.cloned.1.call-start = ((), (), s32[]{:S(2)}) async-start(), calls=%async_computation.18 | async-start | bytes 17694720 | tf_op jit(solution)/shard_map/reduce_scatter | solution.py:398
  3021.0 317.6 %reduce-scatter.23.cloned.1.call-start = ((), (), s32[]{:S(2)}) async-start(), calls=%async_computation.19 | async-start | bytes 17694720 | tf_op jit(solution)/shard_map/reduce_scatter | solution.py:401
  3037.7 413.3 %reduce-scatter.25.cloned.1.call-start = ((), (), s32[]{:S(2)}) async-start(), calls=%async_computation.20 | async-start | bytes 17694720 | tf_op jit(solution)/shard_map/reduce_scatter | solution.py:404
  (162 other events, 2918.6 us)
Sparse Core Ops, SparseCore 0:
  11.2 28.4 all-gather.18
  41.6 25.6 all-gather.12
  69.5 27.9 all-gather.20
  99.4 29.6 all-gather.14
  130.9 37.2 all-gather.16
  169.9 38.9 all-gather.22
  1316.4 47.5 reduce-scatter.28
  1367.0 25.7 reduce-scatter.30
  1407.4 24.4 all-gather.18
  1433.6 25.6 all-gather.12
  1461.4 27.9 all-gather.20
  1491.4 29.6 all-gather.14
  1523.0 37.2 all-gather.16
  1562.0 38.9 all-gather.22
  2708.1 47.5 reduce-scatter.28
  2758.6 26.0 reduce-scatter.30
Sparse Core Ops, SparseCore 1:
  2804.7 42.6 reduce-scatter.14
  2851.1 38.3 reduce-scatter.16
  2892.8 53.7 reduce-scatter.12
  2950.4 53.7 reduce-scatter.18
  3007.9 33.8 reduce-scatter.26
  3044.4 70.5 all-reduce.17
  3118.3 108.0 reduce-scatter.20
  3229.7 108.9 reduce-scatter.22
  3342.0 108.9 reduce-scatter.24
where the time goes:
time: 3470 us; the launch traced here: 3460 us
  waiting for transfers between devices  2230 us (64%)
  local copies, waits for them, and re-layouts  429 us (12%)
  matrix products  380 us (11%)
  other arithmetic  231 us (7%)
  blocking collectives  81.9 us (2%)
  starting transfers between devices  55.8 us (2%)
  loops' own time  40.6 us (1%)
    all_to_all x2, waiting for transfers between devices, micro_step(): lax.all_to_all(result.reshape(1, exp_dev, expert_count * CAP, features),...  440 us
    all_to_all x2, waiting for transfers between devices, micro_step(): lax.all_to_all(grad_inbound.reshape(1, exp_dev, expert_count * CAP, featu...  380 us
    all_to_all x2, waiting for transfers between devices, micro_step(): lax.all_to_all(outgoing.reshape(expert_count, exp_dev, CAP, features), 'e...  328 us
    all_to_all x2, waiting for transfers between devices, micro_step(): lax.all_to_all(grad_outgoing.reshape(expert_count, exp_dev, CAP, features...  315 us
    reduce_scatter x1, waiting for transfers between devices, local(): lax.psum_scatter(expert_acc[2].astype(jnp.bfloat16), 'dp', scatter_dimens...  108 us
    reduce_scatter x1, waiting for transfers between devices, local(): lax.psum_scatter(expert_acc[1].astype(jnp.bfloat16), 'dp', scatter_dimens...  108 us
    reduce_scatter x1, waiting for transfers between devices, local(): lax.psum_scatter(expert_acc[0].astype(jnp.bfloat16), 'dp', scatter_dimens...  105 us
    all_gather x2, waiting for transfers between devices, micro_step(): lax.all_gather(w_query, 'dp', axis=0, tiled=True)  74.4 us
  transfers between devices with their start and end apart: 33, of which 29 were waited for; matrix products, arithmetic and copies ran while one was open for 18% of the time, Pallas kernels for 0%

commit v1 on v0

v1 whole, which is shorter than its diff:
```python
from functools import partial

import jax
import jax.numpy as jnp
from jax import lax
from jax.experimental import pallas as pl
from jax.experimental.pallas import tpu as pltpu
from jax.sharding import PartitionSpec as P

HEADS = 24
KV_HEADS = 8
HEAD = 64
FF = 512
EXPERTS = 40
TOP = 8
BLOCK = 256
SEQ = 1024
CAP = 64
QD = 1536
KD = 512

EPSILON = 1e-06
ROPE_BASE = 10000.0
NEGATIVE = -1e30
LANES = 128
COLUMNS = 256
VMEM_LIMIT = 56 * 2**20

BF = jnp.bfloat16
F32 = jnp.float32


def dense_dot(left, right):
    return jnp.dot(left, right, preferred_element_type=F32)


def left_dot(left, right):
    return lax.dot_general(left, right, (((0,), (0,)), ((), ())), preferred_element_type=F32)


def right_dot(left, right):
    return lax.dot_general(left, right, (((1,), (1,)), ((), ())), preferred_element_type=F32)


def rotary_tables(positions):
    half_size = HEAD // 2
    frequency = ROPE_BASE ** (-jnp.arange(half_size, dtype=F32) / half_size)
    angle = positions.astype(F32)[:, None] * frequency[None, :]
    return (jnp.cos(angle)[:, None, :], jnp.sin(angle)[:, None, :])


def rotate(values, cosine, sine):
    half_size = values.shape[-1] // 2
    first, second = (values[..., :half_size], values[..., half_size:])
    return jnp.concatenate(
        [first * cosine - second * sine, second * cosine + first * sine], axis=-1
    )


def unrotate(grads, cosine, sine):
    half_size = grads.shape[-1] // 2
    first, second = (grads[..., :half_size], grads[..., half_size:])
    return jnp.concatenate(
        [first * cosine + second * sine, second * cosine - first * sine], axis=-1
    )


def params(limit=VMEM_LIMIT):
    return pltpu.CompilerParams(vmem_limit_bytes=limit)


def picks(slot_rows):
    slots = lax.broadcasted_iota(jnp.int32, (CAP, BLOCK), 0).astype(F32)
    one, zero = jnp.float32(1), jnp.float32(0)
    return [jnp.where(slots == slot_rows[e : e + 1, :], one, zero) for e in range(slot_rows.shape[0])]


def dispatch_kernel(slot_ref, rows_ref, out_ref):
    experts = slot_ref.shape[0]
    chosen = jnp.concatenate([p.astype(BF) for p in picks(slot_ref[...])], axis=0)
    for start in range(0, out_ref.shape[2], COLUMNS):
        rows = dense_dot(chosen, rows_ref[:, start : start + COLUMNS])
        out_ref[:, :, start : start + COLUMNS] = rows.astype(BF).reshape(experts, CAP, COLUMNS)


def dispatch(slot_rows, rows, features):
    experts, total = slot_rows.shape
    blocks = total // BLOCK
    return pl.pallas_call(
        dispatch_kernel,
        grid=(blocks,),
        in_specs=[
            pl.BlockSpec((experts, BLOCK), lambda b: (0, b)),
            pl.BlockSpec((BLOCK, features), lambda b: (b, 0)),
        ],
        out_specs=pl.BlockSpec((experts, CAP, features), lambda b: (0, b, 0)),
        out_shape=jax.ShapeDtypeStruct((experts, blocks * CAP, features), BF),
        compiler_params=params(),
        cost_estimate=pl.CostEstimate(
            flops=2 * experts * CAP * total * features,
            bytes_accessed=2 * features * (total + experts * blocks * CAP),
            transcendentals=0,
        ),
        name="dispatch",
    )(slot_rows, rows)


def combine_kernel(slot_ref, slots_ref, *rest):
    out_ref = rest[-1]
    experts, features = slots_ref.shape[0], slots_ref.shape[2]
    chosen = jnp.concatenate([p.astype(BF) for p in picks(slot_ref[...])], axis=0)
    for start in range(0, features, COLUMNS):
        held = slots_ref[:, :, start : start + COLUMNS].reshape(experts * CAP, COLUMNS)
        out_ref[:, start : start + COLUMNS] = left_dot(chosen, held).astype(BF)
    if len(rest) > 1:
        out_ref[:, features:] = rest[0][...]


def combine(slot_rows, slots, extra=None):
    experts, total = slot_rows.shape
    blocks = total // BLOCK
    features = slots.shape[2]
    extras = [] if extra is None else [extra]
    width = features + sum(a.shape[1] for a in extras)
    return pl.pallas_call(
        combine_kernel,
        grid=(blocks,),
        in_specs=[
            pl.BlockSpec((experts, BLOCK), lambda b: (0, b)),
            pl.BlockSpec((experts, CAP, features), lambda b: (0, b, 0)),
            *[pl.BlockSpec((BLOCK, a.shape[1]), lambda b: (b, 0)) for a in extras],
        ],
        out_specs=pl.BlockSpec((BLOCK, width), lambda b: (b, 0)),
        out_shape=jax.ShapeDtypeStruct((total, width), BF),
        compiler_params=params(),
        cost_estimate=pl.CostEstimate(
            flops=2 * experts * CAP * total * features,
            bytes_accessed=2 * features * (total + experts * blocks * CAP),
            transcendentals=0,
        ),
        name="combine",
    )(slot_rows, slots, *extras)


def expert_kernel(
    slot_ref, gate_ref, x_ref, dy_ref, wg_ref, wu_ref, wd_ref,
    ys_ref, dx_ref, gdy_ref, act_ref, dg_ref, du_ref, dgates_ref,
):
    rows = x_ref[0]
    blocks = rows.shape[0] // CAP
    pre = dense_dot(rows, wg_ref[0])
    up = dense_dot(rows, wu_ref[0])
    sigma = 1.0 / (1.0 + jnp.exp(-pre))
    silu = pre * sigma
    active = (silu * up).astype(BF)
    act_ref[0] = active
    chosen = []
    shares = []
    for b in range(blocks):
        where = slice(b * BLOCK, (b + 1) * BLOCK)
        one_hot = picks(slot_ref[0][:, where])[0]
        chosen.append(one_hot)
        shares.append(jnp.sum(one_hot * gate_ref[0][:, where], axis=1, keepdims=True))
    share = jnp.concatenate(shares, axis=0)
    result = dense_dot(active, wd_ref[0])
    grads = dy_ref[0].astype(F32)
    dots = jnp.sum(result * grads, axis=1, keepdims=True)
    ys_ref[0] = (result * share).astype(BF)
    gated = (grads * share).astype(BF)
    gdy_ref[0] = gated
    for b in range(blocks):
        dgates_ref[0, :, b * BLOCK : (b + 1) * BLOCK] = jnp.sum(
            chosen[b] * dots[b * CAP : (b + 1) * CAP], axis=0, keepdims=True
        )
    dact = right_dot(gated, wd_ref[0])
    dpre = (dact * up * sigma * (1.0 + pre * (1.0 - sigma))).astype(BF)
    dup = (dact * silu).astype(BF)
    dg_ref[0] = dpre
    du_ref[0] = dup
    dx_ref[0] = (right_dot(dpre, wg_ref[0]) + right_dot(dup, wu_ref[0])).astype(BF)


def expert_pass(slot_rows, gate_rows, x_slots, dy_slots, w_gate, w_up, w_down):
    experts, total = slot_rows.shape
    _, rows, features = x_slots.shape
    hidden = w_gate.shape[2]
    one = lambda e: (e, 0, 0)
    line = pl.BlockSpec((1, 1, total), one)
    wide = pl.BlockSpec((1, rows, features), one)
    narrow = pl.BlockSpec((1, rows, hidden), one)
    wide_shape = jax.ShapeDtypeStruct((experts, rows, features), BF)
    narrow_shape = jax.ShapeDtypeStruct((experts, rows, hidden), BF)
    outs = pl.pallas_call(
        expert_kernel,
        grid=(experts,),
        in_specs=[
            line, line, wide, wide,
            pl.BlockSpec((1, features, hidden), one),
            pl.BlockSpec((1, features, hidden), one),
            pl.BlockSpec((1, hidden, features), one),
        ],
        out_specs=[wide, wide, wide, narrow, narrow, narrow, line],
        out_shape=[
            wide_shape, wide_shape, wide_shape, narrow_shape, narrow_shape, narrow_shape,
            jax.ShapeDtypeStruct((experts, 1, total), F32),
        ],
        compiler_params=params(),
        cost_estimate=pl.CostEstimate(
            flops=12 * experts * rows * features * hidden,
            bytes_accessed=6 * experts * features * hidden + 10 * experts * rows * features,
            transcendentals=experts * rows * hidden,
        ),
        name="experts",
    )(slot_rows[:, None, :], gate_rows[:, None, :], x_slots, dy_slots, w_gate, w_up, w_down)
    return outs[:-1], outs[-1][:, 0, :]


def weight_kernel(*refs):
    count = (len(refs) - 3) // 5
    ins, (gate_ref, up_ref, down_ref) = refs[: 5 * count], refs[5 * count :]
    xs, gdys, acts, dgs, dus = [ins[i::5] for i in range(5)]
    total = lambda lefts, rights: sum(
        left_dot(left[0], right[0]) for left, right in zip(lefts, rights)
    )
    gate_ref[0] = total(xs, dgs).astype(BF)
    up_ref[0] = total(xs, dus).astype(BF)
    down_ref[0] = total(acts, gdys).astype(BF)


def weight_pass(parts):
    experts, rows, features = parts[0][0].shape
    hidden = parts[0][2].shape[2]
    one = lambda e: (e, 0, 0)
    count = len(parts)
    return pl.pallas_call(
        weight_kernel,
        grid=(experts,),
        in_specs=[
            pl.BlockSpec((1, rows, a.shape[2]), one) for part in parts for a in part
        ],
        out_specs=[
            pl.BlockSpec((1, features, hidden), one),
            pl.BlockSpec((1, features, hidden), one),
            pl.BlockSpec((1, hidden, features), one),
        ],
        out_shape=[
            jax.ShapeDtypeStruct((experts, features, hidden), BF),
            jax.ShapeDtypeStruct((experts, features, hidden), BF),
            jax.ShapeDtypeStruct((experts, hidden, features), BF),
        ],
        compiler_params=params(),
        cost_estimate=pl.CostEstimate(
            flops=6 * count * experts * rows * features * hidden,
            bytes_accessed=6 * experts * features * hidden + 4 * count * experts * rows * (features + hidden),
            transcendentals=0,
        ),
        name="expert_weights",
    )(*[a for part in parts for a in part])


def online_step(carried, query_rows, key_rows, value_rows, score_scale):
    running_max, running_sum, running_out = carried
    scores = (
        jnp.einsum("qgrd,kgd->grqk", query_rows, key_rows, preferred_element_type=F32)
        * score_scale
    )
    new_max = jnp.maximum(running_max, jnp.max(scores, axis=-1))
    factor = jnp.exp(running_max - new_max)
    weights = jnp.exp(scores - new_max[..., None])
    running_sum = running_sum * factor + jnp.sum(weights, axis=-1)
    running_out = running_out * factor[..., None] + jnp.einsum(
        "grqk,kgd->grqd", weights.astype(BF), value_rows, preferred_element_type=F32
    )
    return (new_max, running_sum, running_out)


def keep_state(carried):
    return carried


def attend(query_b, keys, values, first_block, own_rank, score_scale):
    repeat = HEADS // KV_HEADS
    state = (
        jnp.full((KV_HEADS, repeat, BLOCK), NEGATIVE, F32),
        jnp.zeros((KV_HEADS, repeat, BLOCK), F32),
        jnp.zeros((KV_HEADS, repeat, BLOCK, HEAD), F32),
    )
    for index in range(keys.shape[0] // BLOCK):
        rows = slice(index * BLOCK, (index + 1) * BLOCK)
        update = partial(
            online_step,
            query_rows=query_b,
            key_rows=keys[rows].reshape(BLOCK, KV_HEADS, HEAD),
            value_rows=values[rows].reshape(BLOCK, KV_HEADS, HEAD),
            score_scale=score_scale,
        )
        seen = jnp.logical_and(index >= first_block, index <= own_rank)
        state = lax.cond(seen, update, keep_state, state)
    running_max, running_sum, running_out = state
    return running_out / running_sum[..., None], running_max + jnp.log(running_sum)


def attend_back(query_b, grad_attn, row_delta, log_total, keys, values, first_block, own_rank, score_scale):
    repeat = HEADS // KV_HEADS
    count = keys.shape[0] // BLOCK

    def back_block(grad_query, block_index):
        key_rows = lax.dynamic_slice_in_dim(keys, block_index * BLOCK, BLOCK, 0).reshape(BLOCK, KV_HEADS, HEAD)
        value_rows = lax.dynamic_slice_in_dim(values, block_index * BLOCK, BLOCK, 0).reshape(BLOCK, KV_HEADS, HEAD)

        def visible_block(grad_query):
            scores = (
                jnp.einsum("qgrd,kgd->grqk", query_b, key_rows, preferred_element_type=F32)
                * score_scale
            )
            probabilities = jnp.exp(scores - log_total[..., None])
            grad_probs = jnp.einsum("qgrd,kgd->grqk", grad_attn, value_rows, preferred_element_type=F32)
            grad_scores = (probabilities * (grad_probs - row_delta[..., None])).astype(BF)
            grad_query = grad_query + score_scale * jnp.einsum(
                "grqk,kgd->qgrd", grad_scores, key_rows, preferred_element_type=F32
            )
            grad_keys = score_scale * jnp.einsum(
                "grqk,qgrd->kgd", grad_scores, query_b, preferred_element_type=F32
            )
            grad_values = jnp.einsum(
                "grqk,qgrd->kgd", probabilities.astype(BF), grad_attn, preferred_element_type=F32
            )
            return (grad_query, grad_keys.reshape(BLOCK, KD), grad_values.reshape(BLOCK, KD))

        def skipped_block(grad_query):
            zero_rows = jnp.zeros((BLOCK, KD), F32)
            return (grad_query, zero_rows, zero_rows)

        seen = jnp.logical_and(block_index >= first_block, block_index <= own_rank)
        grad_query, grad_keys, grad_values = lax.cond(seen, visible_block, skipped_block, grad_query)
        return (grad_query, (grad_keys, grad_values))

    grad_query, (key_parts, value_parts) = lax.scan(
        back_block,
        jnp.zeros((BLOCK, KV_HEADS, repeat, HEAD), F32),
        jnp.arange(count, dtype=jnp.int32),
    )
    return grad_query, key_parts.reshape(count * BLOCK, KD), value_parts.reshape(count * BLOCK, KD)


def local(
    tokens, out_grad, routes, attn_gain, w_query, w_key, w_value, w_out, moe_gain, w_router,
    w_gate, w_up, w_down,
):
    micros, _, features = tokens.shape
    expert_count = lax.axis_size("expert")
    own_rank = lax.axis_index("expert")
    exp_dev = w_gate.shape[0]
    repeat = HEADS // KV_HEADS
    score_scale = HEAD ** (-0.5)
    seq_blocks = SEQ // BLOCK
    place_in_seq = own_rank % seq_blocks
    first_block = own_rank - place_in_seq
    cosine, sine = rotary_tables(place_in_seq * BLOCK + jnp.arange(BLOCK, dtype=jnp.int32))
    every = lambda a, axis: lax.all_gather(a, axis, axis=0, tiled=True)

    qkv_w = every(jnp.concatenate([w_query, w_key, w_value], axis=1), "dp")
    out_w = every(w_out, "dp")
    router_w = every(w_router, "dp")
    gains = lax.all_gather(jnp.stack([attn_gain, moe_gain]), "dp", axis=1, tiled=True).astype(F32)
    gain_one, gain_two = gains[0:1], gains[1:2]

    route_columns = jnp.pad(routes.astype(BF), ((0, 0), (0, 0), (0, LANES - TOP)))
    dy_sent = jnp.concatenate([out_grad, route_columns], axis=2)
    dy_all = [every(dy_sent[m], "expert") for m in range(micros)]
    experts_row = jnp.arange(EXPERTS, dtype=jnp.int32)
    before = jnp.tril(jnp.ones((BLOCK, BLOCK), F32), -1).astype(BF)

    x_rows = [tokens[m].astype(F32) for m in range(micros)]
    inverse_one = [lax.rsqrt(jnp.mean(x * x, axis=-1, keepdims=True) + EPSILON) for x in x_rows]
    normed = [(x * r * gain_one).astype(BF) for x, r in zip(x_rows, inverse_one)]
    normed_whole = jnp.concatenate(normed, axis=0)
    qkv = dense_dot(normed_whole, qkv_w)

    outputs, grads_x = [], []
    kept = []
    for m in range(micros):
        own = qkv[m * BLOCK : (m + 1) * BLOCK]
        query_b = (
            rotate(own[:, :QD].reshape(BLOCK, HEADS, HEAD), cosine, sine)
            .astype(BF)
            .reshape(BLOCK, KV_HEADS, repeat, HEAD)
        )
        key_b = rotate(own[:, QD : QD + KD].reshape(BLOCK, KV_HEADS, HEAD), cosine, sine).astype(BF)
        kv = jnp.concatenate([key_b.reshape(BLOCK, KD), own[:, QD + KD :].astype(BF)], axis=1)
        kv_all = every(kv, "expert")
        keys, values = kv_all[:, :KD], kv_all[:, KD:]
        out_four, log_total = attend(query_b, keys, values, first_block, own_rank, score_scale)
        out_b = jnp.transpose(out_four, (2, 0, 1, 3)).reshape(BLOCK, QD).astype(BF)
        mid = x_rows[m] + dense_dot(out_b, out_w)
        inverse_two = lax.rsqrt(jnp.mean(mid * mid, axis=-1, keepdims=True) + EPSILON)
        normed_two = (mid * inverse_two * gain_two).astype(BF)
        normed_all = every(normed_two, "expert")
        kept.append((query_b, keys, values, out_four, log_total, out_b, mid, inverse_two, normed_two, normed_all))

    def gate_table(rows, members):
        logits = jnp.where(members, dense_dot(rows, router_w), NEGATIVE)
        weights = jnp.exp(logits - jnp.max(logits, axis=-1, keepdims=True))
        return weights / jnp.sum(weights, axis=-1, keepdims=True)

    def membership(route_rows):
        return jnp.any(route_rows[:, :, None] == experts_row[None, None, :], axis=1)

    expert_parts = []
    sent = []
    for m in range(micros):
        normed_all = kept[m][-1]
        all_routes = dy_all[m][:, features : features + TOP].astype(jnp.int32)
        members = membership(all_routes)
        blocks = members.reshape(expert_count, BLOCK, EXPERTS)
        slots = jnp.einsum("ts,bse->bte", before, blocks.astype(BF), preferred_element_type=F32)
        slots = jnp.where(blocks, slots, -1.0).reshape(-1, EXPERTS)
        mine = lambda table: lax.dynamic_slice_in_dim(table, own_rank * exp_dev, exp_dev, 1).T
        slot_rows = mine(slots)
        gate_rows = mine(gate_table(normed_all, members))
        dy_slots = dispatch(slot_rows, dy_all[m], features)
        x_slots = dispatch(slot_rows, normed_all, features)
        (ys, dx, gdy, act, dg, du), dgates = expert_pass(
            slot_rows, gate_rows, x_slots, dy_slots, w_gate, w_up, w_down
        )
        expert_parts.append((x_slots, gdy, act, dg, du))
        table = lax.dynamic_update_slice_in_dim(
            jnp.zeros((EXPERTS, dgates.shape[1]), F32), dgates, own_rank * exp_dev, 0
        ).T
        high = table.astype(BF)
        low = (table - high.astype(F32)).astype(BF)
        extra = jnp.concatenate(
            [high, low, jnp.zeros((table.shape[0], LANES - 2 * EXPERTS), BF)], axis=1
        )
        scatter = lambda a: lax.psum_scatter(a, "expert", scatter_dimension=0, tiled=True)
        dx_home = scatter(combine(slot_rows, dx, extra))
        mixture = scatter(combine(slot_rows, ys))
        sent.append((dx_home, mixture))

    new_gate, new_up, new_down = weight_pass(expert_parts)
    scatter_dp = lambda a, axis: lax.psum_scatter(a, "dp", scatter_dimension=axis, tiled=True)
    out_gate = scatter_dp(new_gate, 1).astype(F32)
    out_up = scatter_dp(new_up, 1).astype(F32)
    out_down = scatter_dp(new_down, 1).astype(F32)

    router_grads, gain_two_grads, gain_one_grads = [], [], []
    branches, grad_qkvs = [], []
    for m in range(micros):
        query_b, keys, values, out_four, log_total, out_b, mid, inverse_two, normed_two, _ = kept[m]
        dx_home, mixture = sent[m]
        outputs.append((mid + mixture.astype(F32)).astype(BF))
        grad_y = out_grad[m].astype(F32)
        members = membership(routes[m])
        gates = gate_table(normed_two, members)
        high = dx_home[:, features : features + EXPERTS].astype(F32)
        low = dx_home[:, features + EXPERTS : features + 2 * EXPERTS].astype(F32)
        dgates = high + low
        grad_chosen = gates * (dgates - jnp.sum(gates * dgates, axis=-1, keepdims=True))
        grad_logits = jnp.where(members, grad_chosen, 0.0).astype(BF)
        router_grads.append(left_dot(normed_two, grad_logits))
        grad_normed_two = dx_home[:, :features].astype(F32) + right_dot(grad_logits, router_w)
        gain_two_grads.append(jnp.sum(grad_normed_two * mid * inverse_two, axis=0))
        scaled_two = grad_normed_two * gain_two
        grad_mid = (
            grad_y
            + inverse_two * scaled_two
            - mid * inverse_two**3 * jnp.mean(scaled_two * mid, axis=-1, keepdims=True)
        )
        grad_branch = grad_mid.astype(BF)
        branches.append(grad_branch)
        grad_attn = right_dot(grad_branch, out_w).astype(BF).reshape(BLOCK, KV_HEADS, repeat, HEAD)
        row_delta = jnp.sum(jnp.transpose(grad_attn, (1, 2, 0, 3)) * out_four, axis=-1)
        grad_query, key_parts, value_parts = attend_back(
            query_b, grad_attn, row_delta, log_total, keys, values, first_block, own_rank, score_scale
        )
        own_kv = lax.psum_scatter(
            jnp.concatenate([key_parts, value_parts], axis=1).astype(BF),
            "expert", scatter_dimension=0, tiled=True,
        )
        grad_key_b = (
            unrotate(own_kv[:, :KD].astype(F32).reshape(BLOCK, KV_HEADS, HEAD), cosine, sine)
            .astype(BF)
            .reshape(BLOCK, KD)
        )
        grad_query_b = (
            unrotate(grad_query.reshape(BLOCK, HEADS, HEAD), cosine, sine).astype(BF).reshape(BLOCK, QD)
        )
        grad_qkv = jnp.concatenate([grad_query_b, grad_key_b, own_kv[:, KD:]], axis=1)
        grad_qkvs.append(grad_qkv)
        grad_normed = right_dot(grad_qkv, qkv_w)
        gain_one_grads.append(jnp.sum(grad_normed * x_rows[m] * inverse_one[m], axis=0))
        scaled_one = grad_normed * gain_one
        grads_x.append(
            grad_mid
            + inverse_one[m] * scaled_one
            - x_rows[m] * inverse_one[m] ** 3 * jnp.mean(scaled_one * x_rows[m], axis=-1, keepdims=True)
        )

    total = lambda a: lax.psum(a, "expert").astype(F32)
    new_out = left_dot(
        jnp.concatenate([k[5] for k in kept], axis=0), jnp.concatenate(branches, axis=0)
    )
    grad_out = total(scatter_dp(new_out.astype(BF), 0))
    new_qkv = left_dot(normed_whole, jnp.concatenate(grad_qkvs, axis=0))
    qkv_sum = total(scatter_dp(new_qkv.astype(BF), 0))
    small = jnp.concatenate(
        [sum(router_grads), sum(gain_one_grads)[:, None], sum(gain_two_grads)[:, None]], axis=1
    )
    small_sum = total(scatter_dp(small.astype(BF), 0))
    return (
        jnp.stack(outputs),
        jnp.stack(grads_x),
        small_sum[:, EXPERTS],
        qkv_sum[:, :QD],
        qkv_sum[:, QD : QD + KD],
        qkv_sum[:, QD + KD :],
        grad_out,
        small_sum[:, EXPERTS + 1],
        small_sum[:, :EXPERTS],
        out_gate,
        out_up,
        out_down,
    )


def solution(mesh):
    rows = P(None, ("dp", "expert"), None)
    return jax.shard_map(
        local,
        mesh=mesh,
        in_specs=(
            rows, rows, rows, P("dp"), P("dp", None), P("dp", None), P("dp", None), P("dp", None),
            P("dp"), P("dp", None),
            P("expert", None, None), P("expert", None, None), P("expert", None, None),
        ),
        out_specs=(
            rows, rows, P("dp"), P("dp", None), P("dp", None), P("dp", None), P("dp", None),
            P("dp"), P("dp", None),
            P("expert", "dp", None), P("expert", "dp", None), P("expert", "dp", None),
        ),
        check_vma=False,
    )
```

time: 3470 us -> 1610 us (0.46)
  waiting for transfers between devices: 2230 us -> 1070 us
  local copies, waits for them, and re-layouts: 429 us -> 116 us
  matrix products: 380 us -> 97.5 us
  other arithmetic: 231 us -> 61 us
  Pallas kernels: 0 us -> 169 us
  starting transfers between devices: 55.8 us -> 2.21 us
  blocking collectives: 81.9 us -> 38.5 us
    all_to_all x8 -> x0, waiting for transfers between devices: 1460 us -> none  [the longest x2 440 us: micro_step(): lax.all_to_all(result.reshape(1, exp_dev, expert_count * CAP, features),...]
    dot_general x34 -> x15, matrix products: 308 us -> 31.2 us  [the longest x7 22.1 us: dense_dot(): return jnp.dot(left, right, preferred_element_type=F32)]
    pallas_call x0 -> x11, Pallas kernels: none -> 169 us  [the longest x2 76.9 us: expert_pass(): pl.pallas_call(expert_kernel, grid=(experts,), in_specs=[line, line, wide...]
    all_gather x12 -> x8, waiting for transfers between devices: 180 us -> 325 us  [local(): every = lambda a, axis: lax.all_gather(a, axis, axis=0, tiled=True)]
    reshape x6, local copies, waits for them, and re-layouts: 120 us -> 7.84 us  [the longest x2 5.21 us: attend_back(): value_parts.reshape(count * BLOCK, KD)]
    reduce_scatter x11, waiting for transfers between devices: 557 us -> 647 us  [the longest x5 362 us: local(): lax.psum_scatter(a, 'dp', scatter_dimension=axis, tiled=True)]
    all_to_all x8 -> x0, local copies, waits for them, and re-layouts: 77.3 us -> none  [the longest x2 24.2 us: micro_step(): lax.all_to_all(grad_inbound.reshape(1, exp_dev, expert_count * CAP, featu...]
    gather x4 -> x0, local copies, waits for them, and re-layouts: 70.7 us -> none  [the longest x2 35.5 us: micro_step(): grad_back.reshape(EXPERTS * CAP, features)[target]]
  transfers between devices with their start and end apart: 33 -> 21, of which waited for: 29 -> 19; matrix products, arithmetic and copies ran while one was open for 18% -> 12% of each run, Pallas kernels for 0% -> 7%
where the time goes in v1:
time: 1610 us; the launch traced here: 1590 us
  waiting for transfers between devices  1070 us (66%)
  Pallas kernels  169 us (10%)
  local copies, waits for them, and re-layouts  116 us (7%)
  matrix products  97.5 us (6%)
  other arithmetic  61 us (4%)
  blocking collectives  38.5 us (2%)
  loops' own time  19.5 us (1%)
  between operations  16.6 us (1%)
    reduce_scatter x5, waiting for transfers between devices, local(): lax.psum_scatter(a, 'dp', scatter_dimension=axis, tiled=True)  362 us
    all_gather x8, waiting for transfers between devices, local(): every = lambda a, axis: lax.all_gather(a, axis, axis=0, tiled=True)  325 us
    reduce_scatter x4, waiting for transfers between devices, local(): lax.psum_scatter(a, 'expert', scatter_dimension=0, tiled=True)  205 us
    reduce_scatter x2, waiting for transfers between devices, local(): lax.psum_scatter(jnp.concatenate([key_parts, value_parts], axis=1).astype...  80.2 us
    pallas_call x2, Pallas kernels, expert_pass(): pl.pallas_call(expert_kernel, grid=(experts,), in_specs=[line, line, wide...  76.9 us
    psum x1, waiting for transfers between devices, local(): total = lambda a: lax.psum(a, 'expert').astype(F32)  67.9 us
    pallas_call x1, Pallas kernels, weight_pass(): pl.pallas_call(weight_kernel, grid=(experts,), in_specs=[pl.BlockSpec((1,...  36.7 us
    unnamed x22, waiting for transfers between devices  35.1 us
  transfers between devices with their start and end apart: 21, of which 19 were waited for; matrix products, arithmetic and copies ran while one was open for 12% of the time, Pallas kernels for 7%

profile of v1, /device:TPU:0, one launch (start us, length us, event | category | flops | bytes accessed | tf_op | source)
XLA Modules:
  0.0 1594.4 jit_solution(6348192149892561136)
XLA Ops:
  9.8 10.3 all-gather.2
  21.9 43.5 %all-gather.13.cloned.1.call-done = bf16[1536,2560]{1,0:T(8,128)(2,1)} async-done(((bf16[192,2560]{1,0:T(8,128)(2,1)}), bf16[1536,2560]{1,0:T(8,128)(2,1)}) %all-gather.13.cloned.1.call-update) | async-done | bytes 7864336 | tf_op jit(solution)/shard_map/all_gather | solution.py:360
  86.6 36.4 %all-gather.15.cloned.1.call-done = bf16[1024,1024]{1,0:T(8,128)(2,1)} async-done(((bf16[256,1024]{1,0:T(8,128)(2,1)}), bf16[1024,1024]{1,0:T(8,128)(2,1)}) %all-gather.15.cloned.1.call-update) | async-done | bytes 2097168 | tf_op jit(solution)/shard_map/all_gather | solution.py:360
  134.3 7.5 conditional.13
  142.1 20.5 %all-gather.17.cloned.1.call-done = bf16[1536,1536]{1,0:T(8,128)(2,1)} async-done(((bf16[192,1536]{1,0:T(8,128)(2,1)}), bf16[1536,1536]{1,0:T(8,128)(2,1)}) %all-gather.17.cloned.1.call-update) | async-done | bytes 4718608 | tf_op jit(solution)/shard_map/all_gather | solution.py:360
  169.0 9.2 all-gather.3
  178.5 54.0 %all-gather.25.cloned.1.call-done = bf16[1,1024,1664]{2,1,0:T(8,128)(2,1)} async-done(((bf16[1,256,1664]{2,1,0:T(8,128)(2,1)}), bf16[1,1024,1664]{2,1,0:T(8,128)(2,1)}) %all-gather.25.cloned.1.call-update) | async-done | bytes 3407888 | tf_op jit(solution)/shard_map/all_gather | solution.py:360
  243.4 52.6 %all-gather.19.cloned.1.call-done.rows_ref = bf16[1024,1536]{1,0:T(8,128)(2,1)} async-done(((bf16[256,1536]{1,0:T(8,128)(2,1)}), bf16[1024,1536]{1,0:T(8,128)(2,1)}) %all-gather.19.cloned.1.call-update) | async-done | bytes 3145744 | tf_op jit(solution)/shard_map/all_gather | solution.py:360
  306.4 38.6 %experts.2 = (bf16[10,256,1536]{2,1,0:T(8,128)(2,1)}, bf16[10,256,1536]{2,1,0:T(8,128)(2,1)}, bf16[10,256,1536]{2,1,0:T(8,128)(2,1)}, bf16[10,256,512]{2,1,0:T(8...) custom-call(f32[10,1,1024]{2,1,0:T(1,128)} %copy.449.slot_ref, ...), custom_call_target="tpu_custom_call" | custom-call | flops 24159191040 | bytes 86507520 | tf_op jit(solution)/shard_map/experts/pallas_call | solution.py:193
  361.9 7.5 conditional.14
  377.0 43.2 %reduce-scatter.19.cloned.1.call-done = bf16[256,1664]{1,0:T(8,128)(2,1)} async-done(((bf16[1024,1664]{1,0:T(8,128)(2,1)}), bf16[256,1664]{1,0:T(8,128)(2,1)}) %reduce-scatter.19.cloned.1.call-update) | async-done | bytes 851984 | tf_op jit(solution)/shard_map/reduce_scatter | solution.py:435
  426.7 63.7 %all-gather.27.cloned.1.call-done = bf16[1,1024,1664]{2,1,0:T(8,128)(2,1)} async-done(((bf16[1,256,1664]{2,1,0:T(8,128)(2,1)}), bf16[1,1024,1664]{2,1,0:T(8,128)(2,1)}) %all-gather.27.cloned.1.call-update) | async-done | bytes 3407888 | tf_op jit(solution)/shard_map/all_gather | solution.py:360
  500.1 54.0 %all-gather.23.cloned.1.call-done.rows_ref = bf16[1024,1536]{1,0:T(8,128)(2,1)} async-done(((bf16[256,1536]{1,0:T(8,128)(2,1)}), bf16[1024,1536]{1,0:T(8,128)(2,1)}) %all-gather.23.cloned.1.call-update) | async-done | bytes 3145744 | tf_op jit(solution)/shard_map/all_gather | solution.py:360
  564.5 38.3 %experts.3 = (bf16[10,256,1536]{2,1,0:T(8,128)(2,1)}, bf16[10,256,1536]{2,1,0:T(8,128)(2,1)}, bf16[10,256,1536]{2,1,0:T(8,128)(2,1)}, bf16[10,256,512]{2,1,0:T(8...) custom-call(f32[10,1,1024]{2,1,0:T(1,128)} %copy.465.slot_ref, ...), custom_call_target="tpu_custom_call" | custom-call | flops 24159191040 | bytes 86507520 | tf_op jit(solution)/shard_map/experts/pallas_call | solution.py:193
  639.6 40.5 %reduce-scatter.23.cloned.1.call-done = bf16[256,1664]{1,0:T(8,128)(2,1)} async-done(((bf16[1024,1664]{1,0:T(8,128)(2,1)}), bf16[256,1664]{1,0:T(8,128)(2,1)}) %reduce-scatter.23.cloned.1.call-update) | async-done | bytes 851984 | tf_op jit(solution)/shard_map/reduce_scatter | solution.py:435
  685.3 58.1 %reduce-scatter.15.cloned.1.call-done = bf16[256,1536]{1,0:T(8,128)(2,1)} async-done(((bf16[1024,1536]{1,0:T(8,128)(2,1)}), bf16[256,1536]{1,0:T(8,128)(2,1)}) %reduce-scatter.15.cloned.1.call-update) | async-done | bytes 786448 | tf_op jit(solution)/shard_map/reduce_scatter | solution.py:435
  743.5 63.0 %reduce-scatter.17.cloned.1.call-done = bf16[256,1536]{1,0:T(8,128)(2,1)} async-done(((bf16[1024,1536]{1,0:T(8,128)(2,1)}), bf16[256,1536]{1,0:T(8,128)(2,1)}) %reduce-scatter.17.cloned.1.call-update) | async-done | bytes 786448 | tf_op jit(solution)/shard_map/reduce_scatter | solution.py:435
  821.9 32.9 %while.35 = (s32[]{:T(128)}, f32[256,8,3,64]{0,3,2,1:T(8,128)S(1)}, bf16[4,256,512]{2,1,0:T(8,128)(2,1)}, bf16[4,256,512]{2,1,0:T(8,128)(2,1)}, s32[4]{0:T(128)S...) while((s32[]{:T(128)}, f32[256,8,3,64]{0,3,2,1:T(8,128)S(1)}, ...), condition=%wide.region_67.68_spmd, body=%wide.region_64.67_spmd.sunk | while | flops 1020264448 | bytes 39133500 | solution.py:338
  823.8 8.2 conditional.21
  876.1 32.9 %while.34 = (s32[]{:T(128)}, f32[256,8,3,64]{0,3,2,1:T(8,128)S(1)}, bf16[4,256,512]{2,1,0:T(8,128)(2,1)}, bf16[4,256,512]{2,1,0:T(8,128)(2,1)}, s32[4]{0:T(128)S...) while((s32[]{:T(128)}, f32[256,8,3,64]{0,3,2,1:T(8,128)S(1)}, ...), condition=%wide.region_54.55_spmd, body=%wide.region_51.54_spmd.sunk | while | flops 1020264448 | bytes 39133500 | solution.py:338
  878.0 8.2 conditional.20
  929.4 75.6 %reduce-scatter.21.cloned.1.call-done = bf16[256,1024]{0,1:T(8,128)(2,1)} async-done(((bf16[1024,1024]{0,1:T(8,128)(2,1)}), bf16[256,1024]{0,1:T(8,128)(2,1)}) %reduce-scatter.21.cloned.1.call-update) | async-done | bytes 524304 | tf_op jit(solution)/shard_map/reduce_scatter | solution.py:476
  1007.0 15.3 convolution_convert_fusion
  1032.1 7.4 fusion.144
  1040.5 36.7 %expert_weights.1 = (bf16[10,1536,512]{2,1,0:T(8,128)(2,1)}, bf16[10,1536,512]{2,1,0:T(8,128)(2,1)}, bf16[10,512,1536]{2,1,0:T(8,128)(2,1)}) custom-call(bf16[10,256,1536]{2,1,0:T(8,128)(2,1)} %dispatch.4.x_ref.refs_0_, bf16[10,256,1536]{2,1,0:T(8,128)(2,1)} %get-tuple-element.665.refs_1_, bf16[10,256,512]{2,1,0:T(8,128)(2,1)} %get-tuple-element.666.refs_2_, ...), custom_call_target="tpu_custom_call" | custom-call | flops 24159191040 | bytes 89128960 | tf_op jit(solution)/shard_map/expert_weights/pallas_call | solution.py:235
  1081.8 52.8 %reduce-scatter.27.cloned.1.call-done = bf16[192,2560]{1,0:T(8,128)(2,1)} async-done(((bf16[1536,2560]{1,0:T(8,128)(2,1)}), bf16[192,2560]{1,0:T(8,128)(2,1)}) %reduce-scatter.27.cloned.1.call-update) | async-done | bytes 983056 | tf_op jit(solution)/shard_map/reduce_scatter | solution.py:441
  1139.7 32.2 %reduce-scatter.37.cloned.1.call-done = bf16[192,42]{1,0:T(8,128)(2,1)} async-done(((bf16[1536,42]{1,0:T(8,128)(2,1)}), bf16[192,42]{1,0:T(8,128)(2,1)}) %reduce-scatter.37.cloned.1.call-update) | async-done | bytes 16144
  1172.8 19.0 %psum.21 = bf16[192,42]{0,1:T(8,128)(2,1)S(1)} all-reduce(bf16[192,42]{0,1:T(8,128)(2,1)S(1)} %copy.529), channel_id=1, replica_groups=mesh['dp'=8,'expert'=4] {'expert'}, use_global_device_ids=true, to_apply=%region_75.76 | all-reduce | flops 8064 | bytes 32256 | tf_op jit(solution)/shard_map/psum | solution.py:499
  1193.0 91.5 %reduce-scatter.35.cloned.1.call-done = bf16[10,64,1536]{2,1,0:T(8,128)(2,1)} async-done(((bf16[10,512,1536]{2,1,0:T(8,128)(2,1)}), bf16[10,64,1536]{2,1,0:T(8,128)(2,1)}) %reduce-scatter.35.cloned.1.call-update) | async-done | bytes 1966096 | tf_op jit(solution)/shard_map/reduce_scatter | solution.py:441
  1288.5 108.7 %reduce-scatter.33.cloned.1.call-done = bf16[10,192,512]{2,1,0:T(8,128)(2,1)} async-done(((bf16[10,1536,512]{2,1,0:T(8,128)(2,1)}), bf16[10,192,512]{2,1,0:T(8,128)(2,1)}) %reduce-scatter.33.cloned.1.call-update) | async-done | bytes 1966096 | tf_op jit(solution)/shard_map/reduce_scatter | solution.py:441
  1401.2 108.6 %reduce-scatter.31.cloned.1.call-done = bf16[10,192,512]{2,1,0:T(8,128)(2,1)} async-done(((bf16[10,1536,512]{2,1,0:T(8,128)(2,1)}), bf16[10,192,512]{2,1,0:T(8,128)(2,1)}) %reduce-scatter.31.cloned.1.call-update) | async-done | bytes 1966096 | tf_op jit(solution)/shard_map/reduce_scatter | solution.py:441
  1513.8 67.9 %all-reduce.4.cloned.1.call-done = (bf16[192,2560]{1,0:T(8,128)(2,1)}, bf16[192,1536]{1,0:T(8,128)(2,1)}) async-done(((bf16[192,2560]{1,0:T(8,128)(2,1)}, bf16[192,1536]{1,0:T(8,128)(2,1)}), (bf16[192,2560]{1,0:T(8,128)(2,1)}, bf16[192,1536]{1,0:T(8,128)(2,1)})) %all-reduce.4.cloned.1.call-update) | async-done | bytes 1572880 | tf_op jit(solution)/shard_map/psum | solution.py:499
  (488 shorter events, 329.9 us)
Async XLA Ops:
  7.2 58.2 %all-gather.13.cloned.1.call-start = ((), (), s32[]{:S(2)}) async-start(), calls=%async_computation.12 | async-start | bytes 8847360 | tf_op jit(solution)/shard_map/all_gather | solution.py:360
  9.7 113.4 %all-gather.15.cloned.1.call-start = ((), (), s32[]{:S(2)}) async-start(), calls=%async_computation.13 | async-start | bytes 2621440 | tf_op jit(solution)/shard_map/all_gather | solution.py:360
  21.5 63.6 %copy-start.38 = (f32[256,32]{0,1:T(8,128)}, f32[256,32]{0,1:T(8,128)S(1)}, u32[]{:S(2)}) copy-start(f32[256,32]{0,1:T(8,128)S(1)} %get-tuple-element.1193) | copy-start | bytes 98308
  21.5 63.6 %copy-start.40 = (f32[256,32]{0,1:T(8,128)}, f32[256,32]{0,1:T(8,128)S(1)}, u32[]{:S(2)}) copy-start(f32[256,32]{0,1:T(8,128)S(1)} %get-tuple-element.1194) | copy-start | bytes 98308
  76.9 85.7 %all-gather.17.cloned.1.call-start = ((), (), s32[]{:S(2)}) async-start(), calls=%async_computation.14 | async-start | bytes 5308416 | tf_op jit(solution)/shard_map/all_gather | solution.py:360
  77.7 154.8 %all-gather.25.cloned.1.call-start = ((), (), s32[]{:S(2)}) async-start(), calls=%async_computation.29 | async-start | bytes 4259840 | tf_op jit(solution)/shard_map/all_gather | solution.py:360
  79.4 216.6 %all-gather.19.cloned.1.call-start = ((), (), s32[]{:S(2)}) async-start(), calls=%async_computation.15 | async-start | bytes 3932160 | tf_op jit(solution)/shard_map/all_gather | solution.py:360
  168.9 188.6 %all-gather.21.cloned.1.call-start = ((), (), s32[]{:S(2)}) async-start(), calls=%async_computation.17 | async-start | bytes 2621440 | tf_op jit(solution)/shard_map/all_gather | solution.py:360
  178.5 169.9 %copy-start.85 = (bf16[128]{0:T(256)(128)(2,1)}, bf16[128]{0:T(256)(128)(2,1)S(1)}, u32[]{:S(2)}) copy-start(bf16[128]{0:T(256)(128)(2,1)S(1)} %pad.43.clone) | copy-start | bytes 772
  178.5 63.7 %copy-start.91 = (s32[256]{0:T(256)}, s32[256]{0:T(256)S(1)}, u32[]{:S(2)}) copy-start(s32[256]{0:T(256)S(1)} %iota_add_fusion) | copy-start | bytes 3076
  243.3 176.9 %reduce-scatter.19.cloned.1.call-start = ((), (), s32[]{:S(2)}) async-start(), calls=%async_computation.20 | async-start | bytes 4259840 | tf_op jit(solution)/shard_map/reduce_scatter | solution.py:435
  356.3 134.1 %all-gather.27.cloned.1.call-start = ((), (), s32[]{:S(2)}) async-start(), calls=%async_computation.30 | async-start | bytes 4259840 | tf_op jit(solution)/shard_map/all_gather | solution.py:360
  357.1 197.1 %all-gather.23.cloned.1.call-start = ((), (), s32[]{:S(2)}) async-start(), calls=%async_computation.18 | async-start | bytes 3932160 | tf_op jit(solution)/shard_map/all_gather | solution.py:360
  357.3 64.1 %copy-start.51 = (pred[256,40]{1,0:T(32,128)(4,1)}, pred[256,40]{1,0:T(32,128)(4,1)S(1)}, u32[]{:S(2)}) copy-start(pred[256,40]{1,0:T(32,128)(4,1)S(1)} %copy.469) | copy-start | bytes 30724
  421.4 70.3 %copy-start.92 = (s32[256]{0:T(256)S(1)}, s32[256]{0:T(256)}, u32[]{:S(2)}) copy-start(s32[256]{0:T(256)} %copy-done.91) | copy-start | bytes 3076
  426.4 253.7 %reduce-scatter.23.cloned.1.call-start = ((), (), s32[]{:S(2)}) async-start(), calls=%async_computation.22 | async-start | bytes 4259840 | tf_op jit(solution)/shard_map/reduce_scatter | solution.py:435
  616.5 126.9 %reduce-scatter.15.cloned.1.call-start = ((), (), s32[]{:S(2)}) async-start(), calls=%async_computation.16 | async-start | bytes 3932160 | tf_op jit(solution)/shard_map/reduce_scatter | solution.py:435
  623.6 182.9 %reduce-scatter.17.cloned.1.call-start = ((), (), s32[]{:S(2)}) async-start(), calls=%async_computation.19 | async-start | bytes 3932160 | tf_op jit(solution)/shard_map/reduce_scatter | solution.py:435
  630.6 297.7 %reduce-scatter.25.cloned.1.call-start = ((), (), s32[]{:S(2)}) async-start(), calls=%async_computation.23 | async-start | bytes 2621440 | tf_op jit(solution)/shard_map/reduce_scatter | solution.py:476
  639.3 173.0 %copy-start.33 = (f32[256,40]{1,0:T(8,128)}, f32[256,40]{1,0:T(8,128)S(1)}, u32[]{:S(2)}) copy-start(f32[256,40]{1,0:T(8,128)S(1)} %get-tuple-element.1217) | copy-start | bytes 122884
  639.3 173.0 %copy-start.72 = (f32[256]{0:T(256)}, f32[256]{0:T(256)S(1)}, u32[]{:S(2)}) copy-start(f32[256]{0:T(256)S(1)} %get-tuple-element.1216) | copy-start | bytes 3076
  639.5 172.8 %copy-start.81 = (f32[256]{0:T(256)}, f32[256]{0:T(256)S(1)}, u32[]{:S(2)}) copy-start(f32[256]{0:T(256)S(1)} %fusion.207) | copy-start | bytes 3076
  862.0 143.0 %reduce-scatter.21.cloned.1.call-start = ((), (), s32[]{:S(2)}) async-start(), calls=%async_computation.21 | async-start | bytes 2621440 | tf_op jit(solution)/shard_map/reduce_scatter | solution.py:476
  915.9 165.8 %reduce-scatter.29.cloned.1.call-start = ((), (), s32[]{:S(2)}) async-start(), calls=%async_computation.25 | async-start | bytes 5308416 | tf_op jit(solution)/shard_map/reduce_scatter | solution.py:441
  921.6 212.9 %reduce-scatter.27.cloned.1.call-start = ((), (), s32[]{:S(2)}) async-start(), calls=%async_computation.24 | async-start | bytes 8847360 | tf_op jit(solution)/shard_map/reduce_scatter | solution.py:441
  923.7 82.7 %copy-start.44 = (bf16[256,24,64]{0,2,1:T(8,128)(2,1)}, bf16[256,24,64]{0,2,1:T(8,128)(2,1)S(1)}, u32[]{:S(2)}) copy-start(bf16[256,24,64]{0,2,1:T(8,128)(2,1)S(1)} %pad_maximum_fusion.11) | copy-start | bytes 2359300
  929.3 77.0 %copy-start.57 = (bf16[256,512]{0,1:T(8,128)(2,1)}, bf16[256,512]{0,1:T(8,128)(2,1)S(1)}, u32[]{:S(2)}) copy-start(bf16[256,512]{0,1:T(8,128)(2,1)S(1)} %get-tuple-element.1175) | copy-start | bytes 786436
  1022.4 149.5 %reduce-scatter.37.cloned.1.call-start = ((), (), s32[]{:S(2)}) async-start(), calls=%async_computation.31 | async-start | bytes 442368
  1040.5 244.0 %reduce-scatter.35.cloned.1.call-start = ((), (), s32[]{:S(2)}) async-start(), calls=%async_computation.28 | async-start | bytes 17694720 | tf_op jit(solution)/shard_map/reduce_scatter | solution.py:441
  1077.2 319.9 %reduce-scatter.33.cloned.1.call-start = ((), (), s32[]{:S(2)}) async-start(), calls=%async_computation.27 | async-start | bytes 17694720 | tf_op jit(solution)/shard_map/reduce_scatter | solution.py:441
  1078.0 431.8 %reduce-scatter.31.cloned.1.call-start = ((), (), s32[]{:S(2)}) async-start(), calls=%async_computation.26 | async-start | bytes 17694720 | tf_op jit(solution)/shard_map/reduce_scatter | solution.py:441
  1078.6 503.1 %all-reduce.4.cloned.1.call-start = ((), (), s32[]{:S(2)}) async-start(), calls=%async_computation.32 | async-start | bytes 3145728 | tf_op jit(solution)/shard_map/psum | solution.py:499
  (82 other events, 1008.0 us)
Sparse Core Ops, SparseCore 0:
  10.5 54.8 all-gather.12
  77.0 45.9 all-gather.14
  124.9 37.6 all-gather.16
  164.6 67.8 all-gather.24
  233.9 62.0 all-gather.18
  298.0 44.5 all-gather.20
  356.4 63.7 reduce-scatter.18
  422.3 68.0 all-gather.26
  492.0 62.1 all-gather.22
  616.7 63.3 reduce-scatter.22
  683.0 60.4 reduce-scatter.14
  746.2 60.2 reduce-scatter.16
  862.1 66.1 reduce-scatter.24
  931.1 73.8 reduce-scatter.20
  1008.2 53.1 reduce-scatter.28
  1065.2 69.3 reduce-scatter.26
  1138.0 33.8 reduce-scatter.36
  1175.3 109.1 reduce-scatter.34
  1288.0 109.1 reduce-scatter.32
  1400.5 109.1 reduce-scatter.30
  1512.2 69.4 all-reduce.3

commit v2 on v1

v2 whole, which is shorter than its diff:
```python
from functools import partial

import jax
import jax.numpy as jnp
from jax import lax
from jax.experimental import pallas as pl
from jax.experimental.pallas import tpu as pltpu
from jax.sharding import PartitionSpec as P

HEADS = 24
KV_HEADS = 8
HEAD = 64
FF = 512
EXPERTS = 40
TOP = 8
BLOCK = 256
SEQ = 1024
CAP = 64
QD = 1536
KD = 512

EPSILON = 1e-06
ROPE_BASE = 10000.0
NEGATIVE = -1e30
LANES = 128
COLUMNS = 256
VMEM_LIMIT = 56 * 2**20

BF = jnp.bfloat16
F32 = jnp.float32


def dense_dot(left, right):
    return jnp.dot(left, right, preferred_element_type=F32)


def left_dot(left, right):
    return lax.dot_general(left, right, (((0,), (0,)), ((), ())), preferred_element_type=F32)


def right_dot(left, right):
    return lax.dot_general(left, right, (((1,), (1,)), ((), ())), preferred_element_type=F32)


def rotary_tables(positions):
    half_size = HEAD // 2
    frequency = ROPE_BASE ** (-jnp.arange(half_size, dtype=F32) / half_size)
    angle = positions.astype(F32)[:, None] * frequency[None, :]
    cosine, sine = jnp.cos(angle), jnp.sin(angle)
    tiles = LANES // HEAD
    return (
        jnp.concatenate([cosine, cosine] * tiles, axis=1),
        jnp.concatenate([-sine, sine] * tiles, axis=1),
    )


def params(limit=VMEM_LIMIT):
    return pltpu.CompilerParams(vmem_limit_bytes=limit)


def swap_halves(values):
    lane = lax.broadcasted_iota(jnp.int32, values.shape, 1)
    half = HEAD // 2
    return jnp.where(
        lane % HEAD < half,
        pltpu.roll(values, LANES - half, 1),
        pltpu.roll(values, half, 1),
    )


def turn(values, cosine, sine):
    return values * cosine + swap_halves(values) * sine


def norm_kernel(x_ref, gain_ref, normed_ref, scale_ref):
    rows = x_ref[...].astype(F32)
    scale = lax.rsqrt(jnp.mean(rows * rows, axis=1, keepdims=True) + EPSILON)
    scale_ref[...] = scale
    normed_ref[...] = (rows * scale * gain_ref[...]).astype(BF)


def norm_rows(x, gain):
    total, features = x.shape
    return pl.pallas_call(
        norm_kernel,
        grid=(total // BLOCK,),
        in_specs=[
            pl.BlockSpec((BLOCK, features), lambda i: (i, 0)),
            pl.BlockSpec((1, features), lambda i: (0, 0)),
        ],
        out_specs=[
            pl.BlockSpec((BLOCK, features), lambda i: (i, 0)),
            pl.BlockSpec((BLOCK, 1), lambda i: (i, 0)),
        ],
        out_shape=[
            jax.ShapeDtypeStruct((total, features), BF),
            jax.ShapeDtypeStruct((total, 1), F32),
        ],
        compiler_params=params(),
        cost_estimate=pl.CostEstimate(flops=5 * total * features, bytes_accessed=4 * total * features, transcendentals=0),
        name="norm",
    )(x, gain)


def project_kernel(turned, normed_ref, w_ref, cosine_ref, sine_ref, *outs):
    tile = w_ref.shape[1]
    rows = dense_dot(normed_ref[...], w_ref[...])

    def write(turning):
        for start in range(0, tile, LANES):
            for m, out_ref in enumerate(outs):
                part = rows[m * BLOCK : (m + 1) * BLOCK, start : start + LANES]
                if turning:
                    part = turn(part, cosine_ref[...], sine_ref[...])
                out_ref[:, start : start + LANES] = part.astype(BF)

    pl.when(pl.program_id(0) < turned)(lambda: write(True))
    pl.when(pl.program_id(0) >= turned)(lambda: write(False))


def project(normed, weight, columns, turned_columns, cosine, sine):
    total, features = normed.shape
    tile = 2 * COLUMNS
    micros = total // BLOCK
    return pl.pallas_call(
        partial(project_kernel, turned_columns // tile),
        grid=(columns // tile,),
        in_specs=[
            pl.BlockSpec((total, features), lambda j: (0, 0)),
            pl.BlockSpec((features, tile), lambda j: (0, j)),
            pl.BlockSpec((BLOCK, LANES), lambda j: (0, 0)),
            pl.BlockSpec((BLOCK, LANES), lambda j: (0, 0)),
        ],
        out_specs=[pl.BlockSpec((BLOCK, tile), lambda j: (0, j))] * micros,
        out_shape=[jax.ShapeDtypeStruct((BLOCK, columns), BF)] * micros,
        compiler_params=params(),
        cost_estimate=pl.CostEstimate(
            flops=2 * total * features * columns,
            bytes_accessed=2 * (features * columns + total * (features + columns)),
            transcendentals=0,
        ),
        name="project",
    )(normed, weight, cosine, sine)


def outward_kernel(ob_ref, w_ref, x_ref, gain_ref, router_ref, routes_ref, mid_ref, sent_ref, scale_ref, gates_ref):
    j = pl.program_id(0)
    tile = w_ref.shape[1]
    features = mid_ref.shape[1]
    where = pl.ds(pl.multiple_of(j * tile, tile), tile)
    mid_ref[:, where] = x_ref[:, where].astype(F32) + dense_dot(ob_ref[...], w_ref[...])

    @pl.when(j == pl.num_programs(0) - 1)
    def _():
        mid = mid_ref[...]
        scale = lax.rsqrt(jnp.mean(mid * mid, axis=1, keepdims=True) + EPSILON)
        scale_ref[...] = scale
        normed = (mid * scale * gain_ref[...]).astype(BF)
        sent_ref[:, :features] = normed
        lane = lax.broadcasted_iota(jnp.int32, (BLOCK, LANES), 1)
        routes = routes_ref[...]
        member = lane == routes[:, 0:1]
        for k in range(1, TOP):
            member = jnp.logical_or(member, lane == routes[:, k : k + 1])
        logits = jnp.where(member, dense_dot(normed, router_ref[...]), NEGATIVE)
        weights = jnp.exp(logits - jnp.max(logits, axis=1, keepdims=True))
        weights = jnp.where(member, weights, 0.0)
        gates = weights / jnp.sum(weights, axis=1, keepdims=True)
        gates_ref[...] = gates
        high = gates.astype(BF).astype(F32)
        sent_ref[:, features:] = (high + pltpu.roll(gates - high, EXPERTS, 1)).astype(BF)


def outward(ob, w_qo, x, gain, router, routes):
    features = x.shape[1]
    tile = 2 * COLUMNS
    whole = lambda a: pl.BlockSpec(a.shape, lambda j: (0, 0))
    fixed = lambda *shape: pl.BlockSpec(shape, lambda j: (0, 0))
    return pl.pallas_call(
        outward_kernel,
        grid=(features // tile,),
        in_specs=[
            whole(ob),
            pl.BlockSpec((QD, tile), lambda j: (0, QD // tile + j)),
            whole(x), whole(gain), whole(router), whole(routes),
        ],
        out_specs=[fixed(BLOCK, features), fixed(BLOCK, features + LANES), fixed(BLOCK, 1), fixed(BLOCK, LANES)],
        out_shape=[
            jax.ShapeDtypeStruct((BLOCK, features), F32),
            jax.ShapeDtypeStruct((BLOCK, features + LANES), BF),
            jax.ShapeDtypeStruct((BLOCK, 1), F32),
            jax.ShapeDtypeStruct((BLOCK, LANES), F32),
        ],
        compiler_params=params(),
        cost_estimate=pl.CostEstimate(
            flops=2 * BLOCK * features * QD, bytes_accessed=2 * features * QD + 14 * BLOCK * features, transcendentals=0
        ),
        name="outward",
    )(ob, w_qo, x, gain, router, routes)


def home_kernel(
    dx_ref, gates_ref, mid_ref, scale_ref, dy_ref, router_ref, gain_ref, w_ref,
    dmid_ref, da_ref, dob_ref, dlog_ref, dgain_ref,
):
    j = pl.program_id(0)
    features = mid_ref.shape[1]
    tile = w_ref.shape[0]

    @pl.when(j == 0)
    def _():
        table = dx_ref[:, features:].astype(F32)
        dgates = table + pltpu.roll(table, LANES - EXPERTS, 1)
        gates = gates_ref[...]
        dc = gates * (dgates - jnp.sum(gates * dgates, axis=1, keepdims=True))
        dlog = dc.astype(BF)
        dlog_ref[...] = dlog
        dnormed = dx_ref[:, :features].astype(F32) + right_dot(dlog, router_ref[...])
        mid = mid_ref[...]
        scale = scale_ref[...]
        dgain_ref[...] = jnp.sum(dnormed * mid * scale, axis=0, keepdims=True)
        scaled = dnormed * gain_ref[...]
        mean = jnp.mean(scaled * mid, axis=1, keepdims=True)
        dmid = dy_ref[...].astype(F32) + scale * scaled - mid * (scale * scale * scale * mean)
        dmid_ref[...] = dmid
        da_ref[...] = dmid.astype(BF)

    where = pl.ds(pl.multiple_of(j * tile, tile), tile)
    dob_ref[:, where] = right_dot(da_ref[...], w_ref[...]).astype(BF)


def home_back(dx, gates, mid, scale, dy, router, gain, w_qo):
    features = mid.shape[1]
    tile = 2 * COLUMNS
    whole = lambda a: pl.BlockSpec(a.shape, lambda j: (0, 0))
    fixed = lambda *shape: pl.BlockSpec(shape, lambda j: (0, 0))
    return pl.pallas_call(
        home_kernel,
        grid=(QD // tile,),
        in_specs=[
            whole(dx), whole(gates), whole(mid), whole(scale), whole(dy), whole(router), whole(gain),
            pl.BlockSpec((tile, features), lambda j: (j, 1)),
        ],
        out_specs=[
            fixed(BLOCK, features), fixed(BLOCK, features), fixed(BLOCK, QD), fixed(BLOCK, LANES), fixed(1, features),
        ],
        out_shape=[
            jax.ShapeDtypeStruct((BLOCK, features), F32),
            jax.ShapeDtypeStruct((BLOCK, features), BF),
            jax.ShapeDtypeStruct((BLOCK, QD), BF),
            jax.ShapeDtypeStruct((BLOCK, LANES), BF),
            jax.ShapeDtypeStruct((1, features), F32),
        ],
        compiler_params=params(),
        cost_estimate=pl.CostEstimate(
            flops=2 * BLOCK * features * QD, bytes_accessed=2 * features * QD + 18 * BLOCK * features, transcendentals=0
        ),
        name="home_back",
    )(dx, gates, mid, scale, dy, router, gain, w_qo)


def last_kernel(
    dq_ref, dkv_ref, cosine_ref, sine_ref, wq_ref, wkv_ref, x_ref, scale_ref, gain_ref, dmid_ref,
    dx_ref, dkvb_ref, dgain_ref,
):
    j = pl.program_id(0)
    tile = wq_ref.shape[0]

    @pl.when(j == 0)
    def _():
        for start in range(0, KD, LANES):
            part = dkv_ref[0, :, start : start + LANES].astype(F32)
            dkvb_ref[:, start : start + LANES] = turn(part, cosine_ref[...], -sine_ref[...]).astype(BF)
        dkvb_ref[:, KD:] = dkv_ref[1]

    where = pl.ds(pl.multiple_of(j * tile, tile), tile)
    dx_ref[:, where] = right_dot(dq_ref[...], wq_ref[...]) + right_dot(dkvb_ref[...], wkv_ref[...])

    @pl.when(j == pl.num_programs(0) - 1)
    def _():
        dnormed = dx_ref[...]
        rows = x_ref[...].astype(F32)
        scale = scale_ref[...]
        dgain_ref[...] = jnp.sum(dnormed * rows * scale, axis=0, keepdims=True)
        scaled = dnormed * gain_ref[...]
        mean = jnp.mean(scaled * rows, axis=1, keepdims=True)
        dx_ref[...] = dmid_ref[...] + scale * scaled - rows * (scale * scale * scale * mean)


def last_back(dq, dkv, cosine, sine, w_q, w_kv, x, scale, gain, dmid):
    features = x.shape[1]
    tile = 2 * COLUMNS
    whole = lambda a: pl.BlockSpec(a.shape, lambda j: (0,) * a.ndim)
    fixed = lambda *shape: pl.BlockSpec(shape, lambda j: (0, 0))
    return pl.pallas_call(
        last_kernel,
        grid=(features // tile,),
        in_specs=[
            whole(dq), whole(dkv), whole(cosine), whole(sine),
            pl.BlockSpec((tile, QD), lambda j: (j, 0)),
            pl.BlockSpec((tile, 2 * KD), lambda j: (j, 0)),
            whole(x), whole(scale), whole(gain), whole(dmid),
        ],
        out_specs=[fixed(BLOCK, features), fixed(BLOCK, 2 * KD), fixed(1, features)],
        out_shape=[
            jax.ShapeDtypeStruct((BLOCK, features), F32),
            jax.ShapeDtypeStruct((BLOCK, 2 * KD), BF),
            jax.ShapeDtypeStruct((1, features), F32),
        ],
        compiler_params=params(),
        cost_estimate=pl.CostEstimate(
            flops=2 * BLOCK * features * (QD + 2 * KD),
            bytes_accessed=2 * features * (QD + 2 * KD) + 16 * BLOCK * features,
            transcendentals=0,
        ),
        name="last_back",
    )(dq, dkv, cosine, sine, w_q, w_kv, x, scale, gain, dmid)


def halves(core_ref, held_ref, step, keep_ref, send_ref):
    core = core_ref[0]
    for q in range(held_ref.shape[0] // (2 * step)):
        mine = pl.multiple_of((2 * q + core) * step, step)
        other = pl.multiple_of((2 * q + 1 - core) * step, step)
        keep_ref[q * step : (q + 1) * step, :] = held_ref[pl.ds(mine, step), :]
        send_ref[q * step : (q + 1) * step, :] = held_ref[pl.ds(other, step), :]


def dense_kernel(micros, step, core_ref, *refs):
    ins, (gains_ref, keep_ref, send_ref, held_ref) = refs[: 7 * micros], refs[7 * micros :]
    normed, dq, dkv, sent, dlog, ob, da = (ins[i * micros : (i + 1) * micros] for i in range(7))

    def total(lefts, rights):
        return sum(left_dot(left[...], right[...]) for left, right in zip(lefts, rights))

    start = 0
    for lefts, rights in ((normed, dq), (normed, dkv), (sent, dlog), (ob, da)):
        width = rights[0].shape[1]
        part = total(lefts, rights)
        if rights is dlog:
            part = part + gains_ref[...]
        held_ref[:, start : start + width] = part.astype(BF)
        start += width
    halves(core_ref, held_ref, step, keep_ref, send_ref)


def dense_grads(core, step, normed, dq, dkv, sent, dlog, ob, da, gains):
    groups = (normed, dq, dkv, sent, dlog, ob, da)
    micros = len(dq)
    tile = max(3 * LANES, 2 * step)
    lefts = (True, False, False, True, False, True, False)
    width = sum(group[0].shape[1] for group, left in zip(groups, lefts) if not left)
    specs = []
    for group, left in zip(groups, lefts):
        for m, a in enumerate(group):
            if left:
                block = m if a.shape[0] > BLOCK else 0
                specs.append(pl.BlockSpec((BLOCK, tile), lambda j, s, block=block: (block, j)))
            else:
                specs.append(pl.BlockSpec(a.shape, lambda j, s: (0, 0)))
    half = jax.ShapeDtypeStruct((QD // 2, width), BF)
    return pl.pallas_call(
        partial(dense_kernel, micros, step),
        grid_spec=pltpu.PrefetchScalarGridSpec(
            num_scalar_prefetch=1,
            grid=(QD // tile,),
            in_specs=[*specs, pl.BlockSpec((tile, gains.shape[1]), lambda j, s: (j, 0))],
            out_specs=[pl.BlockSpec((tile // 2, width), lambda j, s: (j, 0))] * 2,
            scratch_shapes=[pltpu.VMEM((tile, width), BF)],
        ),
        out_shape=[half, half],
        compiler_params=params(),
        cost_estimate=pl.CostEstimate(
            flops=2 * micros * BLOCK * QD * width,
            bytes_accessed=2 * QD * width + 4 * micros * BLOCK * (QD + width),
            transcendentals=0,
        ),
        name="dense_grads",
    )(core, *[a for group in groups for a in group], gains)


PAIR = 2 * HEAD
GROUP = HEADS // KV_HEADS * PAIR


def spread(values):
    lane = lax.broadcasted_iota(jnp.int32, (BLOCK, LANES), 1)
    first = lane < HEAD
    zero = jnp.zeros((BLOCK, LANES), F32)
    one, two, three = (values[:, i * LANES : (i + 1) * LANES] for i in range(3))
    return jnp.concatenate(
        [
            jnp.where(first, one, zero),
            jnp.where(first, pltpu.roll(one, HEAD, 1), zero),
            jnp.where(first, two, zero),
            jnp.where(first, zero, two),
            jnp.where(first, zero, pltpu.roll(three, HEAD, 1)),
            jnp.where(first, zero, three),
        ],
        axis=0,
    )


def gather_heads(rows):
    lane = lax.broadcasted_iota(jnp.int32, (BLOCK, LANES), 1)
    first = lane < HEAD
    part = [rows[i * BLOCK : (i + 1) * BLOCK] for i in range(6)]
    return (
        jnp.where(first, part[0], pltpu.roll(part[1], HEAD, 1)),
        jnp.where(first, part[2], part[3]),
        jnp.where(first, pltpu.roll(part[4], HEAD, 1), part[5]),
    )


def attend_kernel(place_ref, q_ref, *refs):
    blocks = SEQ // BLOCK
    keys, values = refs[:blocks], refs[blocks : 2 * blocks]
    o_ref, ob_ref, lse_ref, max_ref, sum_ref, acc_ref = refs[2 * blocks :]
    query = spread(q_ref[...].astype(F32) * HEAD ** (-0.5)).astype(BF)
    for r in range(blocks):

        @pl.when(place_ref[0] >= r)
        def _():
            scores = right_dot(keys[r][...], query)
            top = jnp.max(scores, axis=0, keepdims=True)
            if r > 0:
                before = max_ref[...]
                top = jnp.maximum(top, before)
            weights = jnp.exp(scores - top)
            total = jnp.sum(weights, axis=0, keepdims=True)
            out = left_dot(values[r][...], weights.astype(BF))
            if r > 0:
                factor = jnp.exp(before - top)
                total = total + sum_ref[...] * factor
                out = out + acc_ref[...] * factor
            max_ref[...] = top
            sum_ref[...] = total
            acc_ref[...] = out

    lse_ref[0] = max_ref[...] + jnp.log(sum_ref[...])
    rows = jnp.transpose(acc_ref[...] / sum_ref[...])
    for i, part in enumerate(gather_heads(rows)):
        o_ref[:, i * LANES : (i + 1) * LANES] = part
        ob_ref[:, i * LANES : (i + 1) * LANES] = part.astype(BF)


def attend(place, query, kvs):
    pairs = KV_HEADS // 2
    rows = 6 * BLOCK
    return pl.pallas_call(
        attend_kernel,
        grid_spec=pltpu.PrefetchScalarGridSpec(
            num_scalar_prefetch=1,
            grid=(pairs,),
            in_specs=[
                pl.BlockSpec((BLOCK, GROUP), lambda p, s: (0, p)),
                *[pl.BlockSpec((BLOCK, PAIR), lambda p, s: (0, p)) for _ in kvs],
                *[pl.BlockSpec((BLOCK, PAIR), lambda p, s: (0, KV_HEADS // 2 + p)) for _ in kvs],
            ],
            out_specs=[
                pl.BlockSpec((BLOCK, GROUP), lambda p, s: (0, p)),
                pl.BlockSpec((BLOCK, GROUP), lambda p, s: (0, p)),
                pl.BlockSpec((1, 1, rows), lambda p, s: (p, 0, 0)),
            ],
            scratch_shapes=[
                pltpu.VMEM((1, rows), F32),
                pltpu.VMEM((1, rows), F32),
                pltpu.VMEM((PAIR, rows), F32),
            ],
        ),
        out_shape=[
            jax.ShapeDtypeStruct((BLOCK, QD), F32),
            jax.ShapeDtypeStruct((BLOCK, QD), BF),
            jax.ShapeDtypeStruct((pairs, 1, rows), F32),
        ],
        compiler_params=params(),
        cost_estimate=pl.CostEstimate(
            flops=8 * SEQ * BLOCK * HEADS * PAIR, bytes_accessed=10 * BLOCK * QD, transcendentals=SEQ * BLOCK * HEADS
        ),
        name="attend",
    )(place, query, *kvs, *kvs)


def attend_back_kernel(place_ref, q_ref, dob_ref, o_ref, lse_ref, cosine_ref, sine_ref, *refs):
    blocks = SEQ // BLOCK
    keys, values = refs[:blocks], refs[blocks : 2 * blocks]
    dq_ref, outs, acc_ref = refs[2 * blocks], refs[2 * blocks + 1 : 3 * blocks + 1], refs[-1]
    query = spread(q_ref[...].astype(F32) * HEAD ** (-0.5)).astype(BF)
    grads = spread(dob_ref[...].astype(F32))
    delta = jnp.sum(jnp.transpose(grads * spread(o_ref[...])), axis=0, keepdims=True)
    grads = grads.astype(BF)
    for r in range(blocks):

        @pl.when(place_ref[0] >= r)
        def _():
            key = keys[r][...]
            weights = jnp.exp(right_dot(key, query) - lse_ref[0])
            dscores = (weights * (right_dot(values[r][...], grads) - delta)).astype(BF)
            outs[r][0] = dense_dot(dscores, query).astype(BF)
            outs[r][1] = dense_dot(weights.astype(BF), grads).astype(BF)
            part = left_dot(key, dscores)
            acc_ref[...] = part if r == 0 else acc_ref[...] + part

        @pl.when(place_ref[0] < r)
        def _():
            outs[r][...] = jnp.zeros(outs[r].shape, BF)

    rows = jnp.transpose(acc_ref[...]) * HEAD ** (-0.5)
    for i, part in enumerate(gather_heads(rows)):
        dq_ref[:, i * LANES : (i + 1) * LANES] = turn(part, cosine_ref[...], -sine_ref[...]).astype(BF)


def attend_back(place, query, dob, o, lse, cosine, sine, kvs):
    pairs = KV_HEADS // 2
    rows = 6 * BLOCK
    heads = pl.BlockSpec((BLOCK, GROUP), lambda p, s: (0, p))
    table = pl.BlockSpec((BLOCK, LANES), lambda p, s: (0, 0))
    return pl.pallas_call(
        attend_back_kernel,
        grid_spec=pltpu.PrefetchScalarGridSpec(
            num_scalar_prefetch=1,
            grid=(pairs,),
            in_specs=[
                heads, heads, heads,
                pl.BlockSpec((1, 1, rows), lambda p, s: (p, 0, 0)),
                table, table,
                *[pl.BlockSpec((BLOCK, PAIR), lambda p, s: (0, p)) for _ in kvs],
                *[pl.BlockSpec((BLOCK, PAIR), lambda p, s: (0, KV_HEADS // 2 + p)) for _ in kvs],
            ],
            out_specs=[heads, *[pl.BlockSpec((2, BLOCK, PAIR), lambda p, s: (0, 0, p)) for _ in kvs]],
            scratch_shapes=[pltpu.VMEM((PAIR, rows), F32)],
        ),
        out_shape=[
            jax.ShapeDtypeStruct((BLOCK, QD), BF),
            *[jax.ShapeDtypeStruct((2, BLOCK, KD), BF) for _ in kvs],
        ],
        compiler_params=params(),
        cost_estimate=pl.CostEstimate(
            flops=20 * SEQ * BLOCK * HEADS * PAIR, bytes_accessed=14 * BLOCK * QD, transcendentals=SEQ * BLOCK * HEADS
        ),
        name="attend_back",
    )(place, query, dob, o, lse, cosine, sine, *kvs, *kvs)


def picks(slot_rows):
    slots = lax.broadcasted_iota(jnp.int32, (CAP, BLOCK), 0).astype(F32)
    one, zero = jnp.float32(1), jnp.float32(0)
    return [jnp.where(slots == slot_rows[e : e + 1, :], one, zero) for e in range(slot_rows.shape[0])]


def dispatch_kernel(slot_ref, rows_ref, out_ref):
    experts = slot_ref.shape[0]
    chosen = jnp.concatenate([p.astype(BF) for p in picks(slot_ref[...])], axis=0)
    width = out_ref.shape[2]
    for start in range(0, width, COLUMNS):
        size = min(COLUMNS, width - start)
        rows = dense_dot(chosen, rows_ref[:, start : start + size])
        out_ref[:, :, start : start + size] = rows.astype(BF).reshape(experts, CAP, size)


def dispatch(slot_rows, rows, features):
    experts, total = slot_rows.shape
    blocks = total // BLOCK
    return pl.pallas_call(
        dispatch_kernel,
        grid=(blocks,),
        in_specs=[
            pl.BlockSpec((experts, BLOCK), lambda b: (0, b)),
            pl.BlockSpec((BLOCK, features), lambda b: (b, 0)),
        ],
        out_specs=pl.BlockSpec((experts, CAP, features), lambda b: (0, b, 0)),
        out_shape=jax.ShapeDtypeStruct((experts, blocks * CAP, features), BF),
        compiler_params=params(),
        cost_estimate=pl.CostEstimate(
            flops=2 * experts * CAP * total * features,
            bytes_accessed=2 * features * (total + experts * blocks * CAP),
            transcendentals=0,
        ),
        name="dispatch",
    )(slot_rows, rows)


def combine_kernel(slot_ref, slots_ref, out_ref):
    experts, features = slots_ref.shape[0], slots_ref.shape[2]
    chosen = jnp.concatenate([p.astype(BF) for p in picks(slot_ref[...])], axis=0)
    for start in range(0, features, COLUMNS):
        size = min(COLUMNS, features - start)
        held = slots_ref[:, :, start : start + size].reshape(experts * CAP, size)
        out_ref[:, start : start + size] = left_dot(chosen, held).astype(BF)


def combine(slot_rows, slots):
    experts, total = slot_rows.shape
    blocks = total // BLOCK
    features = slots.shape[2]
    return pl.pallas_call(
        combine_kernel,
        grid=(blocks,),
        in_specs=[
            pl.BlockSpec((experts, BLOCK), lambda b: (0, b)),
            pl.BlockSpec((experts, CAP, features), lambda b: (0, b, 0)),
        ],
        out_specs=pl.BlockSpec((BLOCK, features), lambda b: (b, 0)),
        out_shape=jax.ShapeDtypeStruct((total, features), BF),
        compiler_params=params(),
        cost_estimate=pl.CostEstimate(
            flops=2 * experts * CAP * total * features,
            bytes_accessed=2 * features * (total + experts * blocks * CAP),
            transcendentals=0,
        ),
        name="combine",
    )(slot_rows, slots)


def expert_kernel(
    rank_ref, x_ref, dy_ref, wg_ref, wu_ref, wd_ref, ys_ref, dx_ref, gdy_ref, act_ref, dg_ref, du_ref
):
    features = dy_ref.shape[2]
    rows = x_ref[0, :, :features]
    pre = dense_dot(rows, wg_ref[0])
    up = dense_dot(rows, wu_ref[0])
    sigma = 1.0 / (1.0 + jnp.exp(-pre))
    silu = pre * sigma
    active = (silu * up).astype(BF)
    act_ref[0] = active
    column = rank_ref[0] * pl.num_programs(0) + pl.program_id(0)
    lane = lax.broadcasted_iota(jnp.int32, (rows.shape[0], LANES), 1)
    is_high, is_low = lane == column, lane == column + EXPERTS
    table = jnp.where(jnp.logical_or(is_high, is_low), x_ref[0, :, features:].astype(F32), 0.0)
    share = jnp.sum(table, axis=1, keepdims=True)
    result = dense_dot(active, wd_ref[0])
    grads = dy_ref[0].astype(F32)
    dots = jnp.sum(result * grads, axis=1, keepdims=True)
    high = dots.astype(BF).astype(F32)
    dx_ref[0, :, features:] = jnp.where(is_high, high, jnp.where(is_low, dots - high, 0.0)).astype(BF)
    ys_ref[0] = (result * share).astype(BF)
    gated = (grads * share).astype(BF)
    gdy_ref[0] = gated
    dact = right_dot(gated, wd_ref[0])
    dpre = (dact * up * sigma * (1.0 + pre * (1.0 - sigma))).astype(BF)
    dup = (dact * silu).astype(BF)
    dg_ref[0] = dpre
    du_ref[0] = dup
    dx_ref[0, :, :features] = (right_dot(dpre, wg_ref[0]) + right_dot(dup, wu_ref[0])).astype(BF)


def expert_pass(rank, x_slots, dy_slots, w_gate, w_up, w_down):
    experts, rows, features = dy_slots.shape
    hidden = w_gate.shape[2]
    one = lambda e, r: (e, 0, 0)
    longer = pl.BlockSpec((1, rows, features + LANES), one)
    wide = pl.BlockSpec((1, rows, features), one)
    narrow = pl.BlockSpec((1, rows, hidden), one)
    shape = lambda width: jax.ShapeDtypeStruct((experts, rows, width), BF)
    return pl.pallas_call(
        expert_kernel,
        grid_spec=pltpu.PrefetchScalarGridSpec(
            num_scalar_prefetch=1,
            grid=(experts,),
            in_specs=[
                longer, wide,
                pl.BlockSpec((1, features, hidden), one),
                pl.BlockSpec((1, features, hidden), one),
                pl.BlockSpec((1, hidden, features), one),
            ],
            out_specs=[wide, longer, wide, narrow, narrow, narrow],
        ),
        out_shape=[
            shape(features), shape(features + LANES), shape(features), shape(hidden), shape(hidden), shape(hidden)
        ],
        compiler_params=params(),
        cost_estimate=pl.CostEstimate(
            flops=12 * experts * rows * features * hidden,
            bytes_accessed=6 * experts * features * hidden + 10 * experts * rows * features,
            transcendentals=experts * rows * hidden,
        ),
        name="experts",
    )(rank, x_slots, dy_slots, w_gate, w_up, w_down)


def weight_kernel(count, products, step, core_ref, *refs):
    lefts, rights = refs[:count], refs[count : count * (1 + products)]
    outs, held_ref = refs[count * (1 + products) : -1], refs[-1]
    for i in range(products):
        total = sum(left_dot(lefts[m][0], rights[i * count + m][0]) for m in range(count))
        held_ref[...] = total.astype(BF)
        halves(core_ref, held_ref, step, outs[2 * i].at[0], outs[2 * i + 1].at[0])


def weight_pass(core, step, depth, lefts, *rights):
    experts, rows, width = rights[0][0].shape
    one = lambda e, s: (e, 0, 0)
    count, products = len(lefts), len(rights)
    half = jax.ShapeDtypeStruct((experts, depth // 2, width), BF)
    return pl.pallas_call(
        partial(weight_kernel, count, products, step),
        grid_spec=pltpu.PrefetchScalarGridSpec(
            num_scalar_prefetch=1,
            grid=(experts,),
            in_specs=[
                *[pl.BlockSpec((1, rows, depth), one) for _ in lefts],
                *[pl.BlockSpec((1, rows, width), one) for right in rights for _ in right],
            ],
            out_specs=[pl.BlockSpec((1, depth // 2, width), one)] * (2 * products),
            scratch_shapes=[pltpu.VMEM((depth, width), BF)],
        ),
        out_shape=[half] * (2 * products),
        compiler_params=params(),
        cost_estimate=pl.CostEstimate(
            flops=2 * count * products * experts * rows * depth * width,
            bytes_accessed=2 * experts * (products * depth * width + count * rows * (depth + products * width)),
            transcendentals=0,
        ),
        name="expert_weights",
    )(core, *lefts, *[a for right in rights for a in right])


def after(value, *marks):
    return lax.optimization_barrier((value, *marks))[0]


def together(*values):
    return lax.optimization_barrier(values)


def local(
    tokens, out_grad, routes, attn_gain, w_query, w_key, w_value, w_out, moe_gain, w_router,
    w_gate, w_up, w_down,
):
    micros, _, features = tokens.shape
    count = lax.axis_size("expert")
    rank = lax.axis_index("expert")
    exp_dev = w_gate.shape[0]
    dp = lax.axis_size("dp")
    core = (lax.axis_index("dp") % 2).astype(jnp.int32)[None]
    seq_blocks = SEQ // BLOCK
    place = rank % seq_blocks
    cosine, sine = rotary_tables(place * BLOCK + jnp.arange(BLOCK, dtype=jnp.int32))
    place = place.astype(jnp.int32)[None]
    around = [(i, (i + 1) % count) for i in range(count)]
    upward = [(i, i + 1) for i in range(count - 1) if (i + 1) % seq_blocks]
    downward = [(b, a) for a, b in upward]
    ring = lambda a: lax.ppermute(a, "expert", around)
    later = lambda a: lax.ppermute(a, "expert", upward)
    earlier = lambda a: lax.ppermute(a, "expert", downward)
    add = lambda a, b: (a.astype(F32) + b.astype(F32)).astype(BF)
    every = lambda a, axis: lax.all_gather(a, axis, axis=0, tiled=True)
    swap = lambda a: lax.ppermute(a, "dp", [(i, i ^ 1) for i in range(dp)])
    same_core = [list(range(c, dp, 2)) for c in range(2)]
    share = lambda a, dim: lax.psum_scatter(
        a, "dp", scatter_dimension=dim, axis_index_groups=same_core, tiled=True
    )

    beside = jnp.zeros((w_router.shape[0], LANES - EXPERTS - 2), BF)
    kv_w = every(
        jnp.concatenate([w_key, w_value, w_router, attn_gain[:, None], moe_gain[:, None], beside], axis=1), "dp"
    )
    qo_w = every(after(jnp.concatenate([w_query, w_out], axis=1), kv_w), "dp")
    router_w = kv_w[:, 2 * KD :]
    gains = router_w[:, EXPERTS : EXPERTS + 2].T.astype(F32)
    gain_one, gain_two = gains[0:1], gains[1:2]

    members = jnp.any(routes[:, :, :, None] == jnp.arange(EXPERTS, dtype=jnp.int32), axis=2)
    before = jnp.tril(jnp.ones((BLOCK, BLOCK), F32), -1).astype(BF)
    slots = jnp.einsum("ts,mse->mte", before, members.astype(BF), preferred_element_type=F32)
    slots = jnp.where(members, slots, -1.0).astype(BF)
    dy_ring = [
        jnp.concatenate([out_grad, slots, jnp.zeros((micros, BLOCK, LANES - EXPERTS), BF)], axis=2)
    ]

    dy_ring.append(ring(dy_ring[0]))
    x_whole = tokens.reshape(micros * BLOCK, features)
    normed, scale_one = norm_rows(x_whole, gain_one)
    normed_one, dy_ring[1] = together(normed, dy_ring[1])
    kv_own = project(normed_one, kv_w, 2 * KD, KD, cosine, sine)
    dy_ring.append(ring(dy_ring[1]))
    kvs = [[kv_own[0]]]
    for _ in range(seq_blocks - 1):
        kvs[0].append(later(kvs[0][-1]))
    normed_two, dy_ring[2] = together(normed, dy_ring[2])
    queries = project(normed_two, qo_w, QD, QD, cosine, sine)
    while len(dy_ring) < count:
        dy_ring.append(ring(dy_ring[-1]))

    heads, mids, sent = [], [], []
    held = [after(kv_own[1], kvs[0][-1])]
    held.append(later(held[-1]))
    for m in range(micros):
        o, ob, lse = attend(place, queries[m], kvs[m])
        if m == 0:
            held[-1], o, ob, lse = together(held[-1], o, ob, lse)
            held.append(later(held[-1]))
            ob, dy_ring[-1] = together(ob, dy_ring[-1])
        heads.append((o, ob, lse))
        mid, out, scale_two, gates = outward(ob, qo_w, tokens[m], gain_two, router_w, routes[m])
        mids.append((mid, out, scale_two, gates))
        sent.append(every(out, "expert"))
        if m == 0:
            held[-1], out = together(held[-1], out)
            while len(held) < seq_blocks:
                held.append(later(held[-1]))
            kvs.append(held)

    def in_order(m):
        whole = jnp.zeros((count * BLOCK, features + LANES), BF)
        for step, block in enumerate(dy_ring):
            whole = lax.dynamic_update_slice_in_dim(whole, block[m], (rank - step) % count * BLOCK, 0)
        return whole

    parts, slot_rows, scaled, dx_sums, dx_home = [], [], [], [], []
    for m in range(micros):
        dy_all = in_order(m)
        table = lax.dynamic_slice_in_dim(dy_all, features + rank * exp_dev, exp_dev, 1)
        slot_rows.append(table.astype(F32).T)
        dy_slots = dispatch(slot_rows[m], dy_all, features)
        x_slots = dispatch(slot_rows[m], sent[m], features + LANES)
        if m > 0:
            x_slots, dx_sums[-1] = together(x_slots, dx_sums[-1])
        ys, dx, *rest = expert_pass(rank.astype(jnp.int32)[None], x_slots, dy_slots, w_gate, w_up, w_down)
        parts.append((x_slots, *rest))
        scaled.append(ys)
        dx_sums.append(combine(slot_rows[m], dx))
    for a in dx_sums:
        dx_home.append(lax.psum_scatter(a, "expert", scatter_dimension=0, tiled=True))

    xs, gdys, acts, dgs, dus = zip(*parts)
    hidden = w_down.shape[1]
    first_act, dx_home[0], _ = together(acts[0], dx_home[0], dx_sums[-1])
    keep_down, send_down = weight_pass(core, hidden // dp, hidden, (first_act, *acts[1:]), gdys)
    got_down = swap(send_down)
    dgs = after(dgs[0], keep_down), *dgs[1:]
    ups = weight_pass(core, features // dp, features, xs, dgs, dus)
    got_down, *ups = together(got_down, *ups)
    down_half = add(keep_down, got_down)
    down_grad = share(down_half, 1)
    got_gate, got_up = swap(ups[1]), swap(ups[3])

    def back_home(m, dx):
        mid, _, scale_two, gates = mids[m]
        return home_back(dx, gates, mid, scale_two, out_grad[m], router_w, gain_two, qo_w)

    def back_heads(m, dob):
        o, _, lse = heads[m]
        dq, *pieces = attend_back(place, queries[m], dob, o, lse, cosine, sine, kvs[m])
        return dq, pieces[::-1]

    first = list(back_home(0, after(dx_home[0], down_half)))
    dq_one, far_one = back_heads(0, first[2])
    got_gate, got_up, dq_one = together(got_gate, got_up, dq_one)
    gate_half = add(ups[0], got_gate)
    up_half = add(ups[2], got_up)
    gate_grad = share(gate_half, 1)
    up_grad = share(up_half, 1)
    back_one = earlier(far_one[0])
    second = list(back_home(1, after(dx_home[1], gate_half, up_half)))
    back_one, second[2] = together(back_one, second[2])
    back_one = earlier(add(back_one, far_one[1]))
    dq_two, far_two = back_heads(1, second[2])
    back_one, dq_two, far_two[0] = together(back_one, dq_two, far_two[0])
    for piece in far_one[2:-1]:
        back_one = earlier(add(back_one, piece))
    back_two = earlier(far_two[0])
    back_one = add(back_one, far_one[-1])

    def back_last(m, dq, dkv, dmid):
        return last_back(
            dq, dkv, cosine, sine, qo_w, kv_w, tokens[m], scale_one[m * BLOCK : (m + 1) * BLOCK], gain_one, dmid
        )

    back_two, back_one = together(back_two, back_one)
    back_two = earlier(add(back_two, far_two[1]))
    grad_x_one, dkv_one, dgain_one = back_last(0, dq_one, back_one, first[0])
    back_two, dkv_one = together(back_two, dkv_one)
    for piece in far_two[2:-1]:
        back_two = earlier(add(back_two, piece))
    back_two = add(back_two, far_two[-1])
    grad_x_two, dkv_two, dgain_two = back_last(1, dq_two, back_two, second[0])

    gain_rows = jnp.concatenate([dgain_one + dgain_two, first[4] + second[4]], axis=0)
    gain_columns = jnp.pad(gain_rows.T, ((0, 0), (EXPERTS, LANES - EXPERTS - 2)))
    gain_columns = after(gain_columns, down_grad, gate_grad)
    keep, send = dense_grads(
        core, features // dp, [normed] * micros, [dq_one, dq_two], [dkv_one, dkv_two], [k[1] for k in mids],
        [first[3], second[3]], [h[1] for h in heads], [first[1], second[1]], gain_columns,
    )
    dense_sum = share(add(keep, swap(send)), 0)
    dense = lax.psum(dense_sum, "expert").astype(F32)
    columns = lambda start, width: dense[:, start : start + width]
    small = QD + 2 * KD

    mixed = []
    for m in range(micros):
        sums = combine(slot_rows[m], after(scaled[m], keep))
        block = lambda j: lax.dynamic_slice_in_dim(sums, (rank - 1 - j) % count * BLOCK, BLOCK, 0)
        held = block(0)
        for step in range(1, count):
            held = add(ring(held), block(step))
        mixed.append((mids[m][0] + held.astype(F32)).astype(BF))
    return (
        jnp.stack(mixed),
        jnp.stack([grad_x_one, grad_x_two]),
        dense[:, small + EXPERTS],
        columns(0, QD),
        columns(QD, KD),
        columns(QD + KD, KD),
        columns(small + LANES, features),
        dense[:, small + EXPERTS + 1],
        columns(small, EXPERTS),
        gate_grad.astype(F32),
        up_grad.astype(F32),
        down_grad.astype(F32),
    )


def solution(mesh):
    rows = P(None, ("dp", "expert"), None)
    return jax.shard_map(
        local,
        mesh=mesh,
        in_specs=(
            rows, rows, rows, P("dp"), P("dp", None), P("dp", None), P("dp", None), P("dp", None),
            P("dp"), P("dp", None),
            P("expert", None, None), P("expert", None, None), P("expert", None, None),
        ),
        out_specs=(
            rows, rows, P("dp"), P("dp", None), P("dp", None), P("dp", None), P("dp", None),
            P("dp"), P("dp", None),
            P("expert", "dp", None), P("expert", "dp", None), P("expert", "dp", None),
        ),
        check_vma=False,
    )
```

time: 1610 us -> 1020 us (0.63)
  waiting for transfers between devices: 1070 us -> 519 us
  Pallas kernels: 169 us -> 290 us
  matrix products: 97.5 us -> 0.26 us
  local copies, waits for them, and re-layouts: 116 us -> 45.9 us
  starting transfers between devices: 2.21 us -> 56.1 us
  blocking collectives: 38.5 us -> 0 us
  other arithmetic: 61 us -> 81 us
  loops' own time: 19.5 us -> 0 us
    reduce_scatter x7 -> x4, waiting for transfers between devices: 442 us -> 106 us  [local(): lax.psum_scatter(a, 'dp', scatter_dimension=dim, axis_index_groups=same_c...]
    ppermute x0 -> x25, waiting for transfers between devices: none -> 274 us  [the longest x6 109 us: local(): later = lambda a: lax.ppermute(a, 'expert', upward)]
    all_gather x8 -> x4, waiting for transfers between devices: 325 us -> 55.7 us  [local(): every = lambda a, axis: lax.all_gather(a, axis, axis=0, tiled=True)]
    reduce_scatter x4 -> x2, waiting for transfers between devices: 205 us -> 16.9 us  [local(): lax.psum_scatter(a, 'expert', scatter_dimension=0, tiled=True)]
    pallas_call x3 -> x18, Pallas kernels: 114 us -> 233 us  [the longest x2 76.6 us: expert_pass(): pl.pallas_call(expert_kernel, grid_spec=pltpu.PrefetchScalarGridSpec(num_...]
    dot_general x33 -> x1, matrix products: 97.5 us -> 0.26 us  [local(): jnp.einsum('ts,mse->mte', before, members.astype(BF), preferred_element_t...]
    ppermute x0 -> x25, starting transfers between devices: none -> 55 us  [the longest x6 40.8 us: local(): later = lambda a: lax.ppermute(a, 'expert', upward)]
    convert_element_type x15 -> x19, other arithmetic: 24.1 us -> 65.4 us  [the longest x14 53.6 us: local(): add = lambda a, b: (a.astype(F32) + b.astype(F32)).astype(BF)]
  transfers between devices with their start and end apart: 21 -> 36, of which waited for: 19 -> 23; matrix products, arithmetic and copies ran while one was open for 12% -> 10% of each run, Pallas kernels for 7% -> 24%
where the time goes in v2:
time: 1020 us; the launch traced here: 1010 us
  waiting for transfers between devices  519 us (51%)
  Pallas kernels  290 us (28%)
  other arithmetic  81 us (8%)
  starting transfers between devices  56.1 us (6%)
  local copies, waits for them, and re-layouts  45.9 us (4%)
  between operations  15 us (1%)
    ppermute x6, waiting for transfers between devices, local(): later = lambda a: lax.ppermute(a, 'expert', upward)  109 us
    reduce_scatter x4, waiting for transfers between devices, local(): lax.psum_scatter(a, 'dp', scatter_dimension=dim, axis_index_groups=same_c...  106 us
    ppermute x9, waiting for transfers between devices, local(): ring = lambda a: lax.ppermute(a, 'expert', around)  90.8 us
    pallas_call x2, Pallas kernels, expert_pass(): pl.pallas_call(expert_kernel, grid_spec=pltpu.PrefetchScalarGridSpec(num_...  76.6 us
    psum x1, waiting for transfers between devices, local(): dense = lax.psum(dense_sum, 'expert').astype(F32)  64.7 us
    ppermute x6, waiting for transfers between devices, local(): earlier = lambda a: lax.ppermute(a, 'expert', downward)  60.4 us
    all_gather x4, waiting for transfers between devices, local(): every = lambda a, axis: lax.all_gather(a, axis, axis=0, tiled=True)  55.7 us
    convert_element_type x14, other arithmetic, local(): add = lambda a, b: (a.astype(F32) + b.astype(F32)).astype(BF)  53.6 us
  transfers between devices with their start and end apart: 36, of which 23 were waited for; matrix products, arithmetic and copies ran while one was open for 10% of the time, Pallas kernels for 24%

profile of v2, /device:TPU:0, one launch (start us, length us, event | category | flops | bytes accessed | tf_op | source)
XLA Modules:
  0.0 1006.9 jit_solution(6644817548148331548)
XLA Ops:
  14.1 34.4 %all-gather.5.cloned.1.call-done.w_ref.wkv_ref = bf16[1536,1152]{1,0:T(8,128)(2,1)} async-done(((bf16[192,1152]{1,0:T(8,128)(2,1)}), bf16[1536,1152]{1,0:T(8,128)(2,1)}) %all-gather.5.cloned.1.call-update) | async-done | bytes 3538960 | tf_op jit(solution)/shard_map/all_gather | solution.py:747
  56.4 35.1 %collective-permute-done = bf16[2,256,1664]{1,2,0:T(8,128)(2,1)} collective-permute-done((bf16[2,256,1664]{1,2,0:T(8,128)(2,1)S(1)}, bf16[2,256,1664]{1,2,0:T(8,128)(2,1)}, u32[]{:S(2)}, u32[]{:S(2)}) %collective-permute-start) | collective-permute-done | bytes 1703968 | tf_op jit(solution)/shard_map/ppermute | solution.py:743
  102.3 37.0 %collective-permute-done.1.refs_1_.refs_5_ = bf16[256,1024]{1,0:T(8,128)(2,1)} collective-permute-done((bf16[256,1024]{1,0:T(8,128)(2,1)}, bf16[256,1024]{1,0:T(8,128)(2,1)}, u32[]{:S(2)}, u32[]{:S(2)}) %collective-permute-start.1) | collective-permute-done | bytes 524320 | tf_op jit(solution)/shard_map/ppermute | solution.py:744
  145.5 10.9 %collective-permute-done.2.refs_2_.refs_6_ = bf16[256,1024]{1,0:T(8,128)(2,1)} collective-permute-done((bf16[256,1024]{1,0:T(8,128)(2,1)}, bf16[256,1024]{1,0:T(8,128)(2,1)}, u32[]{:S(2)}, u32[]{:S(2)}) %collective-permute-start.2) | collective-permute-done | bytes 524320 | tf_op jit(solution)/shard_map/ppermute | solution.py:744
  163.9 38.1 %collective-permute-done.3.refs_3_.refs_7_ = bf16[256,1024]{1,0:T(8,128)(2,1)S(1)} collective-permute-done((bf16[256,1024]{1,0:T(8,128)(2,1)}, bf16[256,1024]{1,0:T(8,128)(2,1)S(1)}, u32[]{:S(2)}, u32[]{:S(2)}) %collective-permute-start.3) | collective-permute-done | bytes 524320 | tf_op jit(solution)/shard_map/ppermute | solution.py:744
  243.7 17.3 %collective-permute-start.8 = (bf16[256,1024]{1,0:T(8,128)(2,1)S(1)}, bf16[256,1024]{1,0:T(8,128)(2,1)S(1)}, u32[]{:S(2)}, u32[]{:S(2)}) collective-permute-start(bf16[256,1024]{1,0:T(8,128)(2,1)S(1)} %collective-permute-done.7.refs_2_.refs_6_), channel_id=1, source_target_pairs={{0,1},{1,2},{2,3},{4,5},{5,6},{6,7},{8,9},{9,10},{10,11},{12,13},{... | collective-permute-start | bytes 1572872 | tf_op jit(solution)/shard_map/ppermute | solution.py:744
  265.0 14.2 %collective-permute-done.8.refs_3_.refs_7_ = bf16[256,1024]{1,0:T(8,128)(2,1)S(1)} collective-permute-done((bf16[256,1024]{1,0:T(8,128)(2,1)S(1)}, bf16[256,1024]{1,0:T(8,128)(2,1)S(1)}, u32[]{:S(2)}, u32[]{:S(2)}) %collective-permute-start.8) | collective-permute-done | bytes 524320 | tf_op jit(solution)/shard_map/ppermute | solution.py:744
  325.0 38.9 %experts.2 = (bf16[10,256,1536]{2,1,0:T(8,128)(2,1)}, bf16[10,256,1664]{2,1,0:T(8,128)(2,1)}, bf16[10,256,1536]{2,1,0:T(8,128)(2,1)}, bf16[10,256,512]{2,1,0:T(8...) custom-call(s32[1]{0:T(128)} %bitcast.12.rank_ref, ...), custom_call_target="tpu_custom_call" | custom-call | flops 24159191040 | bytes 86507520 | tf_op jit(solution)/shard_map/experts/pallas_call | solution.py:655
  371.3 21.3 %all-gather.11.cloned.1.call-done.rows_ref = bf16[1024,1664]{1,0:T(8,128)(2,1)} async-done(((bf16[256,1664]{1,0:T(8,128)(2,1)}), bf16[1024,1664]{1,0:T(8,128)(2,1)}) %all-gather.11.cloned.1.call-update) | async-done | bytes 3407888 | tf_op jit(solution)/shard_map/all_gather | solution.py:747
  410.3 37.7 %experts.3 = (bf16[10,256,1536]{2,1,0:T(8,128)(2,1)}, bf16[10,256,1664]{2,1,0:T(8,128)(2,1)}, bf16[10,256,1536]{2,1,0:T(8,128)(2,1)}, bf16[10,256,512]{2,1,0:T(8...) custom-call(s32[1]{0:T(128)} %bitcast.12.rank_ref, ...), custom_call_target="tpu_custom_call" | custom-call | flops 24159191040 | bytes 86507520 | tf_op jit(solution)/shard_map/experts/pallas_call | solution.py:655
  455.4 16.9 %reduce-scatter.7.cloned.1.call-done.dx_ref = bf16[256,1664]{1,0:T(8,128)(2,1)} async-done(((bf16[1024,1664]{1,0:T(8,128)(2,1)}), bf16[256,1664]{1,0:T(8,128)(2,1)}) %reduce-scatter.7.cloned.1.call-update) | async-done | bytes 851984 | tf_op jit(solution)/shard_map/reduce_scatter | solution.py:824
  472.4 18.1 %expert_weights.2 = (bf16[10,256,1536]{2,1,0:T(8,128)(2,1)}, bf16[10,256,1536]{2,1,0:T(8,128)(2,1)}) custom-call(s32[1]{0:T(128)} %bitcast.13.core_ref, bf16[10,256,512]{2,1,0:T(8,128)(2,1)} %get-tuple-element.147.refs_0_, bf16[10,256,512]{2,1,0:T(8,128)(2,1)} %get-tuple-element.148.refs_1_, bf16[10,256,1536]{2,1,0:T(8,128)(2,1)} %get-tuple-element.149.refs_2_, ...), custom_call_target="tpu_custom_call" | custom-call | flops 8053063680 | bytes 36700160 | tf_op jit(solution)/shard_map/expert_weights/pallas_call | solution.py:695
  490.6 24.6 %expert_weights.3 = (bf16[10,768,512]{2,1,0:T(8,128)(2,1)}, bf16[10,768,512]{2,1,0:T(8,128)(2,1)}, bf16[10,768,512]{2,1,0:T(8,128)(2,1)}, bf16[10,768,512]{2,1,0:T(8,128)(2,1)}) custom-call(s32[1]{0:T(128)} %bitcast.13.core_ref, bf16[10,256,1664]{2,1,0:T(8,128)(2,1)} %dispatch.4.x_ref.refs_0_, bf16[10,256,1664]{2,1,0:T(8,128)(2,1)} %dispatch.6.x_ref.refs_1_, ...), custom_call_target="tpu_custom_call" | custom-call | flops 16106127360 | bytes 57671680 | tf_op jit(solution)/shard_map/expert_weights/pallas_call | solution.py:695
  515.2 11.0 %add_convert_fusion.2 = bf16[10,256,1536]{2,1,0:T(8,128)(2,1)} fusion(bf16[10,256,1536]{2,1,0:T(8,128)(2,1)} %collective-permute-done.9, bf16[10,256,1536]{2,1,0:T(8,128)(2,1)} %get-tuple-element.153), kind=kLoop, calls=%fused_computation.2 | loop fusion | flops 15728640 | bytes 23592960 | tf_op jit(solution)/shard_map/convert_element_type | solution.py:746
  536.3 11.5 %attend_back.2 = (bf16[256,1536]{1,0:T(8,128)(2,1)}, bf16[2,256,512]{2,1,0:T(8,128)(2,1)}, bf16[2,256,512]{2,1,0:T(8,128)(2,1)}, bf16[2,256,512]{2,1,0:T(8,128)(2,1)}, bf16[2,256,512]{2,1,0:T(8,128)(2,1)}) custom-call(s32[1]{0:T(128)} %bitcast.4.place_ref, bf16[256,1536]{1,0:T(8,128)(2,1)} %get-tuple-element.126.q_ref, ...), custom_call_target="tpu_custom_call" | custom-call | flops 16106127360 | bytes 5505024 | tf_op jit(solution)/shard_map/attend_back/pallas_call | solution.py:518
  550.9 11.0 %add_convert_fusion.1 = bf16[10,768,512]{2,1,0:T(8,128)(2,1)} fusion(bf16[10,768,512]{2,1,0:T(8,128)(2,1)} %collective-permute-done.10, bf16[10,768,512]{2,1,0:T(8,128)(2,1)} %get-tuple-element.175), kind=kLoop, calls=%fused_computation.1 | loop fusion | flops 15728640 | bytes 23592960 | tf_op jit(solution)/shard_map/convert_element_type | solution.py:746
  564.4 12.1 %add_convert_fusion = bf16[10,768,512]{2,1,0:T(8,128)(2,1)} fusion(bf16[10,768,512]{2,1,0:T(8,128)(2,1)} %collective-permute-done.11, bf16[10,768,512]{2,1,0:T(8,128)(2,1)} %get-tuple-element.177), kind=kLoop, calls=%fused_computation | loop fusion | flops 15728640 | bytes 23592960 | tf_op jit(solution)/shard_map/convert_element_type | solution.py:746
  585.5 11.5 %attend_back.3 = (bf16[256,1536]{1,0:T(8,128)(2,1)}, bf16[2,256,512]{2,1,0:T(8,128)(2,1)}, bf16[2,256,512]{2,1,0:T(8,128)(2,1)}, bf16[2,256,512]{2,1,0:T(8,128)(2,1)}, bf16[2,256,512]{2,1,0:T(8,128)(2,1)}) custom-call(s32[1]{0:T(128)} %bitcast.4.place_ref, bf16[256,1536]{1,0:T(8,128)(2,1)} %get-tuple-element.138.q_ref, ...), custom_call_target="tpu_custom_call" | custom-call | flops 16106127360 | bytes 5505024 | tf_op jit(solution)/shard_map/attend_back/pallas_call | solution.py:518
  604.0 19.2 %collective-permute-done.15 = bf16[2,256,512]{2,1,0:T(8,128)(2,1)S(1)} collective-permute-done((bf16[2,256,512]{2,1,0:T(8,128)(2,1)S(1)}, bf16[2,256,512]{2,1,0:T(8,128)(2,1)S(1)}, u32[]{:S(2)}, u32[]{:S(2)}) %collective-permute-start.15) | collective-permute-done | bytes 524320 | tf_op jit(solution)/shard_map/ppermute | solution.py:745
  624.2 9.9 collective-permute-done.14
  645.6 10.9 %collective-permute-done.16 = bf16[2,256,512]{2,1,0:T(8,128)(2,1)S(1)} collective-permute-done((bf16[2,256,512]{2,1,0:T(8,128)(2,1)S(1)}, bf16[2,256,512]{2,1,0:T(8,128)(2,1)S(1)}, u32[]{:S(2)}, u32[]{:S(2)}) %collective-permute-start.16) | collective-permute-done | bytes 524320 | tf_op jit(solution)/shard_map/ppermute | solution.py:745
  657.9 16.2 %collective-permute-done.17 = bf16[2,256,512]{2,1,0:T(8,128)(2,1)S(1)} collective-permute-done((bf16[2,256,512]{2,1,0:T(8,128)(2,1)S(1)}, bf16[2,256,512]{2,1,0:T(8,128)(2,1)S(1)}, u32[]{:S(2)}, u32[]{:S(2)}) %collective-permute-start.17) | collective-permute-done | bytes 524320 | tf_op jit(solution)/shard_map/ppermute | solution.py:745
  675.1 9.3 last_back.3
  686.6 41.7 %reduce-scatter.13.cloned.1.call-done = bf16[10,192,512]{2,1,0:T(8,128)(2,1)} async-done(((bf16[10,768,512]{2,1,0:T(8,128)(2,1)}), bf16[10,192,512]{2,1,0:T(8,128)(2,1)}) %reduce-scatter.13.cloned.1.call-update) | async-done | bytes 1966096 | tf_op jit(solution)/shard_map/reduce_scatter | solution.py:750
  728.3 13.3 %dense_grads.1 = (bf16[768,4224]{1,0:T(8,128)(2,1)}, bf16[768,4224]{1,0:T(8,128)(2,1)}) custom-call(s32[1]{0:T(128)} %bitcast.13.core_ref, bf16[512,1536]{1,0:T(8,128)(2,1)} %get-tuple-element.119.normed_ref.refs_0_.refs_1_, bf16[512,1536]{1,0:T(8,128)(2,1)} %get-tuple-element.119.normed_ref.refs_0_.refs_1_, ...), custom_call_target="tpu_custom_call" | custom-call | flops 6643777536 | bytes 24772608 | tf_op jit(solution)/shard_map/dense_grads/pallas_call | solution.py:362
  741.7 10.8 %collective-permute-done.24 = bf16[768,4224]{1,0:T(8,128)(2,1)} collective-permute-done((bf16[768,4224]{1,0:T(8,128)(2,1)}, bf16[768,4224]{1,0:T(8,128)(2,1)}, u32[]{:S(2)}, u32[]{:S(2)}) %collective-permute-start.24) | collective-permute-done | bytes 6488096 | tf_op jit(solution)/shard_map/ppermute | solution.py:748
  781.9 10.6 %collective-permute-done.21 = bf16[256,1536]{1,0:T(8,128)(2,1)S(1)} collective-permute-done((bf16[256,1536]{1,0:T(8,128)(2,1)S(1)}, bf16[256,1536]{1,0:T(8,128)(2,1)S(1)}, u32[]{:S(2)}, u32[]{:S(2)}) %collective-permute-start.21) | collective-permute-done | bytes 786464 | tf_op jit(solution)/shard_map/ppermute | solution.py:743
  793.5 15.8 %collective-permute-done.18 = bf16[256,1536]{1,0:T(8,128)(2,1)S(1)} collective-permute-done((bf16[256,1536]{1,0:T(8,128)(2,1)S(1)}, bf16[256,1536]{1,0:T(8,128)(2,1)S(1)}, u32[]{:S(2)}, u32[]{:S(2)}) %collective-permute-start.18) | collective-permute-done | bytes 786464 | tf_op jit(solution)/shard_map/ppermute | solution.py:743
  811.5 14.8 %collective-permute-done.22 = bf16[256,1536]{1,0:T(8,128)(2,1)} collective-permute-done((bf16[256,1536]{1,0:T(8,128)(2,1)}, bf16[256,1536]{1,0:T(8,128)(2,1)}, u32[]{:S(2)}, u32[]{:S(2)}) %collective-permute-start.22) | collective-permute-done | bytes 786464 | tf_op jit(solution)/shard_map/ppermute | solution.py:743
  828.5 14.7 %collective-permute-done.19 = bf16[256,1536]{1,0:T(8,128)(2,1)} collective-permute-done((bf16[256,1536]{1,0:T(8,128)(2,1)}, bf16[256,1536]{1,0:T(8,128)(2,1)}, u32[]{:S(2)}, u32[]{:S(2)}) %collective-permute-start.19) | collective-permute-done | bytes 786464 | tf_op jit(solution)/shard_map/ppermute | solution.py:743
  855.0 64.7 %reduce-scatter.17.cloned.1.call-done = bf16[10,192,512]{2,1,0:T(8,128)(2,1)} async-done(((bf16[10,768,512]{2,1,0:T(8,128)(2,1)}), bf16[10,192,512]{2,1,0:T(8,128)(2,1)}) %reduce-scatter.17.cloned.1.call-update) | async-done | bytes 1966096 | tf_op jit(solution)/shard_map/reduce_scatter | solution.py:750
  928.4 64.7 %all-reduce.3.cloned.1.call-done = bf16[192,4224]{1,0:T(8,128)(2,1)} async-done(((bf16[192,4224]{1,0:T(8,128)(2,1)}), bf16[192,4224]{1,0:T(8,128)(2,1)}) %all-reduce.3.cloned.1.call-update) | async-done | bytes 1622032 | tf_op jit(solution)/shard_map/psum | solution.py:887
  (201 shorter events, 273.8 us)
Async XLA Ops:
  7.2 41.3 %all-gather.5.cloned.1.call-start = ((), (), s32[]{:S(2)}) async-start(), calls=%async_computation.6 | async-start | bytes 3981312 | tf_op jit(solution)/shard_map/all_gather | solution.py:747
  11.7 195.5 %all-gather.7.cloned.1.call-start = ((), (), s32[]{:S(2)}) async-start(), calls=%async_computation.7 | async-start | bytes 10616832 | tf_op jit(solution)/shard_map/all_gather | solution.py:747
  48.5 269.3 %all-gather.9.cloned.1.call-start = ((), (), s32[]{:S(2)}) async-start(), calls=%async_computation.8 | async-start | bytes 4259840 | tf_op jit(solution)/shard_map/all_gather | solution.py:747
  50.1 41.3 %collective-permute-start = (bf16[2,256,1664]{1,2,0:T(8,128)(2,1)S(1)}, bf16[2,256,1664]{1,2,0:T(8,128)(2,1)}, u32[]{:S(2)}, u32[]{:S(2)}) collective-permute-start(bf16[2,256,1664]{1,2,0:T(8,128)(2,1)S(1)} %maximum_maximum_fusion), channel_id=1, source_target_pairs={{0,1},{1,2},{2,3},{3,0},{4,5},{5,6},{6,7},{7,4},{8,9},{9,10},{10,1... | collective-permute-start | bytes 5111816 | tf_op jit(solution)/shard_map/ppermute | solution.py:743
  91.4 53.1 %collective-permute-start.5 = (bf16[2,256,1664]{1,2,0:T(8,128)(2,1)}, bf16[2,256,1664]{1,2,0:T(8,128)(2,1)}, u32[]{:S(2)}, u32[]{:S(2)}) collective-permute-start(bf16[2,256,1664]{1,2,0:T(8,128)(2,1)} %collective-permute-done), channel_id=1, source_target_pairs={{0,1},{1,2},{2,3},{3,0},{4,5},{5,6},{6,7},{7,4},{8,9},{9,10},{10,1... | collective-permute-start | bytes 5111816 | tf_op jit(solution)/shard_map/ppermute | solution.py:743
  98.5 40.9 %collective-permute-start.1 = (bf16[256,1024]{1,0:T(8,128)(2,1)}, bf16[256,1024]{1,0:T(8,128)(2,1)}, u32[]{:S(2)}, u32[]{:S(2)}) collective-permute-start(bf16[256,1024]{1,0:T(8,128)(2,1)} %get-tuple-element.121.refs_0_.refs_4_), channel_id=1, source_target_pairs={{0,1},{1,2},{2,3},{4,5},{5,6},{6,7},{8,9},{9,10},{10,11},{12,13},{... | collective-permute-start | bytes 1572872 | tf_op jit(solution)/shard_map/ppermute | solution.py:744
  144.5 77.6 %collective-permute-start.6 = (bf16[2,256,1664]{1,2,0:T(8,128)(2,1)}, bf16[2,256,1664]{1,2,0:T(8,128)(2,1)}, u32[]{:S(2)}, u32[]{:S(2)}) collective-permute-start(bf16[2,256,1664]{1,2,0:T(8,128)(2,1)} %collective-permute-done.5), channel_id=1, source_target_pairs={{0,1},{1,2},{2,3},{3,0},{4,5},{5,6},{6,7},{7,4},{8,9},{9,10},{10,1... | collective-permute-start | bytes 5111816 | tf_op jit(solution)/shard_map/ppermute | solution.py:743
  156.4 45.6 %collective-permute-start.3 = (bf16[256,1024]{1,0:T(8,128)(2,1)}, bf16[256,1024]{1,0:T(8,128)(2,1)S(1)}, u32[]{:S(2)}, u32[]{:S(2)}) collective-permute-start(bf16[256,1024]{1,0:T(8,128)(2,1)} %collective-permute-done.2.refs_2_.refs_6_), channel_id=1, source_target_pairs={{0,1},{1,2},{2,3},{4,5},{5,6},{6,7},{8,9},{9,10},{10,11},{12,13},{... | collective-permute-start | bytes 1572872 | tf_op jit(solution)/shard_map/ppermute | solution.py:744
  202.8 19.3 %collective-permute-start.4 = (bf16[256,1024]{1,0:T(8,128)(2,1)}, bf16[256,1024]{1,0:T(8,128)(2,1)S(1)}, u32[]{:S(2)}, u32[]{:S(2)}) collective-permute-start(bf16[256,1024]{1,0:T(8,128)(2,1)} %get-tuple-element.122.refs_0_.refs_4_), channel_id=1, source_target_pairs={{0,1},{1,2},{2,3},{4,5},{5,6},{6,7},{8,9},{9,10},{10,11},{12,13},{... | collective-permute-start | bytes 1572872 | tf_op jit(solution)/shard_map/ppermute | solution.py:744
  229.3 163.3 %all-gather.11.cloned.1.call-start = ((), (), s32[]{:S(2)}) async-start(), calls=%async_computation.9 | async-start | bytes 4259840 | tf_op jit(solution)/shard_map/all_gather | solution.py:747
  243.7 35.5 %collective-permute-start.8 = (bf16[256,1024]{1,0:T(8,128)(2,1)S(1)}, bf16[256,1024]{1,0:T(8,128)(2,1)S(1)}, u32[]{:S(2)}, u32[]{:S(2)}) collective-permute-start(bf16[256,1024]{1,0:T(8,128)(2,1)S(1)} %collective-permute-done.7.refs_2_.refs_6_), channel_id=1, source_target_pairs={{0,1},{1,2},{2,3},{4,5},{5,6},{6,7},{8,9},{9,10},{10,11},{12,13},{... | collective-permute-start | bytes 1572872 | tf_op jit(solution)/shard_map/ppermute | solution.py:744
  294.3 178.1 %reduce-scatter.7.cloned.1.call-start = ((), (), s32[]{:S(2)}) async-start(), calls=%async_computation.10 | async-start | bytes 4259840 | tf_op jit(solution)/shard_map/reduce_scatter | solution.py:824
  399.7 176.8 %reduce-scatter.9.cloned.1.call-start = ((), (), s32[]{:S(2)}) async-start(), calls=%async_computation.11 | async-start | bytes 4259840 | tf_op jit(solution)/shard_map/reduce_scatter | solution.py:824
  490.5 24.7 %collective-permute-start.9 = (bf16[10,256,1536]{2,1,0:T(8,128)(2,1)}, bf16[10,256,1536]{2,1,0:T(8,128)(2,1)}, u32[]{:S(2)}, u32[]{:S(2)}) collective-permute-start(bf16[10,256,1536]{2,1,0:T(8,128)(2,1)} %get-tuple-element.151), channel_id=1, source_target_pairs={{0,4},{4,0},{8,12},{12,8},{16,20},{20,16},{24,28},{28,24},{1,5},{5... | collective-permute-start | bytes 23592968 | tf_op jit(solution)/shard_map/ppermute | solution.py:748
  490.6 196.1 %reduce-scatter.11.cloned.1.call-start = ((), (), s32[]{:S(2)}) async-start(), calls=%async_computation.12 | async-start | bytes 9830400 | tf_op jit(solution)/shard_map/reduce_scatter | solution.py:750
  526.2 202.2 %reduce-scatter.13.cloned.1.call-start = ((), (), s32[]{:S(2)}) async-start(), calls=%async_computation.13 | async-start | bytes 9830400 | tf_op jit(solution)/shard_map/reduce_scatter | solution.py:750
  526.4 21.3 %collective-permute-start.10 = (bf16[10,768,512]{2,1,0:T(8,128)(2,1)}, bf16[10,768,512]{2,1,0:T(8,128)(2,1)}, u32[]{:S(2)}, u32[]{:S(2)}) collective-permute-start(bf16[10,768,512]{2,1,0:T(8,128)(2,1)} %get-tuple-element.162), channel_id=1, source_target_pairs={{0,4},{4,0},{8,12},{12,8},{16,20},{20,16},{24,28},{28,24},{1,5},{5... | collective-permute-start | bytes 23592968 | tf_op jit(solution)/shard_map/ppermute | solution.py:748
  527.3 23.6 %collective-permute-start.11 = (bf16[10,768,512]{2,1,0:T(8,128)(2,1)}, bf16[10,768,512]{2,1,0:T(8,128)(2,1)}, u32[]{:S(2)}, u32[]{:S(2)}) collective-permute-start(bf16[10,768,512]{2,1,0:T(8,128)(2,1)} %get-tuple-element.163), channel_id=1, source_target_pairs={{0,4},{4,0},{8,12},{12,8},{16,20},{20,16},{24,28},{28,24},{1,5},{5... | collective-permute-start | bytes 23592968 | tf_op jit(solution)/shard_map/ppermute | solution.py:748
  561.9 284.2 %reduce-scatter.15.cloned.1.call-start = ((), (), s32[]{:S(2)}) async-start(), calls=%async_computation.14 | async-start | bytes 8110080 | tf_op jit(solution)/shard_map/reduce_scatter | solution.py:750
  562.9 21.1 %collective-permute-start.12 = (bf16[2,256,512]{2,1,0:T(8,128)(2,1)S(1)}, bf16[2,256,512]{2,1,0:T(8,128)(2,1)S(1)}, u32[]{:S(2)}, u32[]{:S(2)}) collective-permute-start(bf16[2,256,512]{2,1,0:T(8,128)(2,1)S(1)} %copy-done.25), channel_id=1, source_target_pairs={{1,0},{2,1},{3,2},{5,4},{6,5},{7,6},{9,8},{10,9},{11,10},{13,12},{... | collective-permute-start | bytes 1572872 | tf_op jit(solution)/shard_map/ppermute | solution.py:745
  601.5 21.8 %collective-permute-start.15 = (bf16[2,256,512]{2,1,0:T(8,128)(2,1)S(1)}, bf16[2,256,512]{2,1,0:T(8,128)(2,1)S(1)}, u32[]{:S(2)}, u32[]{:S(2)}) collective-permute-start(bf16[2,256,512]{2,1,0:T(8,128)(2,1)S(1)} %add_convert_fusion.16), channel_id=1, source_target_pairs={{1,0},{2,1},{3,2},{5,4},{6,5},{7,6},{9,8},{10,9},{11,10},{13,12},{... | collective-permute-start | bytes 1572872 | tf_op jit(solution)/shard_map/ppermute | solution.py:745
  602.8 31.3 %collective-permute-start.14 = (bf16[2,256,512]{2,1,0:T(8,128)(2,1)}, bf16[2,256,512]{2,1,0:T(8,128)(2,1)S(1)}, u32[]{:S(2)}, u32[]{:S(2)}) collective-permute-start(bf16[2,256,512]{2,1,0:T(8,128)(2,1)} %get-tuple-element.192), channel_id=1, source_target_pairs={{1,0},{2,1},{3,2},{5,4},{6,5},{7,6},{9,8},{10,9},{11,10},{13,12},{... | collective-permute-start | bytes 1572872 | tf_op jit(solution)/shard_map/ppermute | solution.py:745
  634.2 22.2 %collective-permute-start.16 = (bf16[2,256,512]{2,1,0:T(8,128)(2,1)S(1)}, bf16[2,256,512]{2,1,0:T(8,128)(2,1)S(1)}, u32[]{:S(2)}, u32[]{:S(2)}) collective-permute-start(bf16[2,256,512]{2,1,0:T(8,128)(2,1)S(1)} %add_convert_fusion.14), channel_id=1, source_target_pairs={{1,0},{2,1},{3,2},{5,4},{6,5},{7,6},{9,8},{10,9},{11,10},{13,12},{... | collective-permute-start | bytes 1572872 | tf_op jit(solution)/shard_map/ppermute | solution.py:745
  656.6 17.6 %collective-permute-start.17 = (bf16[2,256,512]{2,1,0:T(8,128)(2,1)S(1)}, bf16[2,256,512]{2,1,0:T(8,128)(2,1)S(1)}, u32[]{:S(2)}, u32[]{:S(2)}) collective-permute-start(bf16[2,256,512]{2,1,0:T(8,128)(2,1)S(1)} %add_convert_fusion.13), channel_id=1, source_target_pairs={{1,0},{2,1},{3,2},{5,4},{6,5},{7,6},{9,8},{10,9},{11,10},{13,12},{... | collective-permute-start | bytes 1572872 | tf_op jit(solution)/shard_map/ppermute | solution.py:745
  761.5 158.2 %reduce-scatter.17.cloned.1.call-start = ((), (), s32[]{:S(2)}) async-start(), calls=%async_computation.16 | async-start | bytes 9830400 | tf_op jit(solution)/shard_map/reduce_scatter | solution.py:750
  762.0 231.1 %all-reduce.3.cloned.1.call-start = ((), (), s32[]{:S(2)}) async-start(), calls=%async_computation.15 | async-start | bytes 3244032 | tf_op jit(solution)/shard_map/psum | solution.py:887
  770.2 22.2 %collective-permute-start.21 = (bf16[256,1536]{1,0:T(8,128)(2,1)S(1)}, bf16[256,1536]{1,0:T(8,128)(2,1)S(1)}, u32[]{:S(2)}, u32[]{:S(2)}) collective-permute-start(bf16[256,1536]{1,0:T(8,128)(2,1)S(1)} %constant_dynamic-slice_fusion), channel_id=1, source_target_pairs={{0,1},{1,2},{2,3},{3,0},{4,5},{5,6},{6,7},{7,4},{8,9},{9,10},{10,1... | collective-permute-start | bytes 2359304 | tf_op jit(solution)/shard_map/ppermute | solution.py:743
  780.3 29.0 %collective-permute-start.18 = (bf16[256,1536]{1,0:T(8,128)(2,1)S(1)}, bf16[256,1536]{1,0:T(8,128)(2,1)S(1)}, u32[]{:S(2)}, u32[]{:S(2)}) collective-permute-start(bf16[256,1536]{1,0:T(8,128)(2,1)S(1)} %constant_dynamic-slice_fusion.1), channel_id=1, source_target_pairs={{0,1},{1,2},{2,3},{3,0},{4,5},{5,6},{6,7},{7,4},{8,9},{9,10},{10,1... | collective-permute-start | bytes 2359304 | tf_op jit(solution)/shard_map/ppermute | solution.py:743
  793.5 32.7 %collective-permute-start.22 = (bf16[256,1536]{1,0:T(8,128)(2,1)}, bf16[256,1536]{1,0:T(8,128)(2,1)}, u32[]{:S(2)}, u32[]{:S(2)}) collective-permute-start(bf16[256,1536]{1,0:T(8,128)(2,1)} %add_convert_fusion.7), channel_id=1, source_target_pairs={{0,1},{1,2},{2,3},{3,0},{4,5},{5,6},{6,7},{7,4},{8,9},{9,10},{10,1... | collective-permute-start | bytes 2359304 | tf_op jit(solution)/shard_map/ppermute | solution.py:743
  811.5 31.6 %collective-permute-start.19 = (bf16[256,1536]{1,0:T(8,128)(2,1)}, bf16[256,1536]{1,0:T(8,128)(2,1)}, u32[]{:S(2)}, u32[]{:S(2)}) collective-permute-start(bf16[256,1536]{1,0:T(8,128)(2,1)} %add_convert_fusion.11), channel_id=1, source_target_pairs={{0,1},{1,2},{2,3},{3,0},{4,5},{5,6},{6,7},{7,4},{8,9},{9,10},{10,1... | collective-permute-start | bytes 2359304 | tf_op jit(solution)/shard_map/ppermute | solution.py:743
  828.5 95.4 %collective-permute-start.23 = (bf16[256,1536]{1,0:T(8,128)(2,1)}, bf16[256,1536]{1,0:T(8,128)(2,1)}, u32[]{:S(2)}, u32[]{:S(2)}) collective-permute-start(bf16[256,1536]{1,0:T(8,128)(2,1)} %add_convert_fusion.6), channel_id=1, source_target_pairs={{0,1},{1,2},{2,3},{3,0},{4,5},{5,6},{6,7},{7,4},{8,9},{9,10},{10,1... | collective-permute-start | bytes 2359304 | tf_op jit(solution)/shard_map/ppermute | solution.py:743
  845.8 79.6 %collective-permute-start.20 = (bf16[256,1536]{1,0:T(8,128)(2,1)}, bf16[256,1536]{1,0:T(8,128)(2,1)}, u32[]{:S(2)}, u32[]{:S(2)}) collective-permute-start(bf16[256,1536]{1,0:T(8,128)(2,1)} %add_convert_fusion.10), channel_id=1, source_target_pairs={{0,1},{1,2},{2,3},{3,0},{4,5},{5,6},{6,7},{7,4},{8,9},{9,10},{10,1... | collective-permute-start | bytes 2359304 | tf_op jit(solution)/shard_map/ppermute | solution.py:743
  (30 other events, 751.5 us)
Sparse Core Ops, SparseCore 0:
  11.8 36.6 all-gather.4
  50.9 58.8 all-gather.6
  229.4 81.5 all-gather.8
  313.0 79.5 all-gather.10
  399.8 72.4 reduce-scatter.6
  490.7 64.6 reduce-scatter.8
  558.4 83.5 reduce-scatter.10
  644.9 83.3 reduce-scatter.12
  761.6 71.8 reduce-scatter.14
  836.3 83.3 reduce-scatter.16
  922.1 71.0 all-reduce.2

commit v3 on v2

--- a/solution.py
+++ b/solution.py
@@ -25,6 +25,7 @@
 LANES = 128
 COLUMNS = 256
 VMEM_LIMIT = 56 * 2**20
+COST_SCALE = 0.1
 
 BF = jnp.bfloat16
 F32 = jnp.float32
@@ -54,6 +55,13 @@
     )
 
 
+def cost(flops, bytes_accessed, transcendentals):
+    scale = lambda n: int(n * COST_SCALE)
+    return pl.CostEstimate(
+        flops=scale(flops), bytes_accessed=scale(bytes_accessed), transcendentals=scale(transcendentals)
+    )
+
+
 def params(limit=VMEM_LIMIT):
     return pltpu.CompilerParams(vmem_limit_bytes=limit)
 
@@ -97,7 +105,7 @@
             jax.ShapeDtypeStruct((total, 1), F32),
         ],
         compiler_params=params(),
-        cost_estimate=pl.CostEstimate(flops=5 * total * features, bytes_accessed=4 * total * features, transcendentals=0),
+        cost_estimate=cost(flops=5 * total * features, bytes_accessed=4 * total * features, transcendentals=0),
         name="norm",
     )(x, gain)
 
@@ -118,7 +126,7 @@
     pl.when(pl.program_id(0) >= turned)(lambda: write(False))
 
 
-def project(normed, weight, columns, turned_columns, cosine, sine):
+def project(normed, weight, start, columns, turned_columns, cosine, sine):
     total, features = normed.shape
     tile = 2 * COLUMNS
     micros = total // BLOCK
@@ -127,14 +135,14 @@
         grid=(columns // tile,),
         in_specs=[
             pl.BlockSpec((total, features), lambda j: (0, 0)),
-            pl.BlockSpec((features, tile), lambda j: (0, j)),
+            pl.BlockSpec((features, tile), lambda j: (0, start // tile + j)),
             pl.BlockSpec((BLOCK, LANES), lambda j: (0, 0)),
             pl.BlockSpec((BLOCK, LANES), lambda j: (0, 0)),
         ],
         out_specs=[pl.BlockSpec((BLOCK, tile), lambda j: (0, j))] * micros,
         out_shape=[jax.ShapeDtypeStruct((BLOCK, columns), BF)] * micros,
         compiler_params=params(),
-        cost_estimate=pl.CostEstimate(
+        cost_estimate=cost(
             flops=2 * total * features * columns,
             bytes_accessed=2 * (features * columns + total * (features + columns)),
             transcendentals=0,
@@ -192,7 +200,7 @@
             jax.ShapeDtypeStruct((BLOCK, LANES), F32),
         ],
         compiler_params=params(),
-        cost_estimate=pl.CostEstimate(
+        cost_estimate=cost(
             flops=2 * BLOCK * features * QD, bytes_accessed=2 * features * QD + 14 * BLOCK * features, transcendentals=0
         ),
         name="outward",
@@ -252,7 +260,7 @@
             jax.ShapeDtypeStruct((1, features), F32),
         ],
         compiler_params=params(),
-        cost_estimate=pl.CostEstimate(
+        cost_estimate=cost(
             flops=2 * BLOCK * features * QD, bytes_accessed=2 * features * QD + 18 * BLOCK * features, transcendentals=0
         ),
         name="home_back",
@@ -298,7 +306,7 @@
         in_specs=[
             whole(dq), whole(dkv), whole(cosine), whole(sine),
             pl.BlockSpec((tile, QD), lambda j: (j, 0)),
-            pl.BlockSpec((tile, 2 * KD), lambda j: (j, 0)),
+            pl.BlockSpec((tile, 2 * KD), lambda j: (j, QD // KD)),
             whole(x), whole(scale), whole(gain), whole(dmid),
         ],
         out_specs=[fixed(BLOCK, features), fixed(BLOCK, 2 * KD), fixed(1, features)],
@@ -308,7 +316,7 @@
             jax.ShapeDtypeStruct((1, features), F32),
         ],
         compiler_params=params(),
-        cost_estimate=pl.CostEstimate(
+        cost_estimate=cost(
             flops=2 * BLOCK * features * (QD + 2 * KD),
             bytes_accessed=2 * features * (QD + 2 * KD) + 16 * BLOCK * features,
             transcendentals=0,
@@ -370,7 +378,7 @@
         ),
         out_shape=[half, half],
         compiler_params=params(),
-        cost_estimate=pl.CostEstimate(
+        cost_estimate=cost(
             flops=2 * micros * BLOCK * QD * width,
             bytes_accessed=2 * QD * width + 4 * micros * BLOCK * (QD + width),
             transcendentals=0,
@@ -474,7 +482,7 @@
             jax.ShapeDtypeStruct((pairs, 1, rows), F32),
         ],
         compiler_params=params(),
-        cost_estimate=pl.CostEstimate(
+        cost_estimate=cost(
             flops=8 * SEQ * BLOCK * HEADS * PAIR, bytes_accessed=10 * BLOCK * QD, transcendentals=SEQ * BLOCK * HEADS
         ),
         name="attend",
@@ -535,7 +543,7 @@
             *[jax.ShapeDtypeStruct((2, BLOCK, KD), BF) for _ in kvs],
         ],
         compiler_params=params(),
-        cost_estimate=pl.CostEstimate(
+        cost_estimate=cost(
             flops=20 * SEQ * BLOCK * HEADS * PAIR, bytes_accessed=14 * BLOCK * QD, transcendentals=SEQ * BLOCK * HEADS
         ),
         name="attend_back",
@@ -571,7 +579,7 @@
         out_specs=pl.BlockSpec((experts, CAP, features), lambda b: (0, b, 0)),
         out_shape=jax.ShapeDtypeStruct((experts, blocks * CAP, features), BF),
         compiler_params=params(),
-        cost_estimate=pl.CostEstimate(
+        cost_estimate=cost(
             flops=2 * experts * CAP * total * features,
             bytes_accessed=2 * features * (total + experts * blocks * CAP),
             transcendentals=0,
@@ -603,7 +611,7 @@
         out_specs=pl.BlockSpec((BLOCK, features), lambda b: (b, 0)),
         out_shape=jax.ShapeDtypeStruct((total, features), BF),
         compiler_params=params(),
-        cost_estimate=pl.CostEstimate(
+        cost_estimate=cost(
             flops=2 * experts * CAP * total * features,
             bytes_accessed=2 * features * (total + experts * blocks * CAP),
             transcendentals=0,
@@ -669,7 +677,7 @@
             shape(features), shape(features + LANES), shape(features), shape(hidden), shape(hidden), shape(hidden)
         ],
         compiler_params=params(),
-        cost_estimate=pl.CostEstimate(
+        cost_estimate=cost(
             flops=12 * experts * rows * features * hidden,
             bytes_accessed=6 * experts * features * hidden + 10 * experts * rows * features,
             transcendentals=experts * rows * hidden,
@@ -706,13 +714,98 @@
         ),
         out_shape=[half] * (2 * products),
         compiler_params=params(),
-        cost_estimate=pl.CostEstimate(
+        cost_estimate=cost(
             flops=2 * count * products * experts * rows * depth * width,
             bytes_accessed=2 * experts * (products * depth * width + count * rows * (depth + products * width)),
             transcendentals=0,
         ),
         name="expert_weights",
     )(core, *lefts, *[a for right in rights for a in right])
+
+
+def fold_kernel(cut, step, place_ref, keep_ref, got_ref, *outs):
+    x_place, y_place = place_ref[0], place_ref[1]
+
+    def put(out_ref, slot, block):
+        rows = pl.ds(pl.multiple_of(block * step, step), step)
+        total = keep_ref[0, rows, :].astype(F32) + got_ref[0, rows, :].astype(F32)
+        out_ref[0, slot * step : (slot + 1) * step, :] = total.astype(BF)
+
+    first = pl.program_id(0) < cut
+
+    @pl.when(first)
+    def _():
+        for y in range(2):
+            put(outs[0], y, 2 * y + x_place)
+            put(outs[1], y, 2 * y + 1 - x_place)
+
+    @pl.when(jnp.logical_not(first))
+    def _():
+        for x in range(2):
+            put(outs[2], x, 2 * y_place + x)
+            put(outs[3], x, 2 * (1 - y_place) + x)
+
+
+def fold(places, keep, got, tile=None):
+    some, rows, width = keep.shape
+    step = rows // 4
+    count = some if tile is None else width // tile
+    cut = (count + 1) // 2
+    size = width if tile is None else tile
+    place = (lambda i: (i, 0, 0)) if tile is None else (lambda i: (0, 0, i))
+    block = lambda high, index: pl.BlockSpec((1, high, size), index)
+    whole = block(rows, lambda i, s: place(i))
+    one = block(2 * step, lambda i, s: place(jnp.minimum(i, cut - 1)))
+    two = block(2 * step, lambda i, s: place(jnp.maximum(i - cut, 0)))
+    shape = lambda n: jax.ShapeDtypeStruct(
+        (n, 2 * step, width) if tile is None else (some, 2 * step, n * tile), BF
+    )
+    return pl.pallas_call(
+        partial(fold_kernel, cut, step),
+        grid_spec=pltpu.PrefetchScalarGridSpec(
+            num_scalar_prefetch=1,
+            grid=(count,),
+            in_specs=[whole, whole],
+            out_specs=[one, one, two, two],
+        ),
+        out_shape=[shape(cut), shape(cut), shape(count - cut), shape(count - cut)],
+        compiler_params=params(),
+        cost_estimate=cost(
+            flops=some * rows * width, bytes_accessed=6 * some * rows * width, transcendentals=0
+        ),
+        name="fold",
+    )(places, keep, got)
+
+
+def fold_again_kernel(step, place_ref, keep_ref, got_ref, stay_ref, go_ref):
+    for out_ref, half in ((stay_ref, place_ref[0]), (go_ref, 1 - place_ref[0])):
+        rows = pl.ds(pl.multiple_of(half * step, step), step)
+        total = keep_ref[0, rows, :].astype(F32) + got_ref[0, rows, :].astype(F32)
+        out_ref[0] = total.astype(BF)
+
+
+def fold_again(place, keep, got):
+    some, rows, width = keep.shape
+    step = rows // 2
+    tile = width
+    while tile * rows > 2**19 and tile % 2 == 0 and tile // 2 % LANES == 0:
+        tile //= 2
+    index = lambda i, j, s: (i, 0, j)
+    return pl.pallas_call(
+        partial(fold_again_kernel, step),
+        grid_spec=pltpu.PrefetchScalarGridSpec(
+            num_scalar_prefetch=1,
+            grid=(some, width // tile),
+            in_specs=[pl.BlockSpec((1, rows, tile), index)] * 2,
+            out_specs=[pl.BlockSpec((1, step, tile), index)] * 2,
+        ),
+        out_shape=[jax.ShapeDtypeStruct((some, step, width), BF)] * 2,
+        compiler_params=params(),
+        cost_estimate=cost(
+            flops=some * rows * width, bytes_accessed=6 * some * rows * width, transcendentals=0
+        ),
+        name="fold_again",
+    )(place, keep, got)
 
 
 def after(value, *marks):
@@ -747,59 +840,90 @@
     every = lambda a, axis: lax.all_gather(a, axis, axis=0, tiled=True)
     swap = lambda a: lax.ppermute(a, "dp", [(i, i ^ 1) for i in range(dp)])
     same_core = [list(range(c, dp, 2)) for c in range(2)]
-    share = lambda a, dim: lax.psum_scatter(
-        a, "dp", scatter_dimension=dim, axis_index_groups=same_core, tiled=True
+    across = lambda a, bit: lax.ppermute(a, "dp", [(i, i ^ bit) for i in range(dp)])
+    x_place, y_place = lax.axis_index("dp") // 2 % 2, lax.axis_index("dp") // 4
+    square = dp == 8
+
+    places = jnp.stack([x_place, y_place]).astype(jnp.int32)
+
+    share = lambda a: lax.psum_scatter(a, "dp", scatter_dimension=1, axis_index_groups=same_core, tiled=True)
+
+    def fold_first(keep, got, tile=None):
+        return list(fold(places, keep, got, tile)) if square else [add(keep, got)]
+
+    def send_first(parts):
+        if not square:
+            return parts
+        one, one_sent, two, two_sent = parts
+        return [one, across(one_sent, 2), two, across(two_sent, 4)]
+
+    def halve_first(keep, got, tile=None):
+        return send_first(fold_first(keep, got, tile))
+
+    def halve_second(parts):
+        if not square:
+            return parts
+        one, one_sent = fold_again(places[1:], *parts[:2])
+        two, two_sent = fold_again(places[:1], *parts[2:])
+        return [one, across(one_sent, 4), two, across(two_sent, 2)]
+
+    def halve_last(parts, axis, dtype):
+        if not square:
+            return share(parts[0]).astype(dtype)
+        total = lambda a, b: (a.astype(F32) + b.astype(F32)).astype(dtype)
+        return jnp.concatenate([total(*parts[:2]), total(*parts[2:])], axis=axis)
+
+    beside = jnp.zeros((w_router.shape[0], LANES - EXPERTS - 2), BF)
+    weights = every(
+        jnp.concatenate(
+            [w_query, w_out, w_key, w_value, w_router, attn_gain[:, None], moe_gain[:, None], beside], axis=1
+        ),
+        "dp",
     )
-
-    beside = jnp.zeros((w_router.shape[0], LANES - EXPERTS - 2), BF)
-    kv_w = every(
-        jnp.concatenate([w_key, w_value, w_router, attn_gain[:, None], moe_gain[:, None], beside], axis=1), "dp"
-    )
-    qo_w = every(after(jnp.concatenate([w_query, w_out], axis=1), kv_w), "dp")
-    router_w = kv_w[:, 2 * KD :]
-    gains = router_w[:, EXPERTS : EXPERTS + 2].T.astype(F32)
-    gain_one, gain_two = gains[0:1], gains[1:2]
+    behind = QD + features + 2 * KD
 
     members = jnp.any(routes[:, :, :, None] == jnp.arange(EXPERTS, dtype=jnp.int32), axis=2)
     before = jnp.tril(jnp.ones((BLOCK, BLOCK), F32), -1).astype(BF)
     slots = jnp.einsum("ts,mse->mte", before, members.astype(BF), preferred_element_type=F32)
     slots = jnp.where(members, slots, -1.0).astype(BF)
-    dy_ring = [
-        jnp.concatenate([out_grad, slots, jnp.zeros((micros, BLOCK, LANES - EXPERTS), BF)], axis=2)
-    ]
-
-    dy_ring.append(ring(dy_ring[0]))
+    dy_sent = jnp.concatenate([out_grad, slots, jnp.zeros((micros, BLOCK, LANES - EXPERTS), BF)], axis=2)
+
+    dy_ring = [dy_sent]
+    for _ in range(count - 2):
+        dy_ring.append(ring(dy_ring[-1]))
+    router_w = weights[:, behind:]
+    gains = router_w[:, EXPERTS : EXPERTS + 2].T.astype(F32)
+    gain_one, gain_two = gains[0:1], gains[1:2]
     x_whole = tokens.reshape(micros * BLOCK, features)
     normed, scale_one = norm_rows(x_whole, gain_one)
-    normed_one, dy_ring[1] = together(normed, dy_ring[1])
-    kv_own = project(normed_one, kv_w, 2 * KD, KD, cosine, sine)
-    dy_ring.append(ring(dy_ring[1]))
-    kvs = [[kv_own[0]]]
+    normed = after(normed, dy_ring[-1])
+    kv_own = project(normed, weights, QD + features, 2 * KD, KD, cosine, sine)
+    kv_one = [kv_own[0]]
     for _ in range(seq_blocks - 1):
-        kvs[0].append(later(kvs[0][-1]))
-    normed_two, dy_ring[2] = together(normed, dy_ring[2])
-    queries = project(normed_two, qo_w, QD, QD, cosine, sine)
+        kv_one.append(later(kv_one[-1]))
     while len(dy_ring) < count:
         dy_ring.append(ring(dy_ring[-1]))
-
-    heads, mids, sent = [], [], []
-    held = [after(kv_own[1], kvs[0][-1])]
-    held.append(later(held[-1]))
-    for m in range(micros):
-        o, ob, lse = attend(place, queries[m], kvs[m])
-        if m == 0:
-            held[-1], o, ob, lse = together(held[-1], o, ob, lse)
-            held.append(later(held[-1]))
-            ob, dy_ring[-1] = together(ob, dy_ring[-1])
-        heads.append((o, ob, lse))
-        mid, out, scale_two, gates = outward(ob, qo_w, tokens[m], gain_two, router_w, routes[m])
-        mids.append((mid, out, scale_two, gates))
-        sent.append(every(out, "expert"))
-        if m == 0:
-            held[-1], out = together(held[-1], out)
-            while len(held) < seq_blocks:
-                held.append(later(held[-1]))
-            kvs.append(held)
+    kv_one[-1], dy_ring[-1] = together(kv_one[-1], dy_ring[-1])
+
+    kv_two = [after(kv_own[1], kv_one[-1])]
+    kv_two.append(later(kv_two[-1]))
+    queries = list(project(after(normed, kv_one[-1]), weights, 0, QD, QD, cosine, sine))
+    kv_two[-1], queries[0] = together(kv_two[-1], queries[0])
+    kv_two.append(later(kv_two[-1]))
+    o_one, ob_one, lse_one = attend(place, queries[0], kv_one)
+    kv_two[-1], ob_one = together(kv_two[-1], ob_one)
+    kv_two.append(later(kv_two[-1]))
+    go_out = lambda m, ob: outward(ob, weights, tokens[m], gain_two, router_w, routes[m])
+    mids = [list(go_out(0, ob_one))]
+    sent = [every(mids[0][1], "expert")]
+    kv_two[-1], mids[0][1] = together(kv_two[-1], mids[0][1])
+    while len(kv_two) < seq_blocks:
+        kv_two.append(later(kv_two[-1]))
+    o_two, ob_two, lse_two = attend(place, queries[1], kv_two)
+    mids.append(list(go_out(1, ob_two)))
+    sent.append(every(mids[1][1], "expert"))
+    kvs = (kv_one, kv_two)
+    heads = ((o_one, ob_one, lse_one), (o_two, ob_two, lse_two))
 
     def in_order(m):
         whole = jnp.zeros((count * BLOCK, features + LANES), BF)
@@ -813,31 +937,40 @@
         table = lax.dynamic_slice_in_dim(dy_all, features + rank * exp_dev, exp_dev, 1)
         slot_rows.append(table.astype(F32).T)
         dy_slots = dispatch(slot_rows[m], dy_all, features)
+        if m > 0:
+            mixture_sums = combine(slot_rows[0], after(scaled[0], dx_sums[0]))
+            sent[m], dy_slots, dx_sums[-1], mixture_sums = together(sent[m], dy_slots, dx_sums[-1], mixture_sums)
         x_slots = dispatch(slot_rows[m], sent[m], features + LANES)
-        if m > 0:
-            x_slots, dx_sums[-1] = together(x_slots, dx_sums[-1])
         ys, dx, *rest = expert_pass(rank.astype(jnp.int32)[None], x_slots, dy_slots, w_gate, w_up, w_down)
         parts.append((x_slots, *rest))
         scaled.append(ys)
         dx_sums.append(combine(slot_rows[m], dx))
-    for a in dx_sums:
-        dx_home.append(lax.psum_scatter(a, "expert", scatter_dimension=0, tiled=True))
+    ring_block = lambda sums, j: lax.dynamic_slice_in_dim(sums, (rank - 1 - j) % count * BLOCK, BLOCK, 0)
+    dx_home = [lax.psum_scatter(dx_sums[0], "expert", scatter_dimension=0, tiled=True)]
 
     xs, gdys, acts, dgs, dus = zip(*parts)
     hidden = w_down.shape[1]
-    first_act, dx_home[0], _ = together(acts[0], dx_home[0], dx_sums[-1])
+    first_act, dx_home[0], dx_sums[1] = together(acts[0], dx_home[0], dx_sums[1])
+    dx_held = ring(ring_block(dx_sums[1], 0))
     keep_down, send_down = weight_pass(core, hidden // dp, hidden, (first_act, *acts[1:]), gdys)
+    dx_held, keep_down, send_down = together(dx_held, keep_down, send_down)
     got_down = swap(send_down)
+    dx_held = ring(add(dx_held, ring_block(dx_sums[1], 1)))
     dgs = after(dgs[0], keep_down), *dgs[1:]
     ups = weight_pass(core, features // dp, features, xs, dgs, dus)
-    got_down, *ups = together(got_down, *ups)
+    held = ring(ring_block(after(mixture_sums, keep_down), 0))
+    dx_held, got_down, *ups = together(dx_held, got_down, *ups)
+    for step in range(2, count - 1):
+        dx_held = ring(add(dx_held, ring_block(dx_sums[1], step)))
     down_half = add(keep_down, got_down)
-    down_grad = share(down_half, 1)
+    held, down_half = together(held, down_half)
+    held = ring(add(held, ring_block(mixture_sums, 1)))
+    down_grad = share(down_half)
     got_gate, got_up = swap(ups[1]), swap(ups[3])
 
     def back_home(m, dx):
         mid, _, scale_two, gates = mids[m]
-        return home_back(dx, gates, mid, scale_two, out_grad[m], router_w, gain_two, qo_w)
+        return home_back(dx, gates, mid, scale_two, out_grad[m], router_w, gain_two, weights)
 
     def back_heads(m, dob):
         o, _, lse = heads[m]
@@ -846,28 +979,32 @@
 
     first = list(back_home(0, after(dx_home[0], down_half)))
     dq_one, far_one = back_heads(0, first[2])
-    got_gate, got_up, dq_one = together(got_gate, got_up, dq_one)
-    gate_half = add(ups[0], got_gate)
+    dx_held, held, got_gate, got_up, dq_one = together(dx_held, held, got_gate, got_up, dq_one)
+    dx_home.append(add(dx_held, ring_block(dx_sums[1], count - 1)))
+    for step in range(2, count - 1):
+        held = ring(add(held, ring_block(mixture_sums, step)))
     up_half = add(ups[2], got_up)
-    gate_grad = share(gate_half, 1)
-    up_grad = share(up_half, 1)
+    up_grad = share(up_half)
     back_one = earlier(far_one[0])
-    second = list(back_home(1, after(dx_home[1], gate_half, up_half)))
+    second = list(back_home(1, after(dx_home[1], up_half, dq_one)))
     back_one, second[2] = together(back_one, second[2])
     back_one = earlier(add(back_one, far_one[1]))
     dq_two, far_two = back_heads(1, second[2])
-    back_one, dq_two, far_two[0] = together(back_one, dq_two, far_two[0])
+    back_one, dq_two, far_two[0], held, down_grad = together(back_one, dq_two, far_two[0], held, down_grad)
     for piece in far_one[2:-1]:
         back_one = earlier(add(back_one, piece))
     back_two = earlier(far_two[0])
+    mixtures = [add(held, ring_block(mixture_sums, count - 1))]
+    gate_half = add(after(ups[0], dq_two), got_gate)
+    gate_grad = share(gate_half)
     back_one = add(back_one, far_one[-1])
 
     def back_last(m, dq, dkv, dmid):
         return last_back(
-            dq, dkv, cosine, sine, qo_w, kv_w, tokens[m], scale_one[m * BLOCK : (m + 1) * BLOCK], gain_one, dmid
+            dq, dkv, cosine, sine, weights, weights, tokens[m], scale_one[m * BLOCK : (m + 1) * BLOCK], gain_one, dmid
         )
 
-    back_two, back_one = together(back_two, back_one)
+    back_two, back_one = together(back_two, back_one, gate_half)[:2]
     back_two = earlier(add(back_two, far_two[1]))
     grad_x_one, dkv_one, dgain_one = back_last(0, dq_one, back_one, first[0])
     back_two, dkv_one = together(back_two, dkv_one)
@@ -875,27 +1012,32 @@
         back_two = earlier(add(back_two, piece))
     back_two = add(back_two, far_two[-1])
     grad_x_two, dkv_two, dgain_two = back_last(1, dq_two, back_two, second[0])
-
     gain_rows = jnp.concatenate([dgain_one + dgain_two, first[4] + second[4]], axis=0)
     gain_columns = jnp.pad(gain_rows.T, ((0, 0), (EXPERTS, LANES - EXPERTS - 2)))
-    gain_columns = after(gain_columns, down_grad, gate_grad)
     keep, send = dense_grads(
         core, features // dp, [normed] * micros, [dq_one, dq_two], [dkv_one, dkv_two], [k[1] for k in mids],
         [first[3], second[3]], [h[1] for h in heads], [first[1], second[1]], gain_columns,
     )
-    dense_sum = share(add(keep, swap(send)), 0)
+    got = swap(send)
+    mixture_sums = combine(slot_rows[1], after(scaled[1], keep))
+    got, mixture_sums = together(got, mixture_sums)
+    dense_sums = halve_first(keep[None], got[None], 3 * LANES)
+    held = ring(ring_block(after(mixture_sums, dense_sums[0]), 0))
+    held = ring(add(held, ring_block(mixture_sums, 1)))
+    held, *dense_sums = together(held, *dense_sums)
+    dense_sums = halve_second(dense_sums)
+    held = after(held, *dense_sums[::2])
+    for step in range(2, count - 1):
+        held = ring(add(held, ring_block(mixture_sums, step)))
+    held, gate_grad, up_grad, *dense_sums = together(held, gate_grad, up_grad, *dense_sums)
+    mixtures.append(add(held, ring_block(mixture_sums, count - 1)))
+    dense_sum = halve_last(dense_sums, 2, BF)[0]
+    gate_grad, up_grad, down_grad = gate_grad.astype(F32), up_grad.astype(F32), down_grad.astype(F32)
     dense = lax.psum(dense_sum, "expert").astype(F32)
     columns = lambda start, width: dense[:, start : start + width]
     small = QD + 2 * KD
 
-    mixed = []
-    for m in range(micros):
-        sums = combine(slot_rows[m], after(scaled[m], keep))
-        block = lambda j: lax.dynamic_slice_in_dim(sums, (rank - 1 - j) % count * BLOCK, BLOCK, 0)
-        held = block(0)
-        for step in range(1, count):
-            held = add(ring(held), block(step))
-        mixed.append((mids[m][0] + held.astype(F32)).astype(BF))
+    mixed = [(mids[m][0] + mixtures[m].astype(F32)).astype(BF) for m in range(micros)]
     return (
         jnp.stack(mixed),
         jnp.stack([grad_x_one, grad_x_two]),
@@ -906,9 +1048,9 @@
         columns(small + LANES, features),
         dense[:, small + EXPERTS + 1],
         columns(small, EXPERTS),
-        gate_grad.astype(F32),
-        up_grad.astype(F32),
-        down_grad.astype(F32),
+        gate_grad,
+        up_grad,
+        down_grad,
     )
 
 

time: 1020 us -> 890 us (0.87)
  waiting for transfers between devices: 519 us -> 381 us
  Pallas kernels: 290 us -> 310 us
    reduce_scatter x6 -> x4, waiting for transfers between devices: 123 us -> 12.8 us  [the longest x1 12.8 us: local(): lax.psum_scatter(dx_sums[0], 'expert', scatter_dimension=0, tiled=True)]
    ppermute x0 -> x4, waiting for transfers between devices: none -> 55.9 us  [local(): lax.ppermute(a, 'dp', [(i, i ^ bit) for i in range(dp)])]
    ppermute x6, waiting for transfers between devices: 109 us -> 58 us  [local(): later = lambda a: lax.ppermute(a, 'expert', upward)]
    all_gather x4 -> x3, waiting for transfers between devices: 55.7 us -> 21.5 us  [local(): every = lambda a, axis: lax.all_gather(a, axis, axis=0, tiled=True)]
    ppermute x9 -> x12, waiting for transfers between devices: 90.8 us -> 117 us  [local(): ring = lambda a: lax.ppermute(a, 'expert', around)]
    pallas_call x0 -> x3, Pallas kernels: none -> 18.7 us  [the longest x1 12.6 us: fold(): pl.pallas_call(partial(fold_kernel, cut, step), grid_spec=pltpu.PrefetchS...]
    ppermute x6, starting transfers between devices: 40.8 us -> 24 us  [local(): later = lambda a: lax.ppermute(a, 'expert', upward)]
    ppermute x4, waiting for transfers between devices: 13.9 us -> 3.06 us  [local(): swap = lambda a: lax.ppermute(a, 'dp', [(i, i ^ 1) for i in range(dp)])]
  transfers between devices with their start and end apart: 36 -> 40, of which waited for: 23 -> 25; matrix products, arithmetic and copies ran while one was open for 10% -> 11% of each run, Pallas kernels for 24% -> 34%
where the time goes in v3:
time: 890 us; the launch traced here: 879 us
  waiting for transfers between devices  381 us (43%)
  Pallas kernels  310 us (35%)
  other arithmetic  75.8 us (9%)
  starting transfers between devices  48.3 us (5%)
  local copies, waits for them, and re-layouts  48.1 us (5%)
  between operations  15.4 us (2%)
    ppermute x12, waiting for transfers between devices, local(): ring = lambda a: lax.ppermute(a, 'expert', around)  117 us
    pallas_call x2, Pallas kernels, expert_pass(): pl.pallas_call(expert_kernel, grid_spec=pltpu.PrefetchScalarGridSpec(num_...  76.3 us
    ppermute x6, waiting for transfers between devices, local(): later = lambda a: lax.ppermute(a, 'expert', upward)  58 us
    ppermute x6, waiting for transfers between devices, local(): earlier = lambda a: lax.ppermute(a, 'expert', downward)  57 us
    ppermute x4, waiting for transfers between devices, local(): lax.ppermute(a, 'dp', [(i, i ^ bit) for i in range(dp)])  55.9 us
    psum x1, waiting for transfers between devices, local(): dense = lax.psum(dense_sum, 'expert').astype(F32)  55.5 us
    convert_element_type x16, other arithmetic, local(): add = lambda a, b: (a.astype(F32) + b.astype(F32)).astype(BF)  48.7 us
    pallas_call x2, Pallas kernels, weight_pass(): pl.pallas_call(partial(weight_kernel, count, products, step), grid_spec=p...  42.7 us
  transfers between devices with their start and end apart: 40, of which 25 were waited for; matrix products, arithmetic and copies ran while one was open for 11% of the time, Pallas kernels for 34%

profile of v3, /device:TPU:0, one launch (start us, length us, event | category | flops | bytes accessed | tf_op | source)
XLA Modules:
  0.0 879.2 jit_solution(1296881874998087267)
XLA Ops:
  19.3 39.2 %collective-permute-done = bf16[2,256,1664]{1,2,0:T(8,128)(2,1)S(1)} collective-permute-done((bf16[2,256,1664]{1,2,0:T(8,128)(2,1)S(1)}, bf16[2,256,1664]{1,2,0:T(8,128)(2,1)S(1)}, u32[]{:S(2)}, u32[]{:S(2)}) %collective-permute-start) | collective-permute-done | bytes 1703968 | tf_op jit(solution)/shard_map/ppermute | solution.py:836
  60.0 38.8 %collective-permute-done.1 = bf16[2,256,1664]{1,2,0:T(8,128)(2,1)} collective-permute-done((bf16[2,256,1664]{1,2,0:T(8,128)(2,1)S(1)}, bf16[2,256,1664]{1,2,0:T(8,128)(2,1)}, u32[]{:S(2)}, u32[]{:S(2)}) %collective-permute-start.1) | collective-permute-done | bytes 1703968 | tf_op jit(solution)/shard_map/ppermute | solution.py:836
  110.3 35.3 %collective-permute-done.2.refs_1_.refs_5_ = bf16[256,1024]{1,0:T(8,128)(2,1)S(1)} collective-permute-done((bf16[256,1024]{1,0:T(8,128)(2,1)}, bf16[256,1024]{1,0:T(8,128)(2,1)S(1)}, u32[]{:S(2)}, u32[]{:S(2)}) %collective-permute-start.2) | collective-permute-done | bytes 524320 | tf_op jit(solution)/shard_map/ppermute | solution.py:837
  149.9 9.0 %collective-permute-done.3.refs_2_.refs_6_ = bf16[256,1024]{1,0:T(8,128)(2,1)S(1)} collective-permute-done((bf16[256,1024]{1,0:T(8,128)(2,1)S(1)}, bf16[256,1024]{1,0:T(8,128)(2,1)S(1)}, u32[]{:S(2)}, u32[]{:S(2)}) %collective-permute-start.3) | collective-permute-done | bytes 524320 | tf_op jit(solution)/shard_map/ppermute | solution.py:837
  163.4 8.1 collective-permute-done.4.refs_3_.refs_7_
  176.7 7.8 project.3
  266.4 12.6 %all-gather.6.cloned.1.call-done.rows_ref = bf16[1024,1664]{1,0:T(8,128)(2,1)} async-done(((bf16[256,1664]{1,0:T(8,128)(2,1)}), bf16[1024,1664]{1,0:T(8,128)(2,1)}) %all-gather.6.cloned.1.call-update) | async-done | bytes 3407888 | tf_op jit(solution)/shard_map/all_gather | solution.py:840
  286.1 38.3 %experts.2 = (bf16[10,256,1536]{2,1,0:T(8,128)(2,1)}, bf16[10,256,1664]{2,1,0:T(8,128)(2,1)}, bf16[10,256,1536]{2,1,0:T(8,128)(2,1)}, bf16[10,256,512]{2,1,0:T(8...) custom-call(s32[1]{0:T(128)} %bitcast.7.rank_ref, ...), custom_call_target="tpu_custom_call" | custom-call | flops 2415919104 | bytes 8650752 | tf_op jit(solution)/shard_map/experts/pallas_call | solution.py:663
  338.7 8.9 %all-gather.8.cloned.1.call-done.rows_ref = bf16[1024,1664]{1,0:T(8,128)(2,1)} async-done(((bf16[256,1664]{1,0:T(8,128)(2,1)}), bf16[1024,1664]{1,0:T(8,128)(2,1)}) %all-gather.8.cloned.1.call-update) | async-done | bytes 3407888 | tf_op jit(solution)/shard_map/all_gather | solution.py:840
  355.2 38.0 %experts.3 = (bf16[10,256,1536]{2,1,0:T(8,128)(2,1)}, bf16[10,256,1664]{2,1,0:T(8,128)(2,1)}, bf16[10,256,1536]{2,1,0:T(8,128)(2,1)}, bf16[10,256,512]{2,1,0:T(8...) custom-call(s32[1]{0:T(128)} %bitcast.7.rank_ref, ...), custom_call_target="tpu_custom_call" | custom-call | flops 2415919104 | bytes 8650752 | tf_op jit(solution)/shard_map/experts/pallas_call | solution.py:663
  400.6 12.8 %reduce-scatter.5.cloned.1.call-done.dx_ref = bf16[256,1664]{1,0:T(8,128)(2,1)} async-done(((bf16[1024,1664]{1,0:T(8,128)(2,1)}), bf16[256,1664]{1,0:T(8,128)(2,1)}) %reduce-scatter.5.cloned.1.call-update) | async-done | bytes 851984 | tf_op jit(solution)/shard_map/reduce_scatter | solution.py:949
  416.6 18.3 %expert_weights.2 = (bf16[10,256,1536]{2,1,0:T(8,128)(2,1)}, bf16[10,256,1536]{2,1,0:T(8,128)(2,1)}) custom-call(s32[1]{0:T(128)} %bitcast.20.core_ref, bf16[10,256,512]{2,1,0:T(8,128)(2,1)} %get-tuple-element.185.refs_0_, bf16[10,256,512]{2,1,0:T(8,128)(2,1)} %get-tuple-element.186.refs_1_, bf16[10,256,1536]{2,1,0:T(8,128)(2,1)} %get-tuple-element.187.refs_2_, ...), custom_call_target="tpu_custom_call" | custom-call | flops 805306368 | bytes 3670016 | tf_op jit(solution)/shard_map/expert_weights/pallas_call | solution.py:703
  443.1 24.4 %expert_weights.3 = (bf16[10,768,512]{2,1,0:T(8,128)(2,1)}, bf16[10,768,512]{2,1,0:T(8,128)(2,1)}, bf16[10,768,512]{2,1,0:T(8,128)(2,1)}, bf16[10,768,512]{2,1,0:T(8,128)(2,1)}) custom-call(s32[1]{0:T(128)} %bitcast.20.core_ref, bf16[10,256,1664]{2,1,0:T(8,128)(2,1)} %dispatch.4.x_ref.refs_0_, bf16[10,256,1664]{2,1,0:T(8,128)(2,1)} %dispatch.7.x_ref.refs_1_, ...), custom_call_target="tpu_custom_call" | custom-call | flops 1610612736 | bytes 5767168 | tf_op jit(solution)/shard_map/expert_weights/pallas_call | solution.py:703
  467.6 11.0 %add_convert_fusion.2 = bf16[10,256,1536]{2,1,0:T(8,128)(2,1)} fusion(bf16[10,256,1536]{2,1,0:T(8,128)(2,1)} %collective-permute-done.12, bf16[10,256,1536]{2,1,0:T(8,128)(2,1)} %get-tuple-element.191), kind=kLoop, calls=%fused_computation.2 | loop fusion | flops 15728640 | bytes 23592960 | tf_op jit(solution)/shard_map/convert_element_type | solution.py:839
  494.4 11.8 %attend_back.2 = (bf16[256,1536]{1,0:T(8,128)(2,1)}, bf16[2,256,512]{2,1,0:T(8,128)(2,1)}, bf16[2,256,512]{2,1,0:T(8,128)(2,1)}, bf16[2,256,512]{2,1,0:T(8,128)(2,1)}, bf16[2,256,512]{2,1,0:T(8,128)(2,1)}) custom-call(s32[1]{0:T(128)} %bitcast.4.place_ref, bf16[256,1536]{1,0:T(8,128)(2,1)} %get-tuple-element.163.q_ref, ...), custom_call_target="tpu_custom_call" | custom-call | flops 1610612736 | bytes 550502 | tf_op jit(solution)/shard_map/attend_back/pallas_call | solution.py:526
  506.2 15.0 %collective-permute-done.15 = bf16[256,1536]{1,0:T(8,128)(2,1)S(1)} collective-permute-done((bf16[256,1536]{1,0:T(8,128)(2,1)S(1)}, bf16[256,1536]{1,0:T(8,128)(2,1)S(1)}, u32[]{:S(2)}, u32[]{:S(2)}) %collective-permute-start.15) | collective-permute-done | bytes 786464 | tf_op jit(solution)/shard_map/ppermute | solution.py:836
  522.2 11.1 %add_convert_fusion.1 = bf16[10,768,512]{2,1,0:T(8,128)(2,1)} fusion(bf16[10,768,512]{2,1,0:T(8,128)(2,1)} %collective-permute-done.17, bf16[10,768,512]{2,1,0:T(8,128)(2,1)} %get-tuple-element.219), kind=kLoop, calls=%fused_computation.1 | loop fusion | flops 15728640 | bytes 23592960 | tf_op jit(solution)/shard_map/convert_element_type | solution.py:839
  536.9 8.3 home_back.3
  551.6 11.5 %attend_back.3 = (bf16[256,1536]{1,0:T(8,128)(2,1)}, bf16[2,256,512]{2,1,0:T(8,128)(2,1)}, bf16[2,256,512]{2,1,0:T(8,128)(2,1)}, bf16[2,256,512]{2,1,0:T(8,128)(2,1)}, bf16[2,256,512]{2,1,0:T(8,128)(2,1)}) custom-call(s32[1]{0:T(128)} %bitcast.4.place_ref, bf16[256,1536]{1,0:T(8,128)(2,1)} %get-tuple-element.170.q_ref, ...), custom_call_target="tpu_custom_call" | custom-call | flops 1610612736 | bytes 550502 | tf_op jit(solution)/shard_map/attend_back/pallas_call | solution.py:526
  563.1 16.6 %collective-permute-done.18 = bf16[2,256,512]{2,1,0:T(8,128)(2,1)} collective-permute-done((bf16[2,256,512]{2,1,0:T(8,128)(2,1)S(1)}, bf16[2,256,512]{2,1,0:T(8,128)(2,1)}, u32[]{:S(2)}, u32[]{:S(2)}) %collective-permute-start.18) | collective-permute-done | bytes 524320 | tf_op jit(solution)/shard_map/ppermute | solution.py:838
  579.7 11.5 %add_convert_fusion = bf16[10,768,512]{2,1,0:T(8,128)(2,1)} fusion(bf16[10,768,512]{2,1,0:T(8,128)(2,1)} %collective-permute-done.16, bf16[10,768,512]{2,1,0:T(8,128)(2,1)} %get-tuple-element.242), kind=kLoop, calls=%fused_computation | loop fusion | flops 15728640 | bytes 23592960 | tf_op jit(solution)/shard_map/convert_element_type | solution.py:839
  595.6 14.1 %collective-permute-done.21 = bf16[2,256,512]{2,1,0:T(8,128)(2,1)S(1)} collective-permute-done((bf16[2,256,512]{2,1,0:T(8,128)(2,1)S(1)}, bf16[2,256,512]{2,1,0:T(8,128)(2,1)S(1)}, u32[]{:S(2)}, u32[]{:S(2)}) %collective-permute-start.21) | collective-permute-done | bytes 524320 | tf_op jit(solution)/shard_map/ppermute | solution.py:838
  611.6 8.1 collective-permute-done.20
  621.9 10.2 %last_back.2 = (f32[256,1536]{1,0:T(8,128)}, bf16[256,1024]{1,0:T(8,128)(2,1)}, f32[1,1536]{1,0:T(1,128)}) custom-call(bf16[256,1536]{1,0:T(8,128)(2,1)} %get-tuple-element.221.dq_ref.refs_2_, bf16[2,256,512]{2,1,0:T(8,128)(2,1)} %add_convert_fusion.19.dkv_ref, f32[256,128]{1,0:T(8,128)} %get-tuple-element.393.cosine_ref, ...), custom_call_target="tpu_custom_call" | custom-call | flops 201326592 | bytes 1415577 | tf_op jit(solution)/shard_map/last_back/pallas_call | solution.py:303
  636.3 12.3 %collective-permute-done.23 = bf16[2,256,512]{2,1,0:T(8,128)(2,1)S(1)} collective-permute-done((bf16[2,256,512]{2,1,0:T(8,128)(2,1)S(1)}, bf16[2,256,512]{2,1,0:T(8,128)(2,1)S(1)}, u32[]{:S(2)}, u32[]{:S(2)}) %collective-permute-start.23) | collective-permute-done | bytes 524320 | tf_op jit(solution)/shard_map/ppermute | solution.py:838
  649.5 8.9 %last_back.3 = (f32[256,1536]{1,0:T(8,128)}, bf16[256,1024]{1,0:T(8,128)(2,1)}, f32[1,1536]{1,0:T(1,128)}) custom-call(bf16[256,1536]{1,0:T(8,128)(2,1)} %get-tuple-element.236.dq_ref.refs_3_, bf16[2,256,512]{2,1,0:T(8,128)(2,1)} %add_convert_fusion.16.dkv_ref, f32[256,128]{1,0:T(8,128)} %get-tuple-element.393.cosine_ref, ...), custom_call_target="tpu_custom_call" | custom-call | flops 201326592 | bytes 1415577 | tf_op jit(solution)/shard_map/last_back/pallas_call | solution.py:303
  662.7 13.4 %dense_grads.1 = (bf16[768,4224]{1,0:T(8,128)(2,1)}, bf16[768,4224]{1,0:T(8,128)(2,1)}) custom-call(s32[1]{0:T(128)} %bitcast.20.core_ref, bf16[512,1536]{1,0:T(8,128)(2,1)} %get-tuple-element.160.normed_ref.refs_0_.refs_1_, bf16[512,1536]{1,0:T(8,128)(2,1)} %get-tuple-element.160.normed_ref.refs_0_.refs_1_, ...), custom_call_target="tpu_custom_call" | custom-call | flops 664377728 | bytes 2477260 | tf_op jit(solution)/shard_map/dense_grads/pallas_call | solution.py:370
  686.9 12.6 %fold.1 = (bf16[1,384,2304]{2,1,0:T(8,128)(2,1)}, bf16[1,384,2304]{2,1,0:T(8,128)(2,1)}, bf16[1,384,1920]{2,1,0:T(8,128)(2,1)}, bf16[1,384,1920]{2,1,0:T(8,128)(2,1)}) custom-call(s32[2]{0:T(128)} %pad_add_fusion.place_ref, bf16[1,768,4224]{2,1,0:T(8,128)(2,1)} %bitcast.70, bf16[1,768,4224]{2,1,0:T(8,128)(2,1)} %bitcast.28.got_ref), custom_call_target="tpu_custom_call" | custom-call | flops 324403 | bytes 1946419 | tf_op jit(solution)/shard_map/fold/pallas_call | solution.py:763
  703.2 17.6 %collective-permute-done.25 = bf16[256,1536]{1,0:T(8,128)(2,1)S(1)} collective-permute-done((bf16[256,1536]{1,0:T(8,128)(2,1)S(1)}, bf16[256,1536]{1,0:T(8,128)(2,1)S(1)}, u32[]{:S(2)}, u32[]{:S(2)}) %collective-permute-start.25) | collective-permute-done | bytes 786464 | tf_op jit(solution)/shard_map/ppermute | solution.py:836
  721.1 36.5 %collective-permute-done.28.got_ref = bf16[1,384,1920]{2,1,0:T(8,128)(2,1)S(1)} collective-permute-done((bf16[1,384,1920]{2,1,0:T(8,128)(2,1)}, bf16[1,384,1920]{2,1,0:T(8,128)(2,1)S(1)}, u32[]{:S(2)}, u32[]{:S(2)}) %collective-permute-start.28) | collective-permute-done | bytes 1474592 | tf_op jit(solution)/shard_map/ppermute | solution.py:843
  776.0 14.4 %collective-permute-done.31 = bf16[1,192,1920]{2,1,0:T(8,128)(2,1)} collective-permute-done((bf16[1,192,1920]{2,1,0:T(8,128)(2,1)}, bf16[1,192,1920]{2,1,0:T(8,128)(2,1)}, u32[]{:S(2)}, u32[]{:S(2)}) %collective-permute-start.31) | collective-permute-done | bytes 737312 | tf_op jit(solution)/shard_map/ppermute | solution.py:843
  810.4 55.5 %all-reduce.3.cloned.1.call-done = bf16[192,4224]{1,0:T(8,128)(2,1)} async-done(((bf16[192,4224]{1,0:T(8,128)(2,1)}), bf16[192,4224]{1,0:T(8,128)(2,1)}) %all-reduce.3.cloned.1.call-update) | async-done | bytes 1622032 | tf_op jit(solution)/shard_map/psum | solution.py:1036
  (237 shorter events, 271.9 us)
Async XLA Ops:
  7.2 91.6 %all-gather.4.cloned.1.call-start = ((), (), s32[]{:S(2)}) async-start(), calls=%async_computation.4 | async-start | bytes 14598144 | tf_op jit(solution)/shard_map/all_gather | solution.py:840
  13.4 265.6 %all-gather.6.cloned.1.call-start = ((), (), s32[]{:S(2)}) async-start(), calls=%async_computation.5 | async-start | bytes 4259840 | tf_op jit(solution)/shard_map/all_gather | solution.py:840
  16.2 42.2 %collective-permute-start = (bf16[2,256,1664]{1,2,0:T(8,128)(2,1)S(1)}, bf16[2,256,1664]{1,2,0:T(8,128)(2,1)S(1)}, u32[]{:S(2)}, u32[]{:S(2)}) collective-permute-start(bf16[2,256,1664]{1,2,0:T(8,128)(2,1)S(1)} %maximum_maximum_fusion), channel_id=1, source_target_pairs={{0,1},{1,2},{2,3},{3,0},{4,5},{5,6},{6,7},{7,4},{8,9},{9,10},{10,1... | collective-permute-start | bytes 5111816 | tf_op jit(solution)/shard_map/ppermute | solution.py:836
  58.5 40.3 %collective-permute-start.1 = (bf16[2,256,1664]{1,2,0:T(8,128)(2,1)S(1)}, bf16[2,256,1664]{1,2,0:T(8,128)(2,1)}, u32[]{:S(2)}, u32[]{:S(2)}) collective-permute-start(bf16[2,256,1664]{1,2,0:T(8,128)(2,1)S(1)} %collective-permute-done), channel_id=1, source_target_pairs={{0,1},{1,2},{2,3},{3,0},{4,5},{5,6},{6,7},{7,4},{8,9},{9,10},{10,1... | collective-permute-start | bytes 5111816 | tf_op jit(solution)/shard_map/ppermute | solution.py:836
  98.8 64.6 %collective-permute-start.5 = (bf16[2,256,1664]{1,2,0:T(8,128)(2,1)}, bf16[2,256,1664]{1,2,0:T(8,128)(2,1)}, u32[]{:S(2)}, u32[]{:S(2)}) collective-permute-start(bf16[2,256,1664]{1,2,0:T(8,128)(2,1)} %collective-permute-done.1), channel_id=1, source_target_pairs={{0,1},{1,2},{2,3},{3,0},{4,5},{5,6},{6,7},{7,4},{8,9},{9,10},{10,1... | collective-permute-start | bytes 5111816 | tf_op jit(solution)/shard_map/ppermute | solution.py:836
  109.0 36.6 %collective-permute-start.2 = (bf16[256,1024]{1,0:T(8,128)(2,1)}, bf16[256,1024]{1,0:T(8,128)(2,1)S(1)}, u32[]{:S(2)}, u32[]{:S(2)}) collective-permute-start(bf16[256,1024]{1,0:T(8,128)(2,1)} %get-tuple-element.157.refs_0_.refs_4_), channel_id=1, source_target_pairs={{0,1},{1,2},{2,3},{4,5},{5,6},{6,7},{8,9},{9,10},{10,11},{12,13},{... | collective-permute-start | bytes 1572872 | tf_op jit(solution)/shard_map/ppermute | solution.py:837
  205.4 142.2 %all-gather.8.cloned.1.call-start = ((), (), s32[]{:S(2)}) async-start(), calls=%async_computation.6 | async-start | bytes 4259840 | tf_op jit(solution)/shard_map/all_gather | solution.py:840
  233.2 180.1 %reduce-scatter.5.cloned.1.call-start = ((), (), s32[]{:S(2)}) async-start(), calls=%async_computation.7 | async-start | bytes 4259840 | tf_op jit(solution)/shard_map/reduce_scatter | solution.py:949
  347.6 232.1 %reduce-scatter.7.cloned.1.call-start = ((), (), s32[]{:S(2)}) async-start(), calls=%async_computation.8 | async-start | bytes 9830400 | tf_op jit(solution)/shard_map/reduce_scatter | solution.py:849
  415.4 22.6 %collective-permute-start.9 = (bf16[256,1664]{1,0:T(8,128)(2,1)}, bf16[256,1664]{1,0:T(8,128)(2,1)}, u32[]{:S(2)}, u32[]{:S(2)}) collective-permute-start(bf16[256,1664]{1,0:T(8,128)(2,1)} %constant_dynamic-slice_fusion.2), channel_id=1, source_target_pairs={{0,1},{1,2},{2,3},{3,0},{4,5},{5,6},{6,7},{7,4},{8,9},{9,10},{10,1... | collective-permute-start | bytes 2555912 | tf_op jit(solution)/shard_map/ppermute | solution.py:836
  438.1 29.5 %collective-permute-start.12 = (bf16[10,256,1536]{2,1,0:T(8,128)(2,1)}, bf16[10,256,1536]{2,1,0:T(8,128)(2,1)}, u32[]{:S(2)}, u32[]{:S(2)}) collective-permute-start(bf16[10,256,1536]{2,1,0:T(8,128)(2,1)} %get-tuple-element.194), channel_id=1, source_target_pairs={{0,4},{4,0},{8,12},{12,8},{16,20},{20,16},{24,28},{28,24},{1,5},{5... | collective-permute-start | bytes 23592968 | tf_op jit(solution)/shard_map/ppermute | solution.py:841
  439.4 28.1 %collective-permute-start.11 = (bf16[256,1664]{1,0:T(8,128)(2,1)S(1)}, bf16[256,1664]{1,0:T(8,128)(2,1)}, u32[]{:S(2)}, u32[]{:S(2)}) collective-permute-start(bf16[256,1664]{1,0:T(8,128)(2,1)S(1)} %add_convert_fusion.6), channel_id=1, source_target_pairs={{0,1},{1,2},{2,3},{3,0},{4,5},{5,6},{6,7},{7,4},{8,9},{9,10},{10,1... | collective-permute-start | bytes 2555912 | tf_op jit(solution)/shard_map/ppermute | solution.py:836
  441.6 38.0 %collective-permute-start.10 = (bf16[256,1536]{1,0:T(8,128)(2,1)}, bf16[256,1536]{1,0:T(8,128)(2,1)}, u32[]{:S(2)}, u32[]{:S(2)}) collective-permute-start(bf16[256,1536]{1,0:T(8,128)(2,1)} %constant_dynamic-slice_fusion.1), channel_id=1, source_target_pairs={{0,1},{1,2},{2,3},{3,0},{4,5},{5,6},{6,7},{7,4},{8,9},{9,10},{10,1... | collective-permute-start | bytes 2359304 | tf_op jit(solution)/shard_map/ppermute | solution.py:836
  479.6 296.4 %reduce-scatter.11.cloned.1.call-start = ((), (), s32[]{:S(2)}) async-start(), calls=%async_computation.10 | async-start | bytes 9830400 | tf_op jit(solution)/shard_map/reduce_scatter | solution.py:849
  479.7 42.5 %collective-permute-start.16 = (bf16[10,768,512]{2,1,0:T(8,128)(2,1)}, bf16[10,768,512]{2,1,0:T(8,128)(2,1)}, u32[]{:S(2)}, u32[]{:S(2)}) collective-permute-start(bf16[10,768,512]{2,1,0:T(8,128)(2,1)} %get-tuple-element.215), channel_id=1, source_target_pairs={{0,4},{4,0},{8,12},{12,8},{16,20},{20,16},{24,28},{28,24},{1,5},{5... | collective-permute-start | bytes 23592968 | tf_op jit(solution)/shard_map/ppermute | solution.py:841
  479.8 42.4 %collective-permute-start.17 = (bf16[10,768,512]{2,1,0:T(8,128)(2,1)}, bf16[10,768,512]{2,1,0:T(8,128)(2,1)}, u32[]{:S(2)}, u32[]{:S(2)}) collective-permute-start(bf16[10,768,512]{2,1,0:T(8,128)(2,1)} %get-tuple-element.216), channel_id=1, source_target_pairs={{0,4},{4,0},{8,12},{12,8},{16,20},{20,16},{24,28},{28,24},{1,5},{5... | collective-permute-start | bytes 23592968 | tf_op jit(solution)/shard_map/ppermute | solution.py:841
  481.6 39.6 %collective-permute-start.14 = (bf16[256,1664]{1,0:T(8,128)(2,1)S(1)}, bf16[256,1664]{1,0:T(8,128)(2,1)}, u32[]{:S(2)}, u32[]{:S(2)}) collective-permute-start(bf16[256,1664]{1,0:T(8,128)(2,1)S(1)} %add_convert_fusion.5), channel_id=1, source_target_pairs={{0,1},{1,2},{2,3},{3,0},{4,5},{5,6},{6,7},{7,4},{8,9},{9,10},{10,1... | collective-permute-start | bytes 2555912 | tf_op jit(solution)/shard_map/ppermute | solution.py:836
  483.3 38.0 %collective-permute-start.15 = (bf16[256,1536]{1,0:T(8,128)(2,1)S(1)}, bf16[256,1536]{1,0:T(8,128)(2,1)S(1)}, u32[]{:S(2)}, u32[]{:S(2)}) collective-permute-start(bf16[256,1536]{1,0:T(8,128)(2,1)S(1)} %add_convert_fusion.14), channel_id=1, source_target_pairs={{0,1},{1,2},{2,3},{3,0},{4,5},{5,6},{6,7},{7,4},{8,9},{9,10},{10,1... | collective-permute-start | bytes 2359304 | tf_op jit(solution)/shard_map/ppermute | solution.py:836
  533.3 259.6 %reduce-scatter.9.cloned.1.call-start = ((), (), s32[]{:S(2)}) async-start(), calls=%async_computation.9 | async-start | bytes 9830400 | tf_op jit(solution)/shard_map/reduce_scatter | solution.py:849
  533.3 15.2 %collective-permute-start.13 = (bf16[2,256,512]{2,1,0:T(8,128)(2,1)}, bf16[2,256,512]{2,1,0:T(8,128)(2,1)}, u32[]{:S(2)}, u32[]{:S(2)}) collective-permute-start(bf16[2,256,512]{2,1,0:T(8,128)(2,1)} %get-tuple-element.212), channel_id=1, source_target_pairs={{1,0},{2,1},{3,2},{5,4},{6,5},{7,6},{9,8},{10,9},{11,10},{13,12},{... | collective-permute-start | bytes 1572872 | tf_op jit(solution)/shard_map/ppermute | solution.py:838
  548.8 30.9 %collective-permute-start.19 = (bf16[256,1536]{1,0:T(8,128)(2,1)S(1)}, bf16[256,1536]{1,0:T(8,128)(2,1)}, u32[]{:S(2)}, u32[]{:S(2)}) collective-permute-start(bf16[256,1536]{1,0:T(8,128)(2,1)S(1)} %add_convert_fusion.13), channel_id=1, source_target_pairs={{0,1},{1,2},{2,3},{3,0},{4,5},{5,6},{6,7},{7,4},{8,9},{9,10},{10,1... | collective-permute-start | bytes 2359304 | tf_op jit(solution)/shard_map/ppermute | solution.py:836
  550.0 29.7 %collective-permute-start.18 = (bf16[2,256,512]{2,1,0:T(8,128)(2,1)S(1)}, bf16[2,256,512]{2,1,0:T(8,128)(2,1)}, u32[]{:S(2)}, u32[]{:S(2)}) collective-permute-start(bf16[2,256,512]{2,1,0:T(8,128)(2,1)S(1)} %add_convert_fusion.21), channel_id=1, source_target_pairs={{1,0},{2,1},{3,2},{5,4},{6,5},{7,6},{9,8},{10,9},{11,10},{13,12},{... | collective-permute-start | bytes 1572872 | tf_op jit(solution)/shard_map/ppermute | solution.py:838
  591.2 274.7 %all-reduce.3.cloned.1.call-start = ((), (), s32[]{:S(2)}) async-start(), calls=%async_computation.11 | async-start | bytes 3244032 | tf_op jit(solution)/shard_map/psum | solution.py:1036
  593.0 16.7 %collective-permute-start.21 = (bf16[2,256,512]{2,1,0:T(8,128)(2,1)S(1)}, bf16[2,256,512]{2,1,0:T(8,128)(2,1)S(1)}, u32[]{:S(2)}, u32[]{:S(2)}) collective-permute-start(bf16[2,256,512]{2,1,0:T(8,128)(2,1)S(1)} %add_convert_fusion.20), channel_id=1, source_target_pairs={{1,0},{2,1},{3,2},{5,4},{6,5},{7,6},{9,8},{10,9},{11,10},{13,12},{... | collective-permute-start | bytes 1572872 | tf_op jit(solution)/shard_map/ppermute | solution.py:838
  594.3 25.5 %collective-permute-start.20 = (bf16[2,256,512]{2,1,0:T(8,128)(2,1)}, bf16[2,256,512]{2,1,0:T(8,128)(2,1)S(1)}, u32[]{:S(2)}, u32[]{:S(2)}) collective-permute-start(bf16[2,256,512]{2,1,0:T(8,128)(2,1)} %get-tuple-element.237), channel_id=1, source_target_pairs={{1,0},{2,1},{3,2},{5,4},{6,5},{7,6},{9,8},{10,9},{11,10},{13,12},{... | collective-permute-start | bytes 1572872 | tf_op jit(solution)/shard_map/ppermute | solution.py:838
  699.6 21.2 %collective-permute-start.25 = (bf16[256,1536]{1,0:T(8,128)(2,1)S(1)}, bf16[256,1536]{1,0:T(8,128)(2,1)S(1)}, u32[]{:S(2)}, u32[]{:S(2)}) collective-permute-start(bf16[256,1536]{1,0:T(8,128)(2,1)S(1)} %constant_dynamic-slice_fusion), channel_id=1, source_target_pairs={{0,1},{1,2},{2,3},{3,0},{4,5},{5,6},{6,7},{7,4},{8,9},{9,10},{10,1... | collective-permute-start | bytes 2359304 | tf_op jit(solution)/shard_map/ppermute | solution.py:836
  701.1 61.6 %collective-permute-start.27 = (bf16[1,384,2304]{2,1,0:T(8,128)(2,1)}, bf16[1,384,2304]{2,1,0:T(8,128)(2,1)}, u32[]{:S(2)}, u32[]{:S(2)}) collective-permute-start(bf16[1,384,2304]{2,1,0:T(8,128)(2,1)} %get-tuple-element.273), channel_id=1, source_target_pairs={{0,8},{4,12},{8,0},{12,4},{16,24},{20,28},{24,16},{28,20},{1,9},{5... | collective-permute-start | bytes 5308424 | tf_op jit(solution)/shard_map/ppermute | solution.py:843
  702.6 55.0 %collective-permute-start.28 = (bf16[1,384,1920]{2,1,0:T(8,128)(2,1)}, bf16[1,384,1920]{2,1,0:T(8,128)(2,1)S(1)}, u32[]{:S(2)}, u32[]{:S(2)}) collective-permute-start(bf16[1,384,1920]{2,1,0:T(8,128)(2,1)} %get-tuple-element.275), channel_id=1, source_target_pairs={{0,16},{4,20},{8,24},{12,28},{16,0},{20,4},{24,8},{28,12},{1,17},{... | collective-permute-start | bytes 4423688 | tf_op jit(solution)/shard_map/ppermute | solution.py:843
  721.0 36.6 %collective-permute-start.26 = (bf16[256,1536]{1,0:T(8,128)(2,1)S(1)}, bf16[256,1536]{1,0:T(8,128)(2,1)}, u32[]{:S(2)}, u32[]{:S(2)}) collective-permute-start(bf16[256,1536]{1,0:T(8,128)(2,1)S(1)} %add_convert_fusion.10), channel_id=1, source_target_pairs={{0,1},{1,2},{2,3},{3,0},{4,5},{5,6},{6,7},{7,4},{8,9},{9,10},{10,1... | collective-permute-start | bytes 2359304 | tf_op jit(solution)/shard_map/ppermute | solution.py:836
  768.8 24.1 %collective-permute-start.30 = (bf16[1,192,2304]{2,1,0:T(8,128)(2,1)}, bf16[1,192,2304]{2,1,0:T(8,128)(2,1)}, u32[]{:S(2)}, u32[]{:S(2)}) collective-permute-start(bf16[1,192,2304]{2,1,0:T(8,128)(2,1)} %get-tuple-element.284), channel_id=1, source_target_pairs={{0,16},{4,20},{8,24},{12,28},{16,0},{20,4},{24,8},{28,12},{1,17},{... | collective-permute-start | bytes 2654216 | tf_op jit(solution)/shard_map/ppermute | solution.py:843
  772.6 20.2 %collective-permute-start.29 = (bf16[256,1536]{1,0:T(8,128)(2,1)}, bf16[256,1536]{1,0:T(8,128)(2,1)}, u32[]{:S(2)}, u32[]{:S(2)}) collective-permute-start(bf16[256,1536]{1,0:T(8,128)(2,1)} %add_convert_fusion.9), channel_id=1, source_target_pairs={{0,1},{1,2},{2,3},{3,0},{4,5},{5,6},{6,7},{7,4},{8,9},{9,10},{10,1... | collective-permute-start | bytes 2359304 | tf_op jit(solution)/shard_map/ppermute | solution.py:836
  773.0 17.4 %collective-permute-start.31 = (bf16[1,192,1920]{2,1,0:T(8,128)(2,1)}, bf16[1,192,1920]{2,1,0:T(8,128)(2,1)}, u32[]{:S(2)}, u32[]{:S(2)}) collective-permute-start(bf16[1,192,1920]{2,1,0:T(8,128)(2,1)} %get-tuple-element.285), channel_id=1, source_target_pairs={{0,8},{4,12},{8,0},{12,4},{16,24},{20,28},{24,16},{28,20},{1,9},{5... | collective-permute-start | bytes 2211848 | tf_op jit(solution)/shard_map/ppermute | solution.py:843
  (45 other events, 506.8 us)
Sparse Core Ops, SparseCore 0:
  13.5 76.4 all-gather.3
  205.5 73.3 all-gather.5
  281.1 66.4 all-gather.7
  350.3 62.9 reduce-scatter.4
  479.7 82.6 reduce-scatter.6
  565.3 83.3 reduce-scatter.10
  651.7 104.6 reduce-scatter.8
  797.5 68.4 all-reduce.2

commit v4 on v3

--- a/solution.py
+++ b/solution.py
@@ -691,15 +691,20 @@
     outs, held_ref = refs[count * (1 + products) : -1], refs[-1]
     for i in range(products):
         total = sum(left_dot(lefts[m][0], rights[i * count + m][0]) for m in range(count))
-        held_ref[...] = total.astype(BF)
-        halves(core_ref, held_ref, step, outs[2 * i].at[0], outs[2 * i + 1].at[0])
+        if step is None:
+            outs[i][0] = total.astype(BF)
+        else:
+            held_ref[...] = total.astype(BF)
+            halves(core_ref, held_ref, step, outs[2 * i].at[0], outs[2 * i + 1].at[0])
 
 
 def weight_pass(core, step, depth, lefts, *rights):
     experts, rows, width = rights[0][0].shape
     one = lambda e, s: (e, 0, 0)
     count, products = len(lefts), len(rights)
-    half = jax.ShapeDtypeStruct((experts, depth // 2, width), BF)
+    part = depth if step is None else depth // 2
+    copies = products if step is None else 2 * products
+    half = jax.ShapeDtypeStruct((experts, part, width), BF)
     return pl.pallas_call(
         partial(weight_kernel, count, products, step),
         grid_spec=pltpu.PrefetchScalarGridSpec(
@@ -709,10 +714,10 @@
                 *[pl.BlockSpec((1, rows, depth), one) for _ in lefts],
                 *[pl.BlockSpec((1, rows, width), one) for right in rights for _ in right],
             ],
-            out_specs=[pl.BlockSpec((1, depth // 2, width), one)] * (2 * products),
+            out_specs=[pl.BlockSpec((1, part, width), one)] * copies,
             scratch_shapes=[pltpu.VMEM((depth, width), BF)],
         ),
-        out_shape=[half] * (2 * products),
+        out_shape=[half] * copies,
         compiler_params=params(),
         cost_estimate=cost(
             flops=2 * count * products * experts * rows * depth * width,
@@ -721,6 +726,31 @@
         ),
         name="expert_weights",
     )(core, *lefts, *[a for right in rights for a in right])
+
+
+def split_kernel(sums_ref, query_ref, key_ref, value_ref, router_ref, gains_ref, out_ref):
+    part = lambda start, width: sums_ref[:, start : start + width].astype(F32)
+    small = QD + 2 * KD
+    query_ref[...] = part(0, QD)
+    key_ref[...] = part(QD, KD)
+    value_ref[...] = part(QD + KD, KD)
+    table = part(small, LANES)
+    router_ref[...] = table[:, :EXPERTS]
+    gains_ref[...] = table[:, EXPERTS : EXPERTS + 2]
+    out_ref[...] = part(small + LANES, out_ref.shape[1])
+
+
+def split_dense(sums):
+    rows, width = sums.shape
+    shape = lambda n: jax.ShapeDtypeStruct((rows, n), F32)
+    widths = (QD, KD, KD, EXPERTS, 2, width - QD - 2 * KD - LANES)
+    return pl.pallas_call(
+        split_kernel,
+        out_shape=[shape(n) for n in widths],
+        compiler_params=params(),
+        cost_estimate=cost(flops=0, bytes_accessed=6 * rows * width, transcendentals=0),
+        name="split_dense",
+    )(sums)
 
 
 def fold_kernel(cut, step, place_ref, keep_ref, got_ref, *outs):
@@ -898,12 +928,13 @@
     normed, scale_one = norm_rows(x_whole, gain_one)
     normed = after(normed, dy_ring[-1])
     kv_own = project(normed, weights, QD + features, 2 * KD, KD, cosine, sine)
+    dy_last = [ring(dy_ring[-1][0])]
+    kv_own = list(kv_own)
+    kv_own[0], dy_last[0] = together(kv_own[0], dy_last[0])
     kv_one = [kv_own[0]]
     for _ in range(seq_blocks - 1):
         kv_one.append(later(kv_one[-1]))
-    while len(dy_ring) < count:
-        dy_ring.append(ring(dy_ring[-1]))
-    kv_one[-1], dy_ring[-1] = together(kv_one[-1], dy_ring[-1])
+    dy_last.append(ring(after(dy_ring[-1][1], kv_one[-1])))
 
     kv_two = [after(kv_own[1], kv_one[-1])]
     kv_two.append(later(kv_two[-1]))
@@ -911,7 +942,8 @@
     kv_two[-1], queries[0] = together(kv_two[-1], queries[0])
     kv_two.append(later(kv_two[-1]))
     o_one, ob_one, lse_one = attend(place, queries[0], kv_one)
-    kv_two[-1], ob_one = together(kv_two[-1], ob_one)
+    kv_two[-1], dy_last[1], ob_one = together(kv_two[-1], dy_last[1], ob_one)
+    dy_ring.append(dy_last)
     kv_two.append(later(kv_two[-1]))
     go_out = lambda m, ob: outward(ob, weights, tokens[m], gain_two, router_w, routes[m])
     mids = [list(go_out(0, ob_one))]
@@ -919,53 +951,49 @@
     kv_two[-1], mids[0][1] = together(kv_two[-1], mids[0][1])
     while len(kv_two) < seq_blocks:
         kv_two.append(later(kv_two[-1]))
+    def in_order(m):
+        whole = jnp.zeros((count * BLOCK, features + LANES), BF)
+        for step, block in enumerate(dy_ring):
+            whole = lax.dynamic_update_slice_in_dim(whole, block[m], (rank - step) % count * BLOCK, 0)
+        return whole
+
+    slot_rows, dy_slots = [], []
+    for m in range(micros):
+        dy_all = in_order(m)
+        table = lax.dynamic_slice_in_dim(dy_all, features + rank * exp_dev, exp_dev, 1)
+        slot_rows.append(table.astype(F32).T)
+        dy_slots.append(dispatch(slot_rows[m], dy_all, features))
+    kv_two[-1], *dy_slots = together(kv_two[-1], *dy_slots)
     o_two, ob_two, lse_two = attend(place, queries[1], kv_two)
     mids.append(list(go_out(1, ob_two)))
     sent.append(every(mids[1][1], "expert"))
     kvs = (kv_one, kv_two)
     heads = ((o_one, ob_one, lse_one), (o_two, ob_two, lse_two))
 
-    def in_order(m):
-        whole = jnp.zeros((count * BLOCK, features + LANES), BF)
-        for step, block in enumerate(dy_ring):
-            whole = lax.dynamic_update_slice_in_dim(whole, block[m], (rank - step) % count * BLOCK, 0)
-        return whole
-
-    parts, slot_rows, scaled, dx_sums, dx_home = [], [], [], [], []
-    for m in range(micros):
-        dy_all = in_order(m)
-        table = lax.dynamic_slice_in_dim(dy_all, features + rank * exp_dev, exp_dev, 1)
-        slot_rows.append(table.astype(F32).T)
-        dy_slots = dispatch(slot_rows[m], dy_all, features)
-        if m > 0:
-            mixture_sums = combine(slot_rows[0], after(scaled[0], dx_sums[0]))
-            sent[m], dy_slots, dx_sums[-1], mixture_sums = together(sent[m], dy_slots, dx_sums[-1], mixture_sums)
-        x_slots = dispatch(slot_rows[m], sent[m], features + LANES)
-        ys, dx, *rest = expert_pass(rank.astype(jnp.int32)[None], x_slots, dy_slots, w_gate, w_up, w_down)
-        parts.append((x_slots, *rest))
-        scaled.append(ys)
-        dx_sums.append(combine(slot_rows[m], dx))
+    own = rank.astype(jnp.int32)[None]
+    experts = lambda m, x: expert_pass(own, x, dy_slots[m], w_gate, w_up, w_down)
     ring_block = lambda sums, j: lax.dynamic_slice_in_dim(sums, (rank - 1 - j) % count * BLOCK, BLOCK, 0)
-    dx_home = [lax.psum_scatter(dx_sums[0], "expert", scatter_dimension=0, tiled=True)]
-
-    xs, gdys, acts, dgs, dus = zip(*parts)
+    x_one = dispatch(slot_rows[0], sent[0], features + LANES)
+    ys_one, dx_one, gdy_one, act_one, dg_one, du_one = experts(0, x_one)
+    dx_one = combine(slot_rows[0], dx_one)
+    dx_home = [lax.psum_scatter(dx_one, "expert", scatter_dimension=0, tiled=True)]
+    mixture_one = combine(slot_rows[0], after(ys_one, dx_one))
+    sent[1], mixture_one = together(sent[1], mixture_one)
+    x_two = dispatch(slot_rows[1], sent[1], features + LANES)
+    ys_two, dx_two, gdy_two, act_two, dg_two, du_two = experts(1, x_two)
+
     hidden = w_down.shape[1]
-    first_act, dx_home[0], dx_sums[1] = together(acts[0], dx_home[0], dx_sums[1])
-    dx_held = ring(ring_block(dx_sums[1], 0))
-    keep_down, send_down = weight_pass(core, hidden // dp, hidden, (first_act, *acts[1:]), gdys)
-    dx_held, keep_down, send_down = together(dx_held, keep_down, send_down)
-    got_down = swap(send_down)
-    dx_held = ring(add(dx_held, ring_block(dx_sums[1], 1)))
-    dgs = after(dgs[0], keep_down), *dgs[1:]
-    ups = weight_pass(core, features // dp, features, xs, dgs, dus)
-    held = ring(ring_block(after(mixture_sums, keep_down), 0))
-    dx_held, got_down, *ups = together(dx_held, got_down, *ups)
-    for step in range(2, count - 1):
-        dx_held = ring(add(dx_held, ring_block(dx_sums[1], step)))
-    down_half = add(keep_down, got_down)
-    held, down_half = together(held, down_half)
-    held = ring(add(held, ring_block(mixture_sums, 1)))
-    down_grad = share(down_half)
+    (new_down,) = weight_pass(core, None, hidden, (act_one, act_two), (gdy_one, gdy_two))
+    new_down, dx_home[0] = together(new_down, dx_home[0])
+    down_grad = lax.psum_scatter(new_down, "dp", scatter_dimension=1, tiled=True)
+    dx_two = combine(slot_rows[1], after(dx_two, new_down))
+    dx_held = ring(ring_block(dx_two, 0))
+    ups = weight_pass(
+        core, features // dp, features, (x_one, x_two), (after(dg_one, dx_two), dg_two), (du_one, du_two)
+    )
+    dx_held, *ups = together(dx_held, *ups)
+    for step in range(1, count - 2):
+        dx_held = ring(add(dx_held, ring_block(dx_two, step)))
     got_gate, got_up = swap(ups[1]), swap(ups[3])
 
     def back_home(m, dx):
@@ -977,14 +1005,14 @@
         dq, *pieces = attend_back(place, queries[m], dob, o, lse, cosine, sine, kvs[m])
         return dq, pieces[::-1]
 
-    first = list(back_home(0, after(dx_home[0], down_half)))
+    first = list(back_home(0, after(dx_home[0], ups[0])))
     dq_one, far_one = back_heads(0, first[2])
-    dx_held, held, got_gate, got_up, dq_one = together(dx_held, held, got_gate, got_up, dq_one)
-    dx_home.append(add(dx_held, ring_block(dx_sums[1], count - 1)))
-    for step in range(2, count - 1):
-        held = ring(add(held, ring_block(mixture_sums, step)))
+    dx_held, got_gate, got_up, dq_one = together(dx_held, got_gate, got_up, dq_one)
+    dx_held = ring(add(dx_held, ring_block(dx_two, count - 2)))
     up_half = add(ups[2], got_up)
     up_grad = share(up_half)
+    dx_home.append(add(dx_held, ring_block(dx_two, count - 1)))
+    held = ring(ring_block(after(mixture_one, dx_held), 0))
     back_one = earlier(far_one[0])
     second = list(back_home(1, after(dx_home[1], up_half, dq_one)))
     back_one, second[2] = together(back_one, second[2])
@@ -994,9 +1022,9 @@
     for piece in far_one[2:-1]:
         back_one = earlier(add(back_one, piece))
     back_two = earlier(far_two[0])
-    mixtures = [add(held, ring_block(mixture_sums, count - 1))]
     gate_half = add(after(ups[0], dq_two), got_gate)
     gate_grad = share(gate_half)
+    held = ring(add(held, ring_block(mixture_one, 1)))
     back_one = add(back_one, far_one[-1])
 
     def back_last(m, dq, dkv, dmid):
@@ -1007,7 +1035,7 @@
     back_two, back_one = together(back_two, back_one, gate_half)[:2]
     back_two = earlier(add(back_two, far_two[1]))
     grad_x_one, dkv_one, dgain_one = back_last(0, dq_one, back_one, first[0])
-    back_two, dkv_one = together(back_two, dkv_one)
+    back_two, dkv_one, held = together(back_two, dkv_one, held)
     for piece in far_two[2:-1]:
         back_two = earlier(add(back_two, piece))
     back_two = add(back_two, far_two[-1])
@@ -1018,36 +1046,38 @@
         core, features // dp, [normed] * micros, [dq_one, dq_two], [dkv_one, dkv_two], [k[1] for k in mids],
         [first[3], second[3]], [h[1] for h in heads], [first[1], second[1]], gain_columns,
     )
+    for step in range(2, count - 1):
+        held = ring(add(after(held, keep), ring_block(mixture_one, step)))
     got = swap(send)
-    mixture_sums = combine(slot_rows[1], after(scaled[1], keep))
-    got, mixture_sums = together(got, mixture_sums)
+    mixture_two = combine(slot_rows[1], after(ys_two, keep))
+    got, mixture_two, up_grad = together(got, mixture_two, up_grad)
     dense_sums = halve_first(keep[None], got[None], 3 * LANES)
-    held = ring(ring_block(after(mixture_sums, dense_sums[0]), 0))
-    held = ring(add(held, ring_block(mixture_sums, 1)))
+    held, mixture_two = together(held, mixture_two, dense_sums[0])[:2]
+    mixtures = [add(held, ring_block(mixture_one, count - 1))]
+    held = ring(ring_block(mixture_two, 0))
+    held = ring(add(held, ring_block(mixture_two, 1)))
     held, *dense_sums = together(held, *dense_sums)
     dense_sums = halve_second(dense_sums)
     held = after(held, *dense_sums[::2])
     for step in range(2, count - 1):
-        held = ring(add(held, ring_block(mixture_sums, step)))
-    held, gate_grad, up_grad, *dense_sums = together(held, gate_grad, up_grad, *dense_sums)
-    mixtures.append(add(held, ring_block(mixture_sums, count - 1)))
+        held = ring(add(held, ring_block(mixture_two, step)))
+    held, gate_grad, *dense_sums = together(held, gate_grad, *dense_sums)
+    mixtures.append(add(held, ring_block(mixture_two, count - 1)))
     dense_sum = halve_last(dense_sums, 2, BF)[0]
     gate_grad, up_grad, down_grad = gate_grad.astype(F32), up_grad.astype(F32), down_grad.astype(F32)
-    dense = lax.psum(dense_sum, "expert").astype(F32)
-    columns = lambda start, width: dense[:, start : start + width]
-    small = QD + 2 * KD
-
+    dense = split_dense(lax.psum(dense_sum, "expert"))
+    query, key, value, router, gain_columns, out = dense
     mixed = [(mids[m][0] + mixtures[m].astype(F32)).astype(BF) for m in range(micros)]
     return (
         jnp.stack(mixed),
         jnp.stack([grad_x_one, grad_x_two]),
-        dense[:, small + EXPERTS],
-        columns(0, QD),
-        columns(QD, KD),
-        columns(QD + KD, KD),
-        columns(small + LANES, features),
-        dense[:, small + EXPERTS + 1],
-        columns(small, EXPERTS),
+        gain_columns[:, 0],
+        query,
+        key,
+        value,
+        out,
+        gain_columns[:, 1],
+        router,
         gate_grad,
         up_grad,
         down_grad,

time: 890 us -> 865 us (0.972)
  other arithmetic: 75.8 us -> 60.5 us
  waiting for transfers between devices: 381 us -> 368 us
    ppermute x12 -> x13, waiting for transfers between devices: 117 us -> 154 us  [local(): ring = lambda a: lax.ppermute(a, 'expert', around)]
    ppermute x4, waiting for transfers between devices: 55.9 us -> 28.4 us  [local(): lax.ppermute(a, 'dp', [(i, i ^ bit) for i in range(dp)])]
    ppermute x6, waiting for transfers between devices: 58 us -> 34.1 us  [local(): later = lambda a: lax.ppermute(a, 'expert', upward)]
    convert_element_type x16 -> x15, other arithmetic: 48.7 us -> 34.7 us  [local(): add = lambda a, b: (a.astype(F32) + b.astype(F32)).astype(BF)]
    all_gather x3, waiting for transfers between devices: 21.5 us -> 33.1 us  [local(): every = lambda a, axis: lax.all_gather(a, axis, axis=0, tiled=True)]
    reduce_scatter x1 -> x2, waiting for transfers between devices: 12.8 us -> 1.47 us  [the longest x1 1.47 us: local(): lax.psum_scatter(dx_one, 'expert', scatter_dimension=0, tiled=True)]
  transfers between devices with their start and end apart: 40 -> 40, of which waited for: 25 -> 28; matrix products, arithmetic and copies ran while one was open for 11% -> 10% of each run, Pallas kernels for 34% -> 36%
where the time goes in v4:
time: 865 us; the launch traced here: 853 us
  waiting for transfers between devices  368 us (43%)
  Pallas kernels  316 us (37%)
  other arithmetic  60.5 us (7%)
  starting transfers between devices  53.5 us (6%)
  local copies, waits for them, and re-layouts  39.6 us (5%)
  between operations  15.3 us (2%)
    ppermute x13, waiting for transfers between devices, local(): ring = lambda a: lax.ppermute(a, 'expert', around)  154 us
    pallas_call x2, Pallas kernels, expert_pass(): pl.pallas_call(expert_kernel, grid_spec=pltpu.PrefetchScalarGridSpec(num_...  76.3 us
    ppermute x6, waiting for transfers between devices, local(): earlier = lambda a: lax.ppermute(a, 'expert', downward)  58.3 us
    psum x1, waiting for transfers between devices, local(): dense = split_dense(lax.psum(dense_sum, 'expert'))  56.6 us
    pallas_call x2, Pallas kernels, weight_pass(): pl.pallas_call(partial(weight_kernel, count, products, step), grid_spec=p...  47.5 us
    convert_element_type x15, other arithmetic, local(): add = lambda a, b: (a.astype(F32) + b.astype(F32)).astype(BF)  34.7 us
    ppermute x6, waiting for transfers between devices, local(): later = lambda a: lax.ppermute(a, 'expert', upward)  34.1 us
    all_gather x3, waiting for transfers between devices, local(): every = lambda a, axis: lax.all_gather(a, axis, axis=0, tiled=True)  33.1 us
  transfers between devices with their start and end apart: 40, of which 28 were waited for; matrix products, arithmetic and copies ran while one was open for 10% of the time, Pallas kernels for 36%

profile of v4, /device:TPU:0, one launch (start us, length us, event | category | flops | bytes accessed | tf_op | source)
XLA Modules:
  0.0 853.3 jit_solution(4361966027046542122)
XLA Ops:
  19.3 39.2 %collective-permute-done = bf16[2,256,1664]{1,2,0:T(8,128)(2,1)S(1)} collective-permute-done((bf16[2,256,1664]{1,2,0:T(8,128)(2,1)S(1)}, bf16[2,256,1664]{1,2,0:T(8,128)(2,1)S(1)}, u32[]{:S(2)}, u32[]{:S(2)}) %collective-permute-start) | collective-permute-done | bytes 1703968 | tf_op jit(solution)/shard_map/ppermute | solution.py:866
  60.0 38.6 %collective-permute-done.1 = bf16[2,256,1664]{1,2,0:T(8,128)(2,1)S(1)} collective-permute-done((bf16[2,256,1664]{1,2,0:T(8,128)(2,1)S(1)}, bf16[2,256,1664]{1,2,0:T(8,128)(2,1)S(1)}, u32[]{:S(2)}, u32[]{:S(2)}) %collective-permute-start.1) | collective-permute-done | bytes 1703968 | tf_op jit(solution)/shard_map/ppermute | solution.py:866
  110.3 11.1 %collective-permute-done.2 = bf16[256,1664]{0,1:T(8,128)(2,1)} collective-permute-done((bf16[256,1664]{0,1:T(8,128)(2,1)}, bf16[256,1664]{0,1:T(8,128)(2,1)}, u32[]{:S(2)}, u32[]{:S(2)}) %collective-permute-start.2) | collective-permute-done | bytes 852000 | tf_op jit(solution)/shard_map/ppermute | solution.py:866
  122.7 9.3 %collective-permute-done.3.refs_1_.refs_5_ = bf16[256,1024]{1,0:T(8,128)(2,1)S(1)} collective-permute-done((bf16[256,1024]{1,0:T(8,128)(2,1)}, bf16[256,1024]{1,0:T(8,128)(2,1)S(1)}, u32[]{:S(2)}, u32[]{:S(2)}) %collective-permute-start.3) | collective-permute-done | bytes 524320 | tf_op jit(solution)/shard_map/ppermute | solution.py:867
  136.3 8.1 collective-permute-done.4.refs_2_.refs_6_
  148.8 7.5 collective-permute-done.5.refs_3_.refs_7_
  161.8 7.8 project.3
  251.4 22.3 %all-gather.6.cloned.1.call-done.rows_ref = bf16[1024,1664]{1,0:T(8,128)(2,1)} async-done(((bf16[256,1664]{1,0:T(8,128)(2,1)}), bf16[1024,1664]{1,0:T(8,128)(2,1)}) %all-gather.6.cloned.1.call-update) | async-done | bytes 3407888 | tf_op jit(solution)/shard_map/all_gather | solution.py:870
  280.8 38.1 %experts.2 = (bf16[10,256,1536]{2,1,0:T(8,128)(2,1)}, bf16[10,256,1664]{2,1,0:T(8,128)(2,1)}, bf16[10,256,1536]{2,1,0:T(8,128)(2,1)}, bf16[10,256,512]{2,1,0:T(8...) custom-call(s32[1]{0:T(128)} %bitcast.10.rank_ref, ...), custom_call_target="tpu_custom_call" | custom-call | flops 2415919104 | bytes 8650752 | tf_op jit(solution)/shard_map/experts/pallas_call | solution.py:663
  333.8 10.8 %all-gather.8.cloned.1.call-done.rows_ref = bf16[1024,1664]{1,0:T(8,128)(2,1)} async-done(((bf16[256,1664]{1,0:T(8,128)(2,1)}), bf16[1024,1664]{1,0:T(8,128)(2,1)}) %all-gather.8.cloned.1.call-update) | async-done | bytes 3407888 | tf_op jit(solution)/shard_map/all_gather | solution.py:870
  351.6 38.2 %experts.3 = (bf16[10,256,1536]{2,1,0:T(8,128)(2,1)}, bf16[10,256,1664]{2,1,0:T(8,128)(2,1)}, bf16[10,256,1536]{2,1,0:T(8,128)(2,1)}, bf16[10,256,512]{2,1,0:T(8...) custom-call(s32[1]{0:T(128)} %bitcast.10.rank_ref, ...), custom_call_target="tpu_custom_call" | custom-call | flops 2415919104 | bytes 8650752 | tf_op jit(solution)/shard_map/experts/pallas_call | solution.py:663
  389.8 18.9 %expert_weights.2 = bf16[10,512,1536]{2,1,0:T(8,128)(2,1)} custom-call(s32[1]{0:T(128)} %bitcast.9.core_ref, bf16[10,256,512]{2,1,0:T(8,128)(2,1)} %get-tuple-element.177.refs_0_, bf16[10,256,512]{2,1,0:T(8,128)(2,1)} %get-tuple-element.187.refs_1_, bf16[10,256,1536]{2,1,0:T(8,128)(2,1)} %get-tuple-element.188.refs_2_, ...), custom_call_target="tpu_custom_call" | custom-call | flops 805306368 | bytes 3670016 | tf_op jit(solution)/shard_map/expert_weights/pallas_call | solution.py:708
  420.1 28.6 %expert_weights.3 = (bf16[10,768,512]{2,1,0:T(8,128)(2,1)}, bf16[10,768,512]{2,1,0:T(8,128)(2,1)}, bf16[10,768,512]{2,1,0:T(8,128)(2,1)}, bf16[10,768,512]{2,1,0:T(8,128)(2,1)}) custom-call(s32[1]{0:T(128)} %bitcast.9.core_ref, bf16[10,256,1664]{2,1,0:T(8,128)(2,1)} %dispatch.4.x_ref.refs_0_, bf16[10,256,1664]{2,1,0:T(8,128)(2,1)} %dispatch.7.x_ref.refs_1_, ...), custom_call_target="tpu_custom_call" | custom-call | flops 1610612736 | bytes 5767168 | tf_op jit(solution)/shard_map/expert_weights/pallas_call | solution.py:708
  460.6 11.7 %attend_back.2 = (bf16[256,1536]{1,0:T(8,128)(2,1)}, bf16[2,256,512]{2,1,0:T(8,128)(2,1)}, bf16[2,256,512]{2,1,0:T(8,128)(2,1)}, bf16[2,256,512]{2,1,0:T(8,128)(2,1)}, bf16[2,256,512]{2,1,0:T(8,128)(2,1)}) custom-call(s32[1]{0:T(128)} %bitcast.6.place_ref, bf16[256,1536]{1,0:T(8,128)(2,1)} %get-tuple-element.167.q_ref, ...), custom_call_target="tpu_custom_call" | custom-call | flops 1610612736 | bytes 550502 | tf_op jit(solution)/shard_map/attend_back/pallas_call | solution.py:526
  472.8 11.2 %add_convert_fusion.1 = bf16[10,768,512]{2,1,0:T(8,128)(2,1)} fusion(bf16[10,768,512]{2,1,0:T(8,128)(2,1)} %collective-permute-done.14, bf16[10,768,512]{2,1,0:T(8,128)(2,1)} %get-tuple-element.216), kind=kLoop, calls=%fused_computation.1 | loop fusion | flops 15728640 | bytes 23592960 | tf_op jit(solution)/shard_map/convert_element_type | solution.py:869
  491.8 28.7 %collective-permute-done.15 = bf16[256,1664]{1,0:T(8,128)(2,1)} collective-permute-done((bf16[256,1664]{1,0:T(8,128)(2,1)}, bf16[256,1664]{1,0:T(8,128)(2,1)}, u32[]{:S(2)}, u32[]{:S(2)}) %collective-permute-start.15) | collective-permute-done | bytes 852000 | tf_op jit(solution)/shard_map/ppermute | solution.py:866
  524.0 7.6 home_back.3
  533.2 11.6 %attend_back.3 = (bf16[256,1536]{1,0:T(8,128)(2,1)}, bf16[2,256,512]{2,1,0:T(8,128)(2,1)}, bf16[2,256,512]{2,1,0:T(8,128)(2,1)}, bf16[2,256,512]{2,1,0:T(8,128)(2,1)}, bf16[2,256,512]{2,1,0:T(8,128)(2,1)}) custom-call(s32[1]{0:T(128)} %bitcast.6.place_ref, bf16[256,1536]{1,0:T(8,128)(2,1)} %get-tuple-element.178.q_ref, ...), custom_call_target="tpu_custom_call" | custom-call | flops 1610612736 | bytes 550502 | tf_op jit(solution)/shard_map/attend_back/pallas_call | solution.py:526
  544.8 14.1 %collective-permute-done.16 = bf16[2,256,512]{2,1,0:T(8,128)(2,1)} collective-permute-done((bf16[2,256,512]{2,1,0:T(8,128)(2,1)S(1)}, bf16[2,256,512]{2,1,0:T(8,128)(2,1)}, u32[]{:S(2)}, u32[]{:S(2)}) %collective-permute-start.16) | collective-permute-done | bytes 524320 | tf_op jit(solution)/shard_map/ppermute | solution.py:868
  558.9 11.1 %add_convert_fusion = bf16[10,768,512]{2,1,0:T(8,128)(2,1)} fusion(bf16[10,768,512]{2,1,0:T(8,128)(2,1)} %collective-permute-done.13, bf16[10,768,512]{2,1,0:T(8,128)(2,1)} %get-tuple-element.238), kind=kLoop, calls=%fused_computation | loop fusion | flops 15728640 | bytes 23592960 | tf_op jit(solution)/shard_map/convert_element_type | solution.py:869
  579.0 9.4 %collective-permute-done.19 = bf16[2,256,512]{2,1,0:T(8,128)(2,1)S(1)} collective-permute-done((bf16[2,256,512]{2,1,0:T(8,128)(2,1)S(1)}, bf16[2,256,512]{2,1,0:T(8,128)(2,1)S(1)}, u32[]{:S(2)}, u32[]{:S(2)}) %collective-permute-start.19) | collective-permute-done | bytes 524320 | tf_op jit(solution)/shard_map/ppermute | solution.py:868
  589.3 11.2 %collective-permute-done.18 = bf16[2,256,512]{2,1,0:T(8,128)(2,1)S(1)} collective-permute-done((bf16[2,256,512]{2,1,0:T(8,128)(2,1)}, bf16[2,256,512]{2,1,0:T(8,128)(2,1)S(1)}, u32[]{:S(2)}, u32[]{:S(2)}) %collective-permute-start.18) | collective-permute-done | bytes 524320 | tf_op jit(solution)/shard_map/ppermute | solution.py:868
  602.7 9.1 %last_back.2 = (f32[256,1536]{1,0:T(8,128)}, bf16[256,1024]{1,0:T(8,128)(2,1)}, f32[1,1536]{1,0:T(1,128)}) custom-call(bf16[256,1536]{1,0:T(8,128)(2,1)} %get-tuple-element.218.dq_ref.refs_2_, bf16[2,256,512]{2,1,0:T(8,128)(2,1)} %add_convert_fusion.18.dkv_ref, f32[256,128]{1,0:T(8,128)} %get-tuple-element.395.cosine_ref, ...), custom_call_target="tpu_custom_call" | custom-call | flops 201326592 | bytes 1415577 | tf_op jit(solution)/shard_map/last_back/pallas_call | solution.py:303
  617.4 9.3 %collective-permute-done.20 = bf16[2,256,512]{2,1,0:T(8,128)(2,1)S(1)} collective-permute-done((bf16[2,256,512]{2,1,0:T(8,128)(2,1)S(1)}, bf16[2,256,512]{2,1,0:T(8,128)(2,1)S(1)}, u32[]{:S(2)}, u32[]{:S(2)}) %collective-permute-start.20) | collective-permute-done | bytes 524320 | tf_op jit(solution)/shard_map/ppermute | solution.py:868
  628.5 14.3 %collective-permute-done.22 = bf16[2,256,512]{2,1,0:T(8,128)(2,1)S(1)} collective-permute-done((bf16[2,256,512]{2,1,0:T(8,128)(2,1)S(1)}, bf16[2,256,512]{2,1,0:T(8,128)(2,1)S(1)}, u32[]{:S(2)}, u32[]{:S(2)}) %collective-permute-start.22) | collective-permute-done | bytes 524320 | tf_op jit(solution)/shard_map/ppermute | solution.py:868
  643.7 9.2 %last_back.3 = (f32[256,1536]{1,0:T(8,128)}, bf16[256,1024]{1,0:T(8,128)(2,1)}, f32[1,1536]{1,0:T(1,128)}) custom-call(bf16[256,1536]{1,0:T(8,128)(2,1)} %get-tuple-element.237.dq_ref.refs_3_, bf16[2,256,512]{2,1,0:T(8,128)(2,1)} %add_convert_fusion.15.dkv_ref, f32[256,128]{1,0:T(8,128)} %get-tuple-element.395.cosine_ref, ...), custom_call_target="tpu_custom_call" | custom-call | flops 201326592 | bytes 1415577 | tf_op jit(solution)/shard_map/last_back/pallas_call | solution.py:303
  657.1 13.5 %dense_grads.1 = (bf16[768,4224]{1,0:T(8,128)(2,1)}, bf16[768,4224]{1,0:T(8,128)(2,1)}) custom-call(s32[1]{0:T(128)} %bitcast.9.core_ref, bf16[512,1536]{1,0:T(8,128)(2,1)} %get-tuple-element.163.normed_ref.refs_0_.refs_1_, bf16[512,1536]{1,0:T(8,128)(2,1)} %get-tuple-element.163.normed_ref.refs_0_.refs_1_, ...), custom_call_target="tpu_custom_call" | custom-call | flops 664377728 | bytes 2477260 | tf_op jit(solution)/shard_map/dense_grads/pallas_call | solution.py:370
  681.5 12.6 %fold.1 = (bf16[1,384,2304]{2,1,0:T(8,128)(2,1)}, bf16[1,384,2304]{2,1,0:T(8,128)(2,1)}, bf16[1,384,1920]{2,1,0:T(8,128)(2,1)}, bf16[1,384,1920]{2,1,0:T(8,128)(2,1)}) custom-call(s32[2]{0:T(128)} %pad_add_fusion.place_ref, bf16[1,768,4224]{2,1,0:T(8,128)(2,1)} %bitcast.66, bf16[1,768,4224]{2,1,0:T(8,128)(2,1)} %bitcast.25.got_ref), custom_call_target="tpu_custom_call" | custom-call | flops 324403 | bytes 1946419 | tf_op jit(solution)/shard_map/fold/pallas_call | solution.py:793
  695.8 19.5 %collective-permute-done.25 = bf16[256,1536]{1,0:T(8,128)(2,1)S(1)} collective-permute-done((bf16[256,1536]{1,0:T(8,128)(2,1)S(1)}, bf16[256,1536]{1,0:T(8,128)(2,1)S(1)}, u32[]{:S(2)}, u32[]{:S(2)}) %collective-permute-start.25) | collective-permute-done | bytes 786464 | tf_op jit(solution)/shard_map/ppermute | solution.py:866
  715.6 14.3 %collective-permute-done.28.got_ref = bf16[1,384,1920]{2,1,0:T(8,128)(2,1)S(1)} collective-permute-done((bf16[1,384,1920]{2,1,0:T(8,128)(2,1)}, bf16[1,384,1920]{2,1,0:T(8,128)(2,1)S(1)}, u32[]{:S(2)}, u32[]{:S(2)}) %collective-permute-start.28) | collective-permute-done | bytes 1474592 | tf_op jit(solution)/shard_map/ppermute | solution.py:873
  747.8 14.1 %collective-permute-done.31 = bf16[1,192,1920]{2,1,0:T(8,128)(2,1)S(1)} collective-permute-done((bf16[1,192,1920]{2,1,0:T(8,128)(2,1)}, bf16[1,192,1920]{2,1,0:T(8,128)(2,1)S(1)}, u32[]{:S(2)}, u32[]{:S(2)}) %collective-permute-start.31) | collective-permute-done | bytes 737312 | tf_op jit(solution)/shard_map/ppermute | solution.py:873
  783.0 56.6 %all-reduce.3.cloned.1.call-done.sums_ref = bf16[192,4224]{1,0:T(8,128)(2,1)} async-done(((bf16[192,4224]{1,0:T(8,128)(2,1)}), bf16[192,4224]{1,0:T(8,128)(2,1)}) %all-reduce.3.cloned.1.call-update) | async-done | bytes 1622032 | tf_op jit(solution)/shard_map/psum | solution.py:1068
  (245 shorter events, 270.5 us)
Async XLA Ops:
  7.2 92.9 %all-gather.4.cloned.1.call-start = ((), (), s32[]{:S(2)}) async-start(), calls=%async_computation.4 | async-start | bytes 14598144 | tf_op jit(solution)/shard_map/all_gather | solution.py:870
  13.4 260.3 %all-gather.6.cloned.1.call-start = ((), (), s32[]{:S(2)}) async-start(), calls=%async_computation.5 | async-start | bytes 4259840 | tf_op jit(solution)/shard_map/all_gather | solution.py:870
  16.2 42.2 %collective-permute-start = (bf16[2,256,1664]{1,2,0:T(8,128)(2,1)S(1)}, bf16[2,256,1664]{1,2,0:T(8,128)(2,1)S(1)}, u32[]{:S(2)}, u32[]{:S(2)}) collective-permute-start(bf16[2,256,1664]{1,2,0:T(8,128)(2,1)S(1)} %maximum_maximum_fusion), channel_id=1, source_target_pairs={{0,1},{1,2},{2,3},{3,0},{4,5},{5,6},{6,7},{7,4},{8,9},{9,10},{10,1... | collective-permute-start | bytes 5111816 | tf_op jit(solution)/shard_map/ppermute | solution.py:866
  58.5 40.2 %collective-permute-start.1 = (bf16[2,256,1664]{1,2,0:T(8,128)(2,1)S(1)}, bf16[2,256,1664]{1,2,0:T(8,128)(2,1)S(1)}, u32[]{:S(2)}, u32[]{:S(2)}) collective-permute-start(bf16[2,256,1664]{1,2,0:T(8,128)(2,1)S(1)} %collective-permute-done), channel_id=1, source_target_pairs={{0,1},{1,2},{2,3},{3,0},{4,5},{5,6},{6,7},{7,4},{8,9},{9,10},{10,1... | collective-permute-start | bytes 5111816 | tf_op jit(solution)/shard_map/ppermute | solution.py:866
  100.0 21.3 %collective-permute-start.2 = (bf16[256,1664]{0,1:T(8,128)(2,1)}, bf16[256,1664]{0,1:T(8,128)(2,1)}, u32[]{:S(2)}, u32[]{:S(2)}) collective-permute-start(bf16[256,1664]{0,1:T(8,128)(2,1)} %get-tuple-element.381), channel_id=1, source_target_pairs={{0,1},{1,2},{2,3},{3,0},{4,5},{5,6},{6,7},{7,4},{8,9},{9,10},{10,1... | collective-permute-start | bytes 2555912 | tf_op jit(solution)/shard_map/ppermute | solution.py:866
  160.7 30.5 %collective-permute-start.8 = (bf16[256,1664]{0,1:T(8,128)(2,1)}, bf16[256,1664]{0,1:T(8,128)(2,1)S(1)}, u32[]{:S(2)}, u32[]{:S(2)}) collective-permute-start(bf16[256,1664]{0,1:T(8,128)(2,1)} %get-tuple-element.166), channel_id=1, source_target_pairs={{0,1},{1,2},{2,3},{3,0},{4,5},{5,6},{6,7},{7,4},{8,9},{9,10},{10,1... | collective-permute-start | bytes 2555912 | tf_op jit(solution)/shard_map/ppermute | solution.py:866
  173.4 23.4 %collective-permute-start.7 = (bf16[256,1024]{1,0:T(8,128)(2,1)S(1)}, bf16[256,1024]{1,0:T(8,128)(2,1)}, u32[]{:S(2)}, u32[]{:S(2)}) collective-permute-start(bf16[256,1024]{1,0:T(8,128)(2,1)S(1)} %collective-permute-done.6.refs_1_.refs_5_), channel_id=1, source_target_pairs={{0,1},{1,2},{2,3},{4,5},{5,6},{6,7},{8,9},{9,10},{10,11},{12,13},{... | collective-permute-start | bytes 1572872 | tf_op jit(solution)/shard_map/ppermute | solution.py:867
  203.7 140.9 %all-gather.8.cloned.1.call-start = ((), (), s32[]{:S(2)}) async-start(), calls=%async_computation.6 | async-start | bytes 4259840 | tf_op jit(solution)/shard_map/all_gather | solution.py:870
  208.4 28.6 %collective-permute-start.9 = (bf16[256,1024]{1,0:T(8,128)(2,1)}, bf16[256,1024]{1,0:T(8,128)(2,1)}, u32[]{:S(2)}, u32[]{:S(2)}) collective-permute-start(bf16[256,1024]{1,0:T(8,128)(2,1)} %collective-permute-done.7.refs_2_.refs_6_), channel_id=1, source_target_pairs={{0,1},{1,2},{2,3},{4,5},{5,6},{6,7},{8,9},{9,10},{10,11},{12,13},{... | collective-permute-start | bytes 1572872 | tf_op jit(solution)/shard_map/ppermute | solution.py:867
  251.4 158.9 %reduce-scatter.5.cloned.1.call-start = ((), (), s32[]{:S(2)}) async-start(), calls=%async_computation.7 | async-start | bytes 4259840 | tf_op jit(solution)/shard_map/reduce_scatter | solution.py:979
  326.4 232.5 %reduce-scatter.7.cloned.1.call-start = ((), (), s32[]{:S(2)}) async-start(), calls=%async_computation.8 | async-start | bytes 17694720 | tf_op jit(solution)/shard_map/reduce_scatter | solution.py:988
  410.3 269.8 %reduce-scatter.9.cloned.1.call-start = ((), (), s32[]{:S(2)}) async-start(), calls=%async_computation.9 | async-start | bytes 9830400 | tf_op jit(solution)/shard_map/reduce_scatter | solution.py:879
  418.9 29.8 %collective-permute-start.10 = (bf16[256,1664]{1,0:T(8,128)(2,1)S(1)}, bf16[256,1664]{1,0:T(8,128)(2,1)S(1)}, u32[]{:S(2)}, u32[]{:S(2)}) collective-permute-start(bf16[256,1664]{1,0:T(8,128)(2,1)S(1)} %constant_dynamic-slice_fusion.2), channel_id=1, source_target_pairs={{0,1},{1,2},{2,3},{3,0},{4,5},{5,6},{6,7},{7,4},{8,9},{9,10},{10,1... | collective-permute-start | bytes 2555912 | tf_op jit(solution)/shard_map/ppermute | solution.py:866
  448.7 23.9 %collective-permute-start.13 = (bf16[10,768,512]{2,1,0:T(8,128)(2,1)}, bf16[10,768,512]{2,1,0:T(8,128)(2,1)}, u32[]{:S(2)}, u32[]{:S(2)}) collective-permute-start(bf16[10,768,512]{2,1,0:T(8,128)(2,1)} %get-tuple-element.212), channel_id=1, source_target_pairs={{0,4},{4,0},{8,12},{12,8},{16,20},{20,16},{24,28},{28,24},{1,5},{5... | collective-permute-start | bytes 23592968 | tf_op jit(solution)/shard_map/ppermute | solution.py:871
  448.8 24.0 %collective-permute-start.14 = (bf16[10,768,512]{2,1,0:T(8,128)(2,1)}, bf16[10,768,512]{2,1,0:T(8,128)(2,1)}, u32[]{:S(2)}, u32[]{:S(2)}) collective-permute-start(bf16[10,768,512]{2,1,0:T(8,128)(2,1)} %get-tuple-element.213), channel_id=1, source_target_pairs={{0,4},{4,0},{8,12},{12,8},{16,20},{20,16},{24,28},{28,24},{1,5},{5... | collective-permute-start | bytes 23592968 | tf_op jit(solution)/shard_map/ppermute | solution.py:871
  449.5 23.1 %collective-permute-start.12 = (bf16[256,1664]{1,0:T(8,128)(2,1)S(1)}, bf16[256,1664]{1,0:T(8,128)(2,1)}, u32[]{:S(2)}, u32[]{:S(2)}) collective-permute-start(bf16[256,1664]{1,0:T(8,128)(2,1)S(1)} %add_convert_fusion.5), channel_id=1, source_target_pairs={{0,1},{1,2},{2,3},{3,0},{4,5},{5,6},{6,7},{7,4},{8,9},{9,10},{10,1... | collective-permute-start | bytes 2555912 | tf_op jit(solution)/shard_map/ppermute | solution.py:866
  484.0 281.1 %reduce-scatter.11.cloned.1.call-start = ((), (), s32[]{:S(2)}) async-start(), calls=%async_computation.10 | async-start | bytes 9830400 | tf_op jit(solution)/shard_map/reduce_scatter | solution.py:879
  486.3 34.2 %collective-permute-start.15 = (bf16[256,1664]{1,0:T(8,128)(2,1)}, bf16[256,1664]{1,0:T(8,128)(2,1)}, u32[]{:S(2)}, u32[]{:S(2)}) collective-permute-start(bf16[256,1664]{1,0:T(8,128)(2,1)} %add_convert_fusion.4), channel_id=1, source_target_pairs={{0,1},{1,2},{2,3},{3,0},{4,5},{5,6},{6,7},{7,4},{8,9},{9,10},{10,1... | collective-permute-start | bytes 2555912 | tf_op jit(solution)/shard_map/ppermute | solution.py:866
  490.5 41.1 %collective-permute-start.11 = (bf16[2,256,512]{2,1,0:T(8,128)(2,1)}, bf16[2,256,512]{2,1,0:T(8,128)(2,1)S(1)}, u32[]{:S(2)}, u32[]{:S(2)}) collective-permute-start(bf16[2,256,512]{2,1,0:T(8,128)(2,1)} %get-tuple-element.210), channel_id=1, source_target_pairs={{1,0},{2,1},{3,2},{5,4},{6,5},{7,6},{9,8},{10,9},{11,10},{13,12},{... | collective-permute-start | bytes 1572872 | tf_op jit(solution)/shard_map/ppermute | solution.py:868
  523.9 35.0 %collective-permute-start.17 = (bf16[256,1536]{1,0:T(8,128)(2,1)S(1)}, bf16[256,1536]{1,0:T(8,128)(2,1)}, u32[]{:S(2)}, u32[]{:S(2)}) collective-permute-start(bf16[256,1536]{1,0:T(8,128)(2,1)S(1)} %constant_dynamic-slice_fusion.1), channel_id=1, source_target_pairs={{0,1},{1,2},{2,3},{3,0},{4,5},{5,6},{6,7},{7,4},{8,9},{9,10},{10,1... | collective-permute-start | bytes 2359304 | tf_op jit(solution)/shard_map/ppermute | solution.py:866
  531.7 27.2 %collective-permute-start.16 = (bf16[2,256,512]{2,1,0:T(8,128)(2,1)S(1)}, bf16[2,256,512]{2,1,0:T(8,128)(2,1)}, u32[]{:S(2)}, u32[]{:S(2)}) collective-permute-start(bf16[2,256,512]{2,1,0:T(8,128)(2,1)S(1)} %add_convert_fusion.20), channel_id=1, source_target_pairs={{1,0},{2,1},{3,2},{5,4},{6,5},{7,6},{9,8},{10,9},{11,10},{13,12},{... | collective-permute-start | bytes 1572872 | tf_op jit(solution)/shard_map/ppermute | solution.py:868
  570.0 269.5 %all-reduce.3.cloned.1.call-start = ((), (), s32[]{:S(2)}) async-start(), calls=%async_computation.11 | async-start | bytes 3244032 | tf_op jit(solution)/shard_map/psum | solution.py:1068
  573.0 27.6 %collective-permute-start.18 = (bf16[2,256,512]{2,1,0:T(8,128)(2,1)}, bf16[2,256,512]{2,1,0:T(8,128)(2,1)S(1)}, u32[]{:S(2)}, u32[]{:S(2)}) collective-permute-start(bf16[2,256,512]{2,1,0:T(8,128)(2,1)} %get-tuple-element.233), channel_id=1, source_target_pairs={{1,0},{2,1},{3,2},{5,4},{6,5},{7,6},{9,8},{10,9},{11,10},{13,12},{... | collective-permute-start | bytes 1572872 | tf_op jit(solution)/shard_map/ppermute | solution.py:868
  575.7 41.8 %collective-permute-start.21 = (bf16[256,1536]{1,0:T(8,128)(2,1)S(1)}, bf16[256,1536]{1,0:T(8,128)(2,1)S(1)}, u32[]{:S(2)}, u32[]{:S(2)}) collective-permute-start(bf16[256,1536]{1,0:T(8,128)(2,1)S(1)} %add_convert_fusion.13), channel_id=1, source_target_pairs={{0,1},{1,2},{2,3},{3,0},{4,5},{5,6},{6,7},{7,4},{8,9},{9,10},{10,1... | collective-permute-start | bytes 2359304 | tf_op jit(solution)/shard_map/ppermute | solution.py:866
  600.7 26.1 %collective-permute-start.20 = (bf16[2,256,512]{2,1,0:T(8,128)(2,1)S(1)}, bf16[2,256,512]{2,1,0:T(8,128)(2,1)S(1)}, u32[]{:S(2)}, u32[]{:S(2)}) collective-permute-start(bf16[2,256,512]{2,1,0:T(8,128)(2,1)S(1)} %add_convert_fusion.17), channel_id=1, source_target_pairs={{1,0},{2,1},{3,2},{5,4},{6,5},{7,6},{9,8},{10,9},{11,10},{13,12},{... | collective-permute-start | bytes 1572872 | tf_op jit(solution)/shard_map/ppermute | solution.py:868
  671.8 22.3 %collective-permute-start.23 = (bf16[256,1536]{1,0:T(8,128)(2,1)}, bf16[256,1536]{1,0:T(8,128)(2,1)}, u32[]{:S(2)}, u32[]{:S(2)}) collective-permute-start(bf16[256,1536]{1,0:T(8,128)(2,1)} %add_convert_fusion.12), channel_id=1, source_target_pairs={{0,1},{1,2},{2,3},{3,0},{4,5},{5,6},{6,7},{7,4},{8,9},{9,10},{10,1... | collective-permute-start | bytes 2359304 | tf_op jit(solution)/shard_map/ppermute | solution.py:866
  694.1 21.2 %collective-permute-start.25 = (bf16[256,1536]{1,0:T(8,128)(2,1)S(1)}, bf16[256,1536]{1,0:T(8,128)(2,1)S(1)}, u32[]{:S(2)}, u32[]{:S(2)}) collective-permute-start(bf16[256,1536]{1,0:T(8,128)(2,1)S(1)} %constant_dynamic-slice_fusion), channel_id=1, source_target_pairs={{0,1},{1,2},{2,3},{3,0},{4,5},{5,6},{6,7},{7,4},{8,9},{9,10},{10,1... | collective-permute-start | bytes 2359304 | tf_op jit(solution)/shard_map/ppermute | solution.py:866
  694.6 41.4 %collective-permute-start.27 = (bf16[1,384,2304]{2,1,0:T(8,128)(2,1)}, bf16[1,384,2304]{2,1,0:T(8,128)(2,1)}, u32[]{:S(2)}, u32[]{:S(2)}) collective-permute-start(bf16[1,384,2304]{2,1,0:T(8,128)(2,1)} %get-tuple-element.273), channel_id=1, source_target_pairs={{0,8},{4,12},{8,0},{12,4},{16,24},{20,28},{24,16},{28,20},{1,9},{5... | collective-permute-start | bytes 5308424 | tf_op jit(solution)/shard_map/ppermute | solution.py:873
  695.8 34.1 %collective-permute-start.28 = (bf16[1,384,1920]{2,1,0:T(8,128)(2,1)}, bf16[1,384,1920]{2,1,0:T(8,128)(2,1)S(1)}, u32[]{:S(2)}, u32[]{:S(2)}) collective-permute-start(bf16[1,384,1920]{2,1,0:T(8,128)(2,1)} %get-tuple-element.275), channel_id=1, source_target_pairs={{0,16},{4,20},{8,24},{12,28},{16,0},{20,4},{24,8},{28,12},{1,17},{... | collective-permute-start | bytes 4423688 | tf_op jit(solution)/shard_map/ppermute | solution.py:873
  715.5 20.4 %collective-permute-start.26 = (bf16[256,1536]{1,0:T(8,128)(2,1)S(1)}, bf16[256,1536]{1,0:T(8,128)(2,1)}, u32[]{:S(2)}, u32[]{:S(2)}) collective-permute-start(bf16[256,1536]{1,0:T(8,128)(2,1)S(1)} %add_convert_fusion.9), channel_id=1, source_target_pairs={{0,1},{1,2},{2,3},{3,0},{4,5},{5,6},{6,7},{7,4},{8,9},{9,10},{10,1... | collective-permute-start | bytes 2359304 | tf_op jit(solution)/shard_map/ppermute | solution.py:866
  742.1 23.0 %collective-permute-start.30 = (bf16[1,192,2304]{2,1,0:T(8,128)(2,1)}, bf16[1,192,2304]{2,1,0:T(8,128)(2,1)}, u32[]{:S(2)}, u32[]{:S(2)}) collective-permute-start(bf16[1,192,2304]{2,1,0:T(8,128)(2,1)} %get-tuple-element.284), channel_id=1, source_target_pairs={{0,16},{4,20},{8,24},{12,28},{16,0},{20,4},{24,8},{28,12},{1,17},{... | collective-permute-start | bytes 2654216 | tf_op jit(solution)/shard_map/ppermute | solution.py:873
  744.9 19.3 %collective-permute-start.29 = (bf16[256,1536]{1,0:T(8,128)(2,1)S(1)}, bf16[256,1536]{1,0:T(8,128)(2,1)S(1)}, u32[]{:S(2)}, u32[]{:S(2)}) collective-permute-start(bf16[256,1536]{1,0:T(8,128)(2,1)S(1)} %add_convert_fusion.8), channel_id=1, source_target_pairs={{0,1},{1,2},{2,3},{3,0},{4,5},{5,6},{6,7},{7,4},{8,9},{9,10},{10,1... | collective-permute-start | bytes 2359304 | tf_op jit(solution)/shard_map/ppermute | solution.py:866
  (50 other events, 650.2 us)
Sparse Core Ops, SparseCore 0:
  13.5 76.4 all-gather.3
  203.8 69.9 all-gather.5
  275.9 68.5 all-gather.7
  347.2 62.9 reduce-scatter.4
  413.6 109.3 reduce-scatter.6
  525.8 83.3 reduce-scatter.8
  612.2 83.3 reduce-scatter.10
  769.7 69.7 all-reduce.2

commit v5 on v4

--- a/solution.py
+++ b/solution.py
@@ -890,12 +890,19 @@
     def halve_first(keep, got, tile=None):
         return send_first(fold_first(keep, got, tile))
 
-    def halve_second(parts):
+    def fold_second(parts):
         if not square:
             return parts
-        one, one_sent = fold_again(places[1:], *parts[:2])
-        two, two_sent = fold_again(places[:1], *parts[2:])
+        return [*fold_again(places[1:], *parts[:2]), *fold_again(places[:1], *parts[2:])]
+
+    def send_second(parts):
+        if not square:
+            return parts
+        one, one_sent, two, two_sent = parts
         return [one, across(one_sent, 4), two, across(two_sent, 2)]
+
+    def halve_second(parts):
+        return send_second(fold_second(parts))
 
     def halve_last(parts, axis, dtype):
         if not square:
@@ -1010,6 +1017,7 @@
     dx_held, got_gate, got_up, dq_one = together(dx_held, got_gate, got_up, dq_one)
     dx_held = ring(add(dx_held, ring_block(dx_two, count - 2)))
     up_half = add(ups[2], got_up)
+    dx_held, up_half = together(dx_held, up_half)
     up_grad = share(up_half)
     dx_home.append(add(dx_held, ring_block(dx_two, count - 1)))
     held = ring(ring_block(after(mixture_one, dx_held), 0))
@@ -1022,49 +1030,56 @@
     for piece in far_one[2:-1]:
         back_one = earlier(add(back_one, piece))
     back_two = earlier(far_two[0])
-    gate_half = add(after(ups[0], dq_two), got_gate)
-    gate_grad = share(gate_half)
-    held = ring(add(held, ring_block(mixture_one, 1)))
+    gate_parts = fold_first(after(ups[0], dq_two), got_gate)
+    back_two, back_one, *gate_parts = together(back_two, back_one, *gate_parts)
+    gate_sums = send_first(gate_parts)
     back_one = add(back_one, far_one[-1])
+    back_two = earlier(add(back_two, far_two[1]))
 
     def back_last(m, dq, dkv, dmid):
         return last_back(
             dq, dkv, cosine, sine, weights, weights, tokens[m], scale_one[m * BLOCK : (m + 1) * BLOCK], gain_one, dmid
         )
 
-    back_two, back_one = together(back_two, back_one, gate_half)[:2]
-    back_two = earlier(add(back_two, far_two[1]))
     grad_x_one, dkv_one, dgain_one = back_last(0, dq_one, back_one, first[0])
-    back_two, dkv_one, held = together(back_two, dkv_one, held)
+    back_two, dkv_one = together(back_two, dkv_one)
     for piece in far_two[2:-1]:
         back_two = earlier(add(back_two, piece))
+    mixture_two = combine(slot_rows[1], after(ys_two, dkv_one))
+    back_two, mixture_two = together(back_two, mixture_two)
     back_two = add(back_two, far_two[-1])
     grad_x_two, dkv_two, dgain_two = back_last(1, dq_two, back_two, second[0])
+    held = ring(add(after(held, mixture_two), ring_block(mixture_one, 1)))
+
     gain_rows = jnp.concatenate([dgain_one + dgain_two, first[4] + second[4]], axis=0)
     gain_columns = jnp.pad(gain_rows.T, ((0, 0), (EXPERTS, LANES - EXPERTS - 2)))
     keep, send = dense_grads(
         core, features // dp, [normed] * micros, [dq_one, dq_two], [dkv_one, dkv_two], [k[1] for k in mids],
         [first[3], second[3]], [h[1] for h in heads], [first[1], second[1]], gain_columns,
     )
+    held, keep, send, *gate_sums = together(held, keep, send, *gate_sums)
     for step in range(2, count - 1):
-        held = ring(add(after(held, keep), ring_block(mixture_one, step)))
+        held = ring(add(held, ring_block(mixture_one, step)))
     got = swap(send)
-    mixture_two = combine(slot_rows[1], after(ys_two, keep))
-    got, mixture_two, up_grad = together(got, mixture_two, up_grad)
+    got, up_grad = together(got, up_grad)
     dense_sums = halve_first(keep[None], got[None], 3 * LANES)
-    held, mixture_two = together(held, mixture_two, dense_sums[0])[:2]
+    held = together(held, dense_sums[0])[0]
     mixtures = [add(held, ring_block(mixture_one, count - 1))]
     held = ring(ring_block(mixture_two, 0))
     held = ring(add(held, ring_block(mixture_two, 1)))
-    held, *dense_sums = together(held, *dense_sums)
-    dense_sums = halve_second(dense_sums)
+    gate_parts = fold_second([after(a, dense_sums[0]) for a in gate_sums])
+    each = len(gate_parts)
+    held, *rest = together(held, *gate_parts, *dense_sums)
+    gate_parts, dense_sums = rest[:each], halve_second(rest[each:])
     held = after(held, *dense_sums[::2])
     for step in range(2, count - 1):
         held = ring(add(held, ring_block(mixture_two, step)))
-    held, gate_grad, *dense_sums = together(held, gate_grad, *dense_sums)
+    held, *dense_sums = together(held, *dense_sums)
     mixtures.append(add(held, ring_block(mixture_two, count - 1)))
     dense_sum = halve_last(dense_sums, 2, BF)[0]
-    gate_grad, up_grad, down_grad = gate_grad.astype(F32), up_grad.astype(F32), down_grad.astype(F32)
+    gate_sums = send_second(together(*gate_parts, dense_sum)[:-1])
+    gate_grad = halve_last(gate_sums, 0, F32)
+    up_grad, down_grad = up_grad.astype(F32), down_grad.astype(F32)
     dense = split_dense(lax.psum(dense_sum, "expert"))
     query, key, value, router, gain_columns, out = dense
     mixed = [(mids[m][0] + mixtures[m].astype(F32)).astype(BF) for m in range(micros)]

time: 865 us -> 840 us (0.971)
  waiting for transfers between devices: 368 us -> 322 us
  Pallas kernels: 316 us -> 340 us
  other arithmetic: 60.5 us -> 48.9 us
    ppermute x13, waiting for transfers between devices: 154 us -> 122 us  [local(): ring = lambda a: lax.ppermute(a, 'expert', around)]
    ppermute x6, waiting for transfers between devices: 58.3 us -> 36.1 us  [local(): earlier = lambda a: lax.ppermute(a, 'expert', downward)]
    ppermute x4 -> x8, waiting for transfers between devices: 28.4 us -> 41.8 us  [local(): lax.ppermute(a, 'dp', [(i, i ^ bit) for i in range(dp)])]
    pallas_call x1 -> x2, Pallas kernels: 12.6 us -> 24.9 us  [fold(): pl.pallas_call(partial(fold_kernel, cut, step), grid_spec=pltpu.PrefetchS...]
    psum x1, waiting for transfers between devices: 56.6 us -> 45.1 us  [local(): dense = split_dense(lax.psum(dense_sum, 'expert'))]
    pallas_call x2 -> x4, Pallas kernels: 6.12 us -> 15.7 us  [fold_again(): pl.pallas_call(partial(fold_again_kernel, step), grid_spec=pltpu.Prefetch...]
    convert_element_type x15 -> x14, other arithmetic: 34.7 us -> 25.1 us  [local(): add = lambda a, b: (a.astype(F32) + b.astype(F32)).astype(BF)]
  transfers between devices with their start and end apart: 40 -> 43, of which waited for: 28 -> 28; matrix products, arithmetic and copies ran while one was open for 10% -> 9% of each run, Pallas kernels for 36% -> 40%
where the time goes in v5:
time: 840 us; the launch traced here: 828 us
  Pallas kernels  340 us (40%)
  waiting for transfers between devices  322 us (38%)
  starting transfers between devices  61.4 us (7%)
  other arithmetic  48.9 us (6%)
  local copies, waits for them, and re-layouts  41.1 us (5%)
  between operations  15.4 us (2%)
    ppermute x13, waiting for transfers between devices, local(): ring = lambda a: lax.ppermute(a, 'expert', around)  122 us
    pallas_call x2, Pallas kernels, expert_pass(): pl.pallas_call(expert_kernel, grid_spec=pltpu.PrefetchScalarGridSpec(num_...  76.3 us
    pallas_call x2, Pallas kernels, weight_pass(): pl.pallas_call(partial(weight_kernel, count, products, step), grid_spec=p...  47.6 us
    psum x1, waiting for transfers between devices, local(): dense = split_dense(lax.psum(dense_sum, 'expert'))  45.1 us
    ppermute x8, waiting for transfers between devices, local(): lax.ppermute(a, 'dp', [(i, i ^ bit) for i in range(dp)])  41.8 us
    ppermute x6, waiting for transfers between devices, local(): earlier = lambda a: lax.ppermute(a, 'expert', downward)  36.1 us
    ppermute x6, waiting for transfers between devices, local(): later = lambda a: lax.ppermute(a, 'expert', upward)  34.1 us
    all_gather x3, waiting for transfers between devices, local(): every = lambda a, axis: lax.all_gather(a, axis, axis=0, tiled=True)  32.9 us
  transfers between devices with their start and end apart: 43, of which 28 were waited for; matrix products, arithmetic and copies ran while one was open for 9% of the time, Pallas kernels for 40%

profile of v5, /device:TPU:0, one launch (start us, length us, event | category | flops | bytes accessed | tf_op | source)
XLA Modules:
  0.0 828.4 jit_solution(10276028820473064821)
XLA Ops:
  19.3 39.2 %collective-permute-done = bf16[2,256,1664]{1,2,0:T(8,128)(2,1)S(1)} collective-permute-done((bf16[2,256,1664]{1,2,0:T(8,128)(2,1)S(1)}, bf16[2,256,1664]{1,2,0:T(8,128)(2,1)S(1)}, u32[]{:S(2)}, u32[]{:S(2)}) %collective-permute-start) | collective-permute-done | bytes 1703968 | tf_op jit(solution)/shard_map/ppermute | solution.py:866
  60.1 38.6 %collective-permute-done.1 = bf16[2,256,1664]{1,2,0:T(8,128)(2,1)S(1)} collective-permute-done((bf16[2,256,1664]{1,2,0:T(8,128)(2,1)S(1)}, bf16[2,256,1664]{1,2,0:T(8,128)(2,1)S(1)}, u32[]{:S(2)}, u32[]{:S(2)}) %collective-permute-start.1) | collective-permute-done | bytes 1703968 | tf_op jit(solution)/shard_map/ppermute | solution.py:866
  110.4 11.1 %collective-permute-done.2 = bf16[256,1664]{0,1:T(8,128)(2,1)} collective-permute-done((bf16[256,1664]{0,1:T(8,128)(2,1)}, bf16[256,1664]{0,1:T(8,128)(2,1)}, u32[]{:S(2)}, u32[]{:S(2)}) %collective-permute-start.2) | collective-permute-done | bytes 852000 | tf_op jit(solution)/shard_map/ppermute | solution.py:866
  122.8 9.3 %collective-permute-done.3.refs_1_.refs_5_ = bf16[256,1024]{1,0:T(8,128)(2,1)S(1)} collective-permute-done((bf16[256,1024]{1,0:T(8,128)(2,1)}, bf16[256,1024]{1,0:T(8,128)(2,1)S(1)}, u32[]{:S(2)}, u32[]{:S(2)}) %collective-permute-start.3) | collective-permute-done | bytes 524320 | tf_op jit(solution)/shard_map/ppermute | solution.py:867
  136.4 8.1 collective-permute-done.4.refs_2_.refs_6_
  148.9 7.5 collective-permute-done.5.refs_3_.refs_7_
  161.9 7.8 project.3
  251.7 22.1 %all-gather.6.cloned.1.call-done.rows_ref = bf16[1024,1664]{1,0:T(8,128)(2,1)} async-done(((bf16[256,1664]{1,0:T(8,128)(2,1)}), bf16[1024,1664]{1,0:T(8,128)(2,1)}) %all-gather.6.cloned.1.call-update) | async-done | bytes 3407888 | tf_op jit(solution)/shard_map/all_gather | solution.py:870
  280.9 38.1 %experts.2 = (bf16[10,256,1536]{2,1,0:T(8,128)(2,1)}, bf16[10,256,1664]{2,1,0:T(8,128)(2,1)}, bf16[10,256,1536]{2,1,0:T(8,128)(2,1)}, bf16[10,256,512]{2,1,0:T(8...) custom-call(s32[1]{0:T(128)} %bitcast.10.rank_ref, ...), custom_call_target="tpu_custom_call" | custom-call | flops 2415919104 | bytes 8650752 | tf_op jit(solution)/shard_map/experts/pallas_call | solution.py:663
  333.9 10.8 %all-gather.8.cloned.1.call-done.rows_ref = bf16[1024,1664]{1,0:T(8,128)(2,1)} async-done(((bf16[256,1664]{1,0:T(8,128)(2,1)}), bf16[1024,1664]{1,0:T(8,128)(2,1)}) %all-gather.8.cloned.1.call-update) | async-done | bytes 3407888 | tf_op jit(solution)/shard_map/all_gather | solution.py:870
  351.7 38.2 %experts.3 = (bf16[10,256,1536]{2,1,0:T(8,128)(2,1)}, bf16[10,256,1664]{2,1,0:T(8,128)(2,1)}, bf16[10,256,1536]{2,1,0:T(8,128)(2,1)}, bf16[10,256,512]{2,1,0:T(8...) custom-call(s32[1]{0:T(128)} %bitcast.10.rank_ref, ...), custom_call_target="tpu_custom_call" | custom-call | flops 2415919104 | bytes 8650752 | tf_op jit(solution)/shard_map/experts/pallas_call | solution.py:663
  390.0 18.9 %expert_weights.2 = bf16[10,512,1536]{2,1,0:T(8,128)(2,1)} custom-call(s32[1]{0:T(128)} %bitcast.9.core_ref, bf16[10,256,512]{2,1,0:T(8,128)(2,1)} %get-tuple-element.208.refs_0_, bf16[10,256,512]{2,1,0:T(8,128)(2,1)} %get-tuple-element.218.refs_1_, bf16[10,256,1536]{2,1,0:T(8,128)(2,1)} %get-tuple-element.219.refs_2_, ...), custom_call_target="tpu_custom_call" | custom-call | flops 805306368 | bytes 3670016 | tf_op jit(solution)/shard_map/expert_weights/pallas_call | solution.py:708
  420.3 28.7 %expert_weights.3 = (bf16[10,768,512]{2,1,0:T(8,128)(2,1)}, bf16[10,768,512]{2,1,0:T(8,128)(2,1)}, bf16[10,768,512]{2,1,0:T(8,128)(2,1)}, bf16[10,768,512]{2,1,0:T(8,128)(2,1)}) custom-call(s32[1]{0:T(128)} %bitcast.9.core_ref, bf16[10,256,1664]{2,1,0:T(8,128)(2,1)} %dispatch.4.x_ref.refs_0_, bf16[10,256,1664]{2,1,0:T(8,128)(2,1)} %dispatch.7.x_ref.refs_1_, ...), custom_call_target="tpu_custom_call" | custom-call | flops 1610612736 | bytes 5767168 | tf_op jit(solution)/shard_map/expert_weights/pallas_call | solution.py:708
  453.3 7.5 home_back.2
  460.9 11.6 %attend_back.2 = (bf16[256,1536]{1,0:T(8,128)(2,1)}, bf16[2,256,512]{2,1,0:T(8,128)(2,1)}, bf16[2,256,512]{2,1,0:T(8,128)(2,1)}, bf16[2,256,512]{2,1,0:T(8,128)(2,1)}, bf16[2,256,512]{2,1,0:T(8,128)(2,1)}) custom-call(s32[1]{0:T(128)} %bitcast.6.place_ref, bf16[256,1536]{1,0:T(8,128)(2,1)} %get-tuple-element.198.q_ref, ...), custom_call_target="tpu_custom_call" | custom-call | flops 1610612736 | bytes 550502 | tf_op jit(solution)/shard_map/attend_back/pallas_call | solution.py:526
  478.4 11.2 %add_convert_fusion = bf16[10,768,512]{2,1,0:T(8,128)(2,1)} fusion(bf16[10,768,512]{2,1,0:T(8,128)(2,1)} %collective-permute-done.14, bf16[10,768,512]{2,1,0:T(8,128)(2,1)} %get-tuple-element.247), kind=kLoop, calls=%fused_computation | loop fusion | flops 15728640 | bytes 23592960 | tf_op jit(solution)/shard_map/convert_element_type | solution.py:869
  489.6 17.8 %collective-permute-done.15 = bf16[256,1664]{1,0:T(8,128)(2,1)} collective-permute-done((bf16[256,1664]{1,0:T(8,128)(2,1)}, bf16[256,1664]{1,0:T(8,128)(2,1)}, u32[]{:S(2)}, u32[]{:S(2)}) %collective-permute-start.15) | collective-permute-done | bytes 852000 | tf_op jit(solution)/shard_map/ppermute | solution.py:866
  515.0 7.5 home_back.3
  522.4 17.5 %collective-permute-done.11 = bf16[2,256,512]{2,1,0:T(8,128)(2,1)S(1)} collective-permute-done((bf16[2,256,512]{2,1,0:T(8,128)(2,1)}, bf16[2,256,512]{2,1,0:T(8,128)(2,1)S(1)}, u32[]{:S(2)}, u32[]{:S(2)}) %collective-permute-start.11) | collective-permute-done | bytes 524320 | tf_op jit(solution)/shard_map/ppermute | solution.py:868
  541.6 11.7 %attend_back.3 = (bf16[256,1536]{1,0:T(8,128)(2,1)}, bf16[2,256,512]{2,1,0:T(8,128)(2,1)}, bf16[2,256,512]{2,1,0:T(8,128)(2,1)}, bf16[2,256,512]{2,1,0:T(8,128)(2,1)}, bf16[2,256,512]{2,1,0:T(8,128)(2,1)}) custom-call(s32[1]{0:T(128)} %bitcast.6.place_ref, bf16[256,1536]{1,0:T(8,128)(2,1)} %get-tuple-element.209.q_ref, ...), custom_call_target="tpu_custom_call" | custom-call | flops 1610612736 | bytes 550502 | tf_op jit(solution)/shard_map/attend_back/pallas_call | solution.py:526
  556.7 12.6 %fold.2 = (bf16[5,384,512]{2,1,0:T(8,128)(2,1)}, bf16[5,384,512]{2,1,0:T(8,128)(2,1)}, bf16[5,384,512]{2,1,0:T(8,128)(2,1)}, bf16[5,384,512]{2,1,0:T(8,128)(2,1)}) custom-call(s32[2]{0:T(128)} %pad_add_fusion.place_ref, bf16[10,768,512]{2,1,0:T(8,128)(2,1)} %get-tuple-element.271.keep_ref, bf16[10,768,512]{2,1,0:T(8,128)(2,1)} %collective-permute-done.13.got_ref), custom_call_target="tpu_custom_call" | custom-call | flops 393216 | bytes 2359296 | tf_op jit(solution)/shard_map/fold/pallas_call | solution.py:793
  571.1 9.5 %collective-permute-done.19 = bf16[2,256,512]{2,1,0:T(8,128)(2,1)S(1)} collective-permute-done((bf16[2,256,512]{2,1,0:T(8,128)(2,1)S(1)}, bf16[2,256,512]{2,1,0:T(8,128)(2,1)S(1)}, u32[]{:S(2)}, u32[]{:S(2)}) %collective-permute-start.19) | collective-permute-done | bytes 524320 | tf_op jit(solution)/shard_map/ppermute | solution.py:868
  586.8 10.1 %last_back.2 = (f32[256,1536]{1,0:T(8,128)}, bf16[256,1024]{1,0:T(8,128)(2,1)}, f32[1,1536]{1,0:T(1,128)}) custom-call(bf16[256,1536]{1,0:T(8,128)(2,1)} %get-tuple-element.251.dq_ref.refs_2_, bf16[2,256,512]{2,1,0:T(8,128)(2,1)} %add_convert_fusion.16.dkv_ref, f32[256,128]{1,0:T(8,128)} %get-tuple-element.457.cosine_ref, ...), custom_call_target="tpu_custom_call" | custom-call | flops 201326592 | bytes 1415577 | tf_op jit(solution)/shard_map/last_back/pallas_call | solution.py:303
  616.9 8.9 %last_back.3 = (f32[256,1536]{1,0:T(8,128)}, bf16[256,1024]{1,0:T(8,128)(2,1)}, f32[1,1536]{1,0:T(1,128)}) custom-call(bf16[256,1536]{1,0:T(8,128)(2,1)} %get-tuple-element.270.dq_ref.refs_3_, bf16[2,256,512]{2,1,0:T(8,128)(2,1)} %add_convert_fusion.14.dkv_ref, f32[256,128]{1,0:T(8,128)} %get-tuple-element.457.cosine_ref, ...), custom_call_target="tpu_custom_call" | custom-call | flops 201326592 | bytes 1415577 | tf_op jit(solution)/shard_map/last_back/pallas_call | solution.py:303
  630.0 13.4 %dense_grads.1 = (bf16[768,4224]{1,0:T(8,128)(2,1)}, bf16[768,4224]{1,0:T(8,128)(2,1)}) custom-call(s32[1]{0:T(128)} %bitcast.9.core_ref, bf16[512,1536]{1,0:T(8,128)(2,1)} %get-tuple-element.194.normed_ref.refs_0_.refs_1_, bf16[512,1536]{1,0:T(8,128)(2,1)} %get-tuple-element.194.normed_ref.refs_0_.refs_1_, ...), custom_call_target="tpu_custom_call" | custom-call | flops 664377728 | bytes 2477260 | tf_op jit(solution)/shard_map/dense_grads/pallas_call | solution.py:370
  646.2 8.1 collective-permute-done.26
  654.2 12.3 %fold.3 = (bf16[1,384,2304]{2,1,0:T(8,128)(2,1)}, bf16[1,384,2304]{2,1,0:T(8,128)(2,1)}, bf16[1,384,1920]{2,1,0:T(8,128)(2,1)}, bf16[1,384,1920]{2,1,0:T(8,128)(2,1)}) custom-call(s32[2]{0:T(128)} %pad_add_fusion.place_ref, bf16[1,768,4224]{2,1,0:T(8,128)(2,1)} %bitcast.66, bf16[1,768,4224]{2,1,0:T(8,128)(2,1)} %bitcast.25.got_ref), custom_call_target="tpu_custom_call" | custom-call | flops 324403 | bytes 1946419 | tf_op jit(solution)/shard_map/fold/pallas_call | solution.py:793
  683.7 10.2 %collective-permute-done.28 = bf16[256,1536]{1,0:T(8,128)(2,1)} collective-permute-done((bf16[256,1536]{1,0:T(8,128)(2,1)}, bf16[256,1536]{1,0:T(8,128)(2,1)}, u32[]{:S(2)}, u32[]{:S(2)}) %collective-permute-start.28) | collective-permute-done | bytes 786464 | tf_op jit(solution)/shard_map/ppermute | solution.py:866
  693.9 8.4 %collective-permute-done.30.got_ref = bf16[1,384,1920]{2,1,0:T(8,128)(2,1)S(1)} collective-permute-done((bf16[1,384,1920]{2,1,0:T(8,128)(2,1)}, bf16[1,384,1920]{2,1,0:T(8,128)(2,1)S(1)}, u32[]{:S(2)}, u32[]{:S(2)}) %collective-permute-start.30) | collective-permute-done | bytes 1474592 | tf_op jit(solution)/shard_map/ppermute | solution.py:873
  722.5 11.9 %collective-permute-done.33 = bf16[1,192,1920]{2,1,0:T(8,128)(2,1)S(1)} collective-permute-done((bf16[1,192,1920]{2,1,0:T(8,128)(2,1)}, bf16[1,192,1920]{2,1,0:T(8,128)(2,1)S(1)}, u32[]{:S(2)}, u32[]{:S(2)}) %collective-permute-start.33) | collective-permute-done | bytes 737312 | tf_op jit(solution)/shard_map/ppermute | solution.py:873
  749.1 11.9 %collective-permute-done.34 = bf16[5,192,512]{2,1,0:T(8,128)(2,1)} collective-permute-done((bf16[5,192,512]{2,1,0:T(8,128)(2,1)}, bf16[5,192,512]{2,1,0:T(8,128)(2,1)}, u32[]{:S(2)}, u32[]{:S(2)}) %collective-permute-start.34) | collective-permute-done | bytes 983072 | tf_op jit(solution)/shard_map/ppermute | solution.py:873
  769.6 45.1 %all-reduce.3.cloned.1.call-done.sums_ref = bf16[192,4224]{1,0:T(8,128)(2,1)} async-done(((bf16[192,4224]{1,0:T(8,128)(2,1)}), bf16[192,4224]{1,0:T(8,128)(2,1)}) %all-reduce.3.cloned.1.call-update) | async-done | bytes 1622032 | tf_op jit(solution)/shard_map/psum | solution.py:1083
  (260 shorter events, 287.5 us)
Async XLA Ops:
  7.2 93.0 %all-gather.4.cloned.1.call-start = ((), (), s32[]{:S(2)}) async-start(), calls=%async_computation.3 | async-start | bytes 14598144 | tf_op jit(solution)/shard_map/all_gather | solution.py:870
  13.4 260.4 %all-gather.6.cloned.1.call-start = ((), (), s32[]{:S(2)}) async-start(), calls=%async_computation.4 | async-start | bytes 4259840 | tf_op jit(solution)/shard_map/all_gather | solution.py:870
  16.2 42.2 %collective-permute-start = (bf16[2,256,1664]{1,2,0:T(8,128)(2,1)S(1)}, bf16[2,256,1664]{1,2,0:T(8,128)(2,1)S(1)}, u32[]{:S(2)}, u32[]{:S(2)}) collective-permute-start(bf16[2,256,1664]{1,2,0:T(8,128)(2,1)S(1)} %maximum_maximum_fusion), channel_id=1, source_target_pairs={{0,1},{1,2},{2,3},{3,0},{4,5},{5,6},{6,7},{7,4},{8,9},{9,10},{10,1... | collective-permute-start | bytes 5111816 | tf_op jit(solution)/shard_map/ppermute | solution.py:866
  58.5 40.2 %collective-permute-start.1 = (bf16[2,256,1664]{1,2,0:T(8,128)(2,1)S(1)}, bf16[2,256,1664]{1,2,0:T(8,128)(2,1)S(1)}, u32[]{:S(2)}, u32[]{:S(2)}) collective-permute-start(bf16[2,256,1664]{1,2,0:T(8,128)(2,1)S(1)} %collective-permute-done), channel_id=1, source_target_pairs={{0,1},{1,2},{2,3},{3,0},{4,5},{5,6},{6,7},{7,4},{8,9},{9,10},{10,1... | collective-permute-start | bytes 5111816 | tf_op jit(solution)/shard_map/ppermute | solution.py:866
  100.1 21.3 %collective-permute-start.2 = (bf16[256,1664]{0,1:T(8,128)(2,1)}, bf16[256,1664]{0,1:T(8,128)(2,1)}, u32[]{:S(2)}, u32[]{:S(2)}) collective-permute-start(bf16[256,1664]{0,1:T(8,128)(2,1)} %get-tuple-element.443), channel_id=1, source_target_pairs={{0,1},{1,2},{2,3},{3,0},{4,5},{5,6},{6,7},{7,4},{8,9},{9,10},{10,1... | collective-permute-start | bytes 2555912 | tf_op jit(solution)/shard_map/ppermute | solution.py:866
  160.8 30.5 %collective-permute-start.8 = (bf16[256,1664]{0,1:T(8,128)(2,1)}, bf16[256,1664]{0,1:T(8,128)(2,1)S(1)}, u32[]{:S(2)}, u32[]{:S(2)}) collective-permute-start(bf16[256,1664]{0,1:T(8,128)(2,1)} %get-tuple-element.197), channel_id=1, source_target_pairs={{0,1},{1,2},{2,3},{3,0},{4,5},{5,6},{6,7},{7,4},{8,9},{9,10},{10,1... | collective-permute-start | bytes 2555912 | tf_op jit(solution)/shard_map/ppermute | solution.py:866
  173.5 23.4 %collective-permute-start.7 = (bf16[256,1024]{1,0:T(8,128)(2,1)S(1)}, bf16[256,1024]{1,0:T(8,128)(2,1)}, u32[]{:S(2)}, u32[]{:S(2)}) collective-permute-start(bf16[256,1024]{1,0:T(8,128)(2,1)S(1)} %collective-permute-done.6.refs_1_.refs_5_), channel_id=1, source_target_pairs={{0,1},{1,2},{2,3},{4,5},{5,6},{6,7},{8,9},{9,10},{10,11},{12,13},{... | collective-permute-start | bytes 1572872 | tf_op jit(solution)/shard_map/ppermute | solution.py:867
  203.8 140.9 %all-gather.8.cloned.1.call-start = ((), (), s32[]{:S(2)}) async-start(), calls=%async_computation.5 | async-start | bytes 4259840 | tf_op jit(solution)/shard_map/all_gather | solution.py:870
  208.6 28.8 %collective-permute-start.9 = (bf16[256,1024]{1,0:T(8,128)(2,1)}, bf16[256,1024]{1,0:T(8,128)(2,1)}, u32[]{:S(2)}, u32[]{:S(2)}) collective-permute-start(bf16[256,1024]{1,0:T(8,128)(2,1)} %collective-permute-done.7.refs_2_.refs_6_), channel_id=1, source_target_pairs={{0,1},{1,2},{2,3},{4,5},{5,6},{6,7},{8,9},{9,10},{10,11},{12,13},{... | collective-permute-start | bytes 1572872 | tf_op jit(solution)/shard_map/ppermute | solution.py:867
  251.7 158.7 %reduce-scatter.4.cloned.1.call-start = ((), (), s32[]{:S(2)}) async-start(), calls=%async_computation.6 | async-start | bytes 4259840 | tf_op jit(solution)/shard_map/reduce_scatter | solution.py:986
  326.5 226.9 %reduce-scatter.6.cloned.1.call-start = ((), (), s32[]{:S(2)}) async-start(), calls=%async_computation.7 | async-start | bytes 17694720 | tf_op jit(solution)/shard_map/reduce_scatter | solution.py:995
  410.4 235.8 %reduce-scatter.8.cloned.1.call-start = ((), (), s32[]{:S(2)}) async-start(), calls=%async_computation.8 | async-start | bytes 9830400 | tf_op jit(solution)/shard_map/reduce_scatter | solution.py:879
  419.1 29.9 %collective-permute-start.10 = (bf16[256,1664]{1,0:T(8,128)(2,1)S(1)}, bf16[256,1664]{1,0:T(8,128)(2,1)S(1)}, u32[]{:S(2)}, u32[]{:S(2)}) collective-permute-start(bf16[256,1664]{1,0:T(8,128)(2,1)S(1)} %constant_dynamic-slice_fusion.2), channel_id=1, source_target_pairs={{0,1},{1,2},{2,3},{3,0},{4,5},{5,6},{6,7},{7,4},{8,9},{9,10},{10,1... | collective-permute-start | bytes 2555912 | tf_op jit(solution)/shard_map/ppermute | solution.py:866
  449.0 23.7 %collective-permute-start.13 = (bf16[10,768,512]{2,1,0:T(8,128)(2,1)}, bf16[10,768,512]{2,1,0:T(8,128)(2,1)}, u32[]{:S(2)}, u32[]{:S(2)}) collective-permute-start(bf16[10,768,512]{2,1,0:T(8,128)(2,1)} %get-tuple-element.243), channel_id=1, source_target_pairs={{0,4},{4,0},{8,12},{12,8},{16,20},{20,16},{24,28},{28,24},{1,5},{5... | collective-permute-start | bytes 23592968 | tf_op jit(solution)/shard_map/ppermute | solution.py:871
  449.0 24.0 %collective-permute-start.14 = (bf16[10,768,512]{2,1,0:T(8,128)(2,1)}, bf16[10,768,512]{2,1,0:T(8,128)(2,1)}, u32[]{:S(2)}, u32[]{:S(2)}) collective-permute-start(bf16[10,768,512]{2,1,0:T(8,128)(2,1)} %get-tuple-element.244), channel_id=1, source_target_pairs={{0,4},{4,0},{8,12},{12,8},{16,20},{20,16},{24,28},{28,24},{1,5},{5... | collective-permute-start | bytes 23592968 | tf_op jit(solution)/shard_map/ppermute | solution.py:871
  449.8 23.0 %collective-permute-start.12 = (bf16[256,1664]{1,0:T(8,128)(2,1)S(1)}, bf16[256,1664]{1,0:T(8,128)(2,1)S(1)}, u32[]{:S(2)}, u32[]{:S(2)}) collective-permute-start(bf16[256,1664]{1,0:T(8,128)(2,1)S(1)} %add_convert_fusion.4), channel_id=1, source_target_pairs={{0,1},{1,2},{2,3},{3,0},{4,5},{5,6},{6,7},{7,4},{8,9},{9,10},{10,1... | collective-permute-start | bytes 2555912 | tf_op jit(solution)/shard_map/ppermute | solution.py:866
  474.1 33.3 %collective-permute-start.15 = (bf16[256,1664]{1,0:T(8,128)(2,1)}, bf16[256,1664]{1,0:T(8,128)(2,1)}, u32[]{:S(2)}, u32[]{:S(2)}) collective-permute-start(bf16[256,1664]{1,0:T(8,128)(2,1)} %add_convert_fusion.3), channel_id=1, source_target_pairs={{0,1},{1,2},{2,3},{3,0},{4,5},{5,6},{6,7},{7,4},{8,9},{9,10},{10,1... | collective-permute-start | bytes 2555912 | tf_op jit(solution)/shard_map/ppermute | solution.py:866
  507.4 307.2 %all-reduce.3.cloned.1.call-start = ((), (), s32[]{:S(2)}) async-start(), calls=%async_computation.9 | async-start | bytes 3244032 | tf_op jit(solution)/shard_map/psum | solution.py:1083
  507.5 32.4 %collective-permute-start.11 = (bf16[2,256,512]{2,1,0:T(8,128)(2,1)}, bf16[2,256,512]{2,1,0:T(8,128)(2,1)S(1)}, u32[]{:S(2)}, u32[]{:S(2)}) collective-permute-start(bf16[2,256,512]{2,1,0:T(8,128)(2,1)} %get-tuple-element.241), channel_id=1, source_target_pairs={{1,0},{2,1},{3,2},{5,4},{6,5},{7,6},{9,8},{10,9},{11,10},{13,12},{... | collective-permute-start | bytes 1572872 | tf_op jit(solution)/shard_map/ppermute | solution.py:868
  512.2 41.1 %collective-permute-start.17 = (bf16[256,1536]{1,0:T(8,128)(2,1)S(1)}, bf16[256,1536]{1,0:T(8,128)(2,1)}, u32[]{:S(2)}, u32[]{:S(2)}) collective-permute-start(bf16[256,1536]{1,0:T(8,128)(2,1)S(1)} %constant_dynamic-slice_fusion.1), channel_id=1, source_target_pairs={{0,1},{1,2},{2,3},{3,0},{4,5},{5,6},{6,7},{7,4},{8,9},{9,10},{10,1... | collective-permute-start | bytes 2359304 | tf_op jit(solution)/shard_map/ppermute | solution.py:866
  554.8 25.8 %collective-permute-start.19 = (bf16[2,256,512]{2,1,0:T(8,128)(2,1)S(1)}, bf16[2,256,512]{2,1,0:T(8,128)(2,1)S(1)}, u32[]{:S(2)}, u32[]{:S(2)}) collective-permute-start(bf16[2,256,512]{2,1,0:T(8,128)(2,1)S(1)} %add_convert_fusion.18), channel_id=1, source_target_pairs={{1,0},{2,1},{3,2},{5,4},{6,5},{7,6},{9,8},{10,9},{11,10},{13,12},{... | collective-permute-start | bytes 1572872 | tf_op jit(solution)/shard_map/ppermute | solution.py:868
  582.8 60.6 %collective-permute-start.23 = (bf16[5,384,512]{2,1,0:T(8,128)(2,1)}, bf16[5,384,512]{2,1,0:T(8,128)(2,1)}, u32[]{:S(2)}, u32[]{:S(2)}) collective-permute-start(bf16[5,384,512]{2,1,0:T(8,128)(2,1)} %get-tuple-element.307), channel_id=1, source_target_pairs={{0,8},{4,12},{8,0},{12,4},{16,24},{20,28},{24,16},{28,20},{1,9},{5... | collective-permute-start | bytes 5898248 | tf_op jit(solution)/shard_map/ppermute | solution.py:873
  583.8 59.6 %collective-permute-start.24 = (bf16[5,384,512]{2,1,0:T(8,128)(2,1)}, bf16[5,384,512]{2,1,0:T(8,128)(2,1)}, u32[]{:S(2)}, u32[]{:S(2)}) collective-permute-start(bf16[5,384,512]{2,1,0:T(8,128)(2,1)} %get-tuple-element.309), channel_id=1, source_target_pairs={{0,16},{4,20},{8,24},{12,28},{16,0},{20,4},{24,8},{28,12},{1,17},{... | collective-permute-start | bytes 5898248 | tf_op jit(solution)/shard_map/ppermute | solution.py:873
  615.1 28.3 %collective-permute-start.22 = (bf16[256,1536]{1,0:T(8,128)(2,1)}, bf16[256,1536]{1,0:T(8,128)(2,1)}, u32[]{:S(2)}, u32[]{:S(2)}) collective-permute-start(bf16[256,1536]{1,0:T(8,128)(2,1)} %add_convert_fusion.12), channel_id=1, source_target_pairs={{0,1},{1,2},{2,3},{3,0},{4,5},{5,6},{6,7},{7,4},{8,9},{9,10},{10,1... | collective-permute-start | bytes 2359304 | tf_op jit(solution)/shard_map/ppermute | solution.py:866
  645.5 23.6 %collective-permute-start.27 = (bf16[256,1536]{1,0:T(8,128)(2,1)}, bf16[256,1536]{1,0:T(8,128)(2,1)}, u32[]{:S(2)}, u32[]{:S(2)}) collective-permute-start(bf16[256,1536]{1,0:T(8,128)(2,1)} %constant_dynamic-slice_fusion), channel_id=1, source_target_pairs={{0,1},{1,2},{2,3},{3,0},{4,5},{5,6},{6,7},{7,4},{8,9},{9,10},{10,1... | collective-permute-start | bytes 2359304 | tf_op jit(solution)/shard_map/ppermute | solution.py:866
  666.6 41.0 %collective-permute-start.29 = (bf16[1,384,2304]{2,1,0:T(8,128)(2,1)}, bf16[1,384,2304]{2,1,0:T(8,128)(2,1)}, u32[]{:S(2)}, u32[]{:S(2)}) collective-permute-start(bf16[1,384,2304]{2,1,0:T(8,128)(2,1)} %get-tuple-element.328), channel_id=1, source_target_pairs={{0,8},{4,12},{8,0},{12,4},{16,24},{20,28},{24,16},{28,20},{1,9},{5... | collective-permute-start | bytes 5308424 | tf_op jit(solution)/shard_map/ppermute | solution.py:873
  668.1 34.3 %collective-permute-start.30 = (bf16[1,384,1920]{2,1,0:T(8,128)(2,1)}, bf16[1,384,1920]{2,1,0:T(8,128)(2,1)S(1)}, u32[]{:S(2)}, u32[]{:S(2)}) collective-permute-start(bf16[1,384,1920]{2,1,0:T(8,128)(2,1)} %get-tuple-element.330), channel_id=1, source_target_pairs={{0,16},{4,20},{8,24},{12,28},{16,0},{20,4},{24,8},{28,12},{1,17},{... | collective-permute-start | bytes 4423688 | tf_op jit(solution)/shard_map/ppermute | solution.py:873
  671.3 22.6 %collective-permute-start.28 = (bf16[256,1536]{1,0:T(8,128)(2,1)}, bf16[256,1536]{1,0:T(8,128)(2,1)}, u32[]{:S(2)}, u32[]{:S(2)}) collective-permute-start(bf16[256,1536]{1,0:T(8,128)(2,1)} %add_convert_fusion.8), channel_id=1, source_target_pairs={{0,1},{1,2},{2,3},{3,0},{4,5},{5,6},{6,7},{7,4},{8,9},{9,10},{10,1... | collective-permute-start | bytes 2359304 | tf_op jit(solution)/shard_map/ppermute | solution.py:866
  674.1 48.4 %collective-permute-start.25 = (bf16[256,1536]{1,0:T(8,128)(2,1)}, bf16[256,1536]{1,0:T(8,128)(2,1)}, u32[]{:S(2)}, u32[]{:S(2)}) collective-permute-start(bf16[256,1536]{1,0:T(8,128)(2,1)} %add_convert_fusion.11), channel_id=1, source_target_pairs={{0,1},{1,2},{2,3},{3,0},{4,5},{5,6},{6,7},{7,4},{8,9},{9,10},{10,1... | collective-permute-start | bytes 2359304 | tf_op jit(solution)/shard_map/ppermute | solution.py:866
  713.7 23.1 %collective-permute-start.32 = (bf16[1,192,2304]{2,1,0:T(8,128)(2,1)}, bf16[1,192,2304]{2,1,0:T(8,128)(2,1)S(1)}, u32[]{:S(2)}, u32[]{:S(2)}) collective-permute-start(bf16[1,192,2304]{2,1,0:T(8,128)(2,1)} %get-tuple-element.339), channel_id=1, source_target_pairs={{0,16},{4,20},{8,24},{12,28},{16,0},{20,4},{24,8},{28,12},{1,17},{... | collective-permute-start | bytes 2654216 | tf_op jit(solution)/shard_map/ppermute | solution.py:873
  738.9 22.1 %collective-permute-start.34 = (bf16[5,192,512]{2,1,0:T(8,128)(2,1)}, bf16[5,192,512]{2,1,0:T(8,128)(2,1)}, u32[]{:S(2)}, u32[]{:S(2)}) collective-permute-start(bf16[5,192,512]{2,1,0:T(8,128)(2,1)} %get-tuple-element.359), channel_id=1, source_target_pairs={{0,16},{4,20},{8,24},{12,28},{16,0},{20,4},{24,8},{28,12},{1,17},{... | collective-permute-start | bytes 2949128 | tf_op jit(solution)/shard_map/ppermute | solution.py:873
  745.0 21.9 %collective-permute-start.35 = (bf16[5,192,512]{2,1,0:T(8,128)(2,1)}, bf16[5,192,512]{2,1,0:T(8,128)(2,1)S(1)}, u32[]{:S(2)}, u32[]{:S(2)}) collective-permute-start(bf16[5,192,512]{2,1,0:T(8,128)(2,1)} %get-tuple-element.361), channel_id=1, source_target_pairs={{0,8},{4,12},{8,0},{12,4},{16,24},{20,28},{24,16},{28,20},{1,9},{5... | collective-permute-start | bytes 2949128 | tf_op jit(solution)/shard_map/ppermute | solution.py:873
  (56 other events, 702.0 us)
Sparse Core Ops, SparseCore 0:
  13.5 76.4 all-gather.3
  203.9 69.9 all-gather.5
  276.0 68.5 all-gather.7
  347.4 62.9 reduce-scatter.3
  413.7 109.3 reduce-scatter.5
  525.9 106.8 reduce-scatter.7
  745.1 69.5 all-reduce.2

commit v6 on v5

--- a/solution.py
+++ b/solution.py
@@ -758,8 +758,7 @@
 
     def put(out_ref, slot, block):
         rows = pl.ds(pl.multiple_of(block * step, step), step)
-        total = keep_ref[0, rows, :].astype(F32) + got_ref[0, rows, :].astype(F32)
-        out_ref[0, slot * step : (slot + 1) * step, :] = total.astype(BF)
+        out_ref[0, slot * step : (slot + 1) * step, :] = keep_ref[0, rows, :] + got_ref[0, rows, :]
 
     first = pl.program_id(0) < cut
 
@@ -810,8 +809,7 @@
 def fold_again_kernel(step, place_ref, keep_ref, got_ref, stay_ref, go_ref):
     for out_ref, half in ((stay_ref, place_ref[0]), (go_ref, 1 - place_ref[0])):
         rows = pl.ds(pl.multiple_of(half * step, step), step)
-        total = keep_ref[0, rows, :].astype(F32) + got_ref[0, rows, :].astype(F32)
-        out_ref[0] = total.astype(BF)
+        out_ref[0] = keep_ref[0, rows, :] + got_ref[0, rows, :]
 
 
 def fold_again(place, keep, got):

time: 840 us -> 839 us (level)
  no operation moved by 1% of the time
where the time goes in v6:
time: 839 us; the launch traced here: 827 us
  Pallas kernels  339 us (40%)
  waiting for transfers between devices  321 us (38%)
  starting transfers between devices  61.5 us (7%)
  other arithmetic  49 us (6%)
  local copies, waits for them, and re-layouts  41.1 us (5%)
  between operations  15.4 us (2%)
    ppermute x13, waiting for transfers between devices, local(): ring = lambda a: lax.ppermute(a, 'expert', around)  122 us
    pallas_call x2, Pallas kernels, expert_pass(): pl.pallas_call(expert_kernel, grid_spec=pltpu.PrefetchScalarGridSpec(num_...  76.3 us
    pallas_call x2, Pallas kernels, weight_pass(): pl.pallas_call(partial(weight_kernel, count, products, step), grid_spec=p...  47.6 us
    psum x1, waiting for transfers between devices, local(): dense = split_dense(lax.psum(dense_sum, 'expert'))  45.4 us
    ppermute x8, waiting for transfers between devices, local(): lax.ppermute(a, 'dp', [(i, i ^ bit) for i in range(dp)])  41.6 us
    ppermute x6, waiting for transfers between devices, local(): earlier = lambda a: lax.ppermute(a, 'expert', downward)  35.5 us
    ppermute x6, waiting for transfers between devices, local(): later = lambda a: lax.ppermute(a, 'expert', upward)  34.1 us
    all_gather x3, waiting for transfers between devices, local(): every = lambda a, axis: lax.all_gather(a, axis, axis=0, tiled=True)  32.9 us
  transfers between devices with their start and end apart: 43, of which 28 were waited for; matrix products, arithmetic and copies ran while one was open for 9% of the time, Pallas kernels for 40%

profile of v6, /device:TPU:0, one launch (start us, length us, event | category | flops | bytes accessed | tf_op | source)
XLA Modules:
  0.0 827.3 jit_solution(936836902831864042)
XLA Ops:
  19.3 39.2 %collective-permute-done = bf16[2,256,1664]{1,2,0:T(8,128)(2,1)S(1)} collective-permute-done((bf16[2,256,1664]{1,2,0:T(8,128)(2,1)S(1)}, bf16[2,256,1664]{1,2,0:T(8,128)(2,1)S(1)}, u32[]{:S(2)}, u32[]{:S(2)}) %collective-permute-start) | collective-permute-done | bytes 1703968 | tf_op jit(solution)/shard_map/ppermute | solution.py:864
  60.1 38.6 %collective-permute-done.1 = bf16[2,256,1664]{1,2,0:T(8,128)(2,1)S(1)} collective-permute-done((bf16[2,256,1664]{1,2,0:T(8,128)(2,1)S(1)}, bf16[2,256,1664]{1,2,0:T(8,128)(2,1)S(1)}, u32[]{:S(2)}, u32[]{:S(2)}) %collective-permute-start.1) | collective-permute-done | bytes 1703968 | tf_op jit(solution)/shard_map/ppermute | solution.py:864
  110.4 11.1 %collective-permute-done.2 = bf16[256,1664]{0,1:T(8,128)(2,1)} collective-permute-done((bf16[256,1664]{0,1:T(8,128)(2,1)}, bf16[256,1664]{0,1:T(8,128)(2,1)}, u32[]{:S(2)}, u32[]{:S(2)}) %collective-permute-start.2) | collective-permute-done | bytes 852000 | tf_op jit(solution)/shard_map/ppermute | solution.py:864
  122.8 9.3 %collective-permute-done.3.refs_1_.refs_5_ = bf16[256,1024]{1,0:T(8,128)(2,1)S(1)} collective-permute-done((bf16[256,1024]{1,0:T(8,128)(2,1)}, bf16[256,1024]{1,0:T(8,128)(2,1)S(1)}, u32[]{:S(2)}, u32[]{:S(2)}) %collective-permute-start.3) | collective-permute-done | bytes 524320 | tf_op jit(solution)/shard_map/ppermute | solution.py:865
  136.4 8.1 collective-permute-done.4.refs_2_.refs_6_
  148.9 7.5 collective-permute-done.5.refs_3_.refs_7_
  161.9 7.8 project.3
  251.7 22.1 %all-gather.6.cloned.1.call-done.rows_ref = bf16[1024,1664]{1,0:T(8,128)(2,1)} async-done(((bf16[256,1664]{1,0:T(8,128)(2,1)}), bf16[1024,1664]{1,0:T(8,128)(2,1)}) %all-gather.6.cloned.1.call-update) | async-done | bytes 3407888 | tf_op jit(solution)/shard_map/all_gather | solution.py:868
  280.9 38.1 %experts.2 = (bf16[10,256,1536]{2,1,0:T(8,128)(2,1)}, bf16[10,256,1664]{2,1,0:T(8,128)(2,1)}, bf16[10,256,1536]{2,1,0:T(8,128)(2,1)}, bf16[10,256,512]{2,1,0:T(8...) custom-call(s32[1]{0:T(128)} %bitcast.10.rank_ref, ...), custom_call_target="tpu_custom_call" | custom-call | flops 2415919104 | bytes 8650752 | tf_op jit(solution)/shard_map/experts/pallas_call | solution.py:663
  333.9 10.8 %all-gather.8.cloned.1.call-done.rows_ref = bf16[1024,1664]{1,0:T(8,128)(2,1)} async-done(((bf16[256,1664]{1,0:T(8,128)(2,1)}), bf16[1024,1664]{1,0:T(8,128)(2,1)}) %all-gather.8.cloned.1.call-update) | async-done | bytes 3407888 | tf_op jit(solution)/shard_map/all_gather | solution.py:868
  351.7 38.2 %experts.3 = (bf16[10,256,1536]{2,1,0:T(8,128)(2,1)}, bf16[10,256,1664]{2,1,0:T(8,128)(2,1)}, bf16[10,256,1536]{2,1,0:T(8,128)(2,1)}, bf16[10,256,512]{2,1,0:T(8...) custom-call(s32[1]{0:T(128)} %bitcast.10.rank_ref, ...), custom_call_target="tpu_custom_call" | custom-call | flops 2415919104 | bytes 8650752 | tf_op jit(solution)/shard_map/experts/pallas_call | solution.py:663
  390.0 18.9 %expert_weights.2 = bf16[10,512,1536]{2,1,0:T(8,128)(2,1)} custom-call(s32[1]{0:T(128)} %bitcast.9.core_ref, bf16[10,256,512]{2,1,0:T(8,128)(2,1)} %get-tuple-element.208.refs_0_, bf16[10,256,512]{2,1,0:T(8,128)(2,1)} %get-tuple-element.218.refs_1_, bf16[10,256,1536]{2,1,0:T(8,128)(2,1)} %get-tuple-element.219.refs_2_, ...), custom_call_target="tpu_custom_call" | custom-call | flops 805306368 | bytes 3670016 | tf_op jit(solution)/shard_map/expert_weights/pallas_call | solution.py:708
  420.3 28.7 %expert_weights.3 = (bf16[10,768,512]{2,1,0:T(8,128)(2,1)}, bf16[10,768,512]{2,1,0:T(8,128)(2,1)}, bf16[10,768,512]{2,1,0:T(8,128)(2,1)}, bf16[10,768,512]{2,1,0:T(8,128)(2,1)}) custom-call(s32[1]{0:T(128)} %bitcast.9.core_ref, bf16[10,256,1664]{2,1,0:T(8,128)(2,1)} %dispatch.4.x_ref.refs_0_, bf16[10,256,1664]{2,1,0:T(8,128)(2,1)} %dispatch.7.x_ref.refs_1_, ...), custom_call_target="tpu_custom_call" | custom-call | flops 1610612736 | bytes 5767168 | tf_op jit(solution)/shard_map/expert_weights/pallas_call | solution.py:708
  453.3 7.5 home_back.2
  460.9 11.6 %attend_back.2 = (bf16[256,1536]{1,0:T(8,128)(2,1)}, bf16[2,256,512]{2,1,0:T(8,128)(2,1)}, bf16[2,256,512]{2,1,0:T(8,128)(2,1)}, bf16[2,256,512]{2,1,0:T(8,128)(2,1)}, bf16[2,256,512]{2,1,0:T(8,128)(2,1)}) custom-call(s32[1]{0:T(128)} %bitcast.6.place_ref, bf16[256,1536]{1,0:T(8,128)(2,1)} %get-tuple-element.198.q_ref, ...), custom_call_target="tpu_custom_call" | custom-call | flops 1610612736 | bytes 550502 | tf_op jit(solution)/shard_map/attend_back/pallas_call | solution.py:526
  478.4 11.2 %add_convert_fusion = bf16[10,768,512]{2,1,0:T(8,128)(2,1)} fusion(bf16[10,768,512]{2,1,0:T(8,128)(2,1)} %collective-permute-done.14, bf16[10,768,512]{2,1,0:T(8,128)(2,1)} %get-tuple-element.247), kind=kLoop, calls=%fused_computation | loop fusion | flops 15728640 | bytes 23592960 | tf_op jit(solution)/shard_map/convert_element_type | solution.py:867
  489.6 17.8 %collective-permute-done.15 = bf16[256,1664]{1,0:T(8,128)(2,1)} collective-permute-done((bf16[256,1664]{1,0:T(8,128)(2,1)}, bf16[256,1664]{1,0:T(8,128)(2,1)}, u32[]{:S(2)}, u32[]{:S(2)}) %collective-permute-start.15) | collective-permute-done | bytes 852000 | tf_op jit(solution)/shard_map/ppermute | solution.py:864
  515.0 7.5 home_back.3
  522.4 17.5 %collective-permute-done.11 = bf16[2,256,512]{2,1,0:T(8,128)(2,1)S(1)} collective-permute-done((bf16[2,256,512]{2,1,0:T(8,128)(2,1)}, bf16[2,256,512]{2,1,0:T(8,128)(2,1)S(1)}, u32[]{:S(2)}, u32[]{:S(2)}) %collective-permute-start.11) | collective-permute-done | bytes 524320 | tf_op jit(solution)/shard_map/ppermute | solution.py:866
  541.6 11.7 %attend_back.3 = (bf16[256,1536]{1,0:T(8,128)(2,1)}, bf16[2,256,512]{2,1,0:T(8,128)(2,1)}, bf16[2,256,512]{2,1,0:T(8,128)(2,1)}, bf16[2,256,512]{2,1,0:T(8,128)(2,1)}, bf16[2,256,512]{2,1,0:T(8,128)(2,1)}) custom-call(s32[1]{0:T(128)} %bitcast.6.place_ref, bf16[256,1536]{1,0:T(8,128)(2,1)} %get-tuple-element.209.q_ref, ...), custom_call_target="tpu_custom_call" | custom-call | flops 1610612736 | bytes 550502 | tf_op jit(solution)/shard_map/attend_back/pallas_call | solution.py:526
  556.7 12.1 %fold.2 = (bf16[5,384,512]{2,1,0:T(8,128)(2,1)}, bf16[5,384,512]{2,1,0:T(8,128)(2,1)}, bf16[5,384,512]{2,1,0:T(8,128)(2,1)}, bf16[5,384,512]{2,1,0:T(8,128)(2,1)}) custom-call(s32[2]{0:T(128)} %pad_add_fusion.place_ref, bf16[10,768,512]{2,1,0:T(8,128)(2,1)} %get-tuple-element.271.keep_ref, bf16[10,768,512]{2,1,0:T(8,128)(2,1)} %collective-permute-done.13.got_ref), custom_call_target="tpu_custom_call" | custom-call | flops 393216 | bytes 2359296 | tf_op jit(solution)/shard_map/fold/pallas_call | solution.py:792
  571.5 9.1 %collective-permute-done.19 = bf16[2,256,512]{2,1,0:T(8,128)(2,1)S(1)} collective-permute-done((bf16[2,256,512]{2,1,0:T(8,128)(2,1)S(1)}, bf16[2,256,512]{2,1,0:T(8,128)(2,1)S(1)}, u32[]{:S(2)}, u32[]{:S(2)}) %collective-permute-start.19) | collective-permute-done | bytes 524320 | tf_op jit(solution)/shard_map/ppermute | solution.py:866
  586.8 10.2 %last_back.2 = (f32[256,1536]{1,0:T(8,128)}, bf16[256,1024]{1,0:T(8,128)(2,1)}, f32[1,1536]{1,0:T(1,128)}) custom-call(bf16[256,1536]{1,0:T(8,128)(2,1)} %get-tuple-element.251.dq_ref.refs_2_, bf16[2,256,512]{2,1,0:T(8,128)(2,1)} %add_convert_fusion.16.dkv_ref, f32[256,128]{1,0:T(8,128)} %get-tuple-element.457.cosine_ref, ...), custom_call_target="tpu_custom_call" | custom-call | flops 201326592 | bytes 1415577 | tf_op jit(solution)/shard_map/last_back/pallas_call | solution.py:303
  615.9 8.9 %last_back.3 = (f32[256,1536]{1,0:T(8,128)}, bf16[256,1024]{1,0:T(8,128)(2,1)}, f32[1,1536]{1,0:T(1,128)}) custom-call(bf16[256,1536]{1,0:T(8,128)(2,1)} %get-tuple-element.270.dq_ref.refs_3_, bf16[2,256,512]{2,1,0:T(8,128)(2,1)} %add_convert_fusion.14.dkv_ref, f32[256,128]{1,0:T(8,128)} %get-tuple-element.457.cosine_ref, ...), custom_call_target="tpu_custom_call" | custom-call | flops 201326592 | bytes 1415577 | tf_op jit(solution)/shard_map/last_back/pallas_call | solution.py:303
  629.0 13.3 %dense_grads.1 = (bf16[768,4224]{1,0:T(8,128)(2,1)}, bf16[768,4224]{1,0:T(8,128)(2,1)}) custom-call(s32[1]{0:T(128)} %bitcast.9.core_ref, bf16[512,1536]{1,0:T(8,128)(2,1)} %get-tuple-element.194.normed_ref.refs_0_.refs_1_, bf16[512,1536]{1,0:T(8,128)(2,1)} %get-tuple-element.194.normed_ref.refs_0_.refs_1_, ...), custom_call_target="tpu_custom_call" | custom-call | flops 664377728 | bytes 2477260 | tf_op jit(solution)/shard_map/dense_grads/pallas_call | solution.py:370
  645.3 7.9 collective-permute-done.26
  653.3 12.0 %fold.3 = (bf16[1,384,2304]{2,1,0:T(8,128)(2,1)}, bf16[1,384,2304]{2,1,0:T(8,128)(2,1)}, bf16[1,384,1920]{2,1,0:T(8,128)(2,1)}, bf16[1,384,1920]{2,1,0:T(8,128)(2,1)}) custom-call(s32[2]{0:T(128)} %pad_add_fusion.place_ref, bf16[1,768,4224]{2,1,0:T(8,128)(2,1)} %bitcast.66, bf16[1,768,4224]{2,1,0:T(8,128)(2,1)} %bitcast.25.got_ref), custom_call_target="tpu_custom_call" | custom-call | flops 324403 | bytes 1946419 | tf_op jit(solution)/shard_map/fold/pallas_call | solution.py:792
  682.4 10.2 %collective-permute-done.28 = bf16[256,1536]{1,0:T(8,128)(2,1)} collective-permute-done((bf16[256,1536]{1,0:T(8,128)(2,1)}, bf16[256,1536]{1,0:T(8,128)(2,1)}, u32[]{:S(2)}, u32[]{:S(2)}) %collective-permute-start.28) | collective-permute-done | bytes 786464 | tf_op jit(solution)/shard_map/ppermute | solution.py:864
  692.6 8.2 collective-permute-done.30.got_ref
  721.2 11.7 %collective-permute-done.33 = bf16[1,192,1920]{2,1,0:T(8,128)(2,1)S(1)} collective-permute-done((bf16[1,192,1920]{2,1,0:T(8,128)(2,1)}, bf16[1,192,1920]{2,1,0:T(8,128)(2,1)S(1)}, u32[]{:S(2)}, u32[]{:S(2)}) %collective-permute-start.33) | collective-permute-done | bytes 737312 | tf_op jit(solution)/shard_map/ppermute | solution.py:871
  747.6 11.9 %collective-permute-done.34 = bf16[5,192,512]{2,1,0:T(8,128)(2,1)} collective-permute-done((bf16[5,192,512]{2,1,0:T(8,128)(2,1)}, bf16[5,192,512]{2,1,0:T(8,128)(2,1)}, u32[]{:S(2)}, u32[]{:S(2)}) %collective-permute-start.34) | collective-permute-done | bytes 983072 | tf_op jit(solution)/shard_map/ppermute | solution.py:871
  768.1 45.4 %all-reduce.3.cloned.1.call-done.sums_ref = bf16[192,4224]{1,0:T(8,128)(2,1)} async-done(((bf16[192,4224]{1,0:T(8,128)(2,1)}), bf16[192,4224]{1,0:T(8,128)(2,1)}) %all-reduce.3.cloned.1.call-update) | async-done | bytes 1622032 | tf_op jit(solution)/shard_map/psum | solution.py:1081
  (260 shorter events, 287.7 us)
Async XLA Ops:
  7.2 93.0 %all-gather.4.cloned.1.call-start = ((), (), s32[]{:S(2)}) async-start(), calls=%async_computation.3 | async-start | bytes 14598144 | tf_op jit(solution)/shard_map/all_gather | solution.py:868
  13.4 260.4 %all-gather.6.cloned.1.call-start = ((), (), s32[]{:S(2)}) async-start(), calls=%async_computation.4 | async-start | bytes 4259840 | tf_op jit(solution)/shard_map/all_gather | solution.py:868
  16.2 42.2 %collective-permute-start = (bf16[2,256,1664]{1,2,0:T(8,128)(2,1)S(1)}, bf16[2,256,1664]{1,2,0:T(8,128)(2,1)S(1)}, u32[]{:S(2)}, u32[]{:S(2)}) collective-permute-start(bf16[2,256,1664]{1,2,0:T(8,128)(2,1)S(1)} %maximum_maximum_fusion), channel_id=1, source_target_pairs={{0,1},{1,2},{2,3},{3,0},{4,5},{5,6},{6,7},{7,4},{8,9},{9,10},{10,1... | collective-permute-start | bytes 5111816 | tf_op jit(solution)/shard_map/ppermute | solution.py:864
  58.5 40.2 %collective-permute-start.1 = (bf16[2,256,1664]{1,2,0:T(8,128)(2,1)S(1)}, bf16[2,256,1664]{1,2,0:T(8,128)(2,1)S(1)}, u32[]{:S(2)}, u32[]{:S(2)}) collective-permute-start(bf16[2,256,1664]{1,2,0:T(8,128)(2,1)S(1)} %collective-permute-done), channel_id=1, source_target_pairs={{0,1},{1,2},{2,3},{3,0},{4,5},{5,6},{6,7},{7,4},{8,9},{9,10},{10,1... | collective-permute-start | bytes 5111816 | tf_op jit(solution)/shard_map/ppermute | solution.py:864
  100.1 21.3 %collective-permute-start.2 = (bf16[256,1664]{0,1:T(8,128)(2,1)}, bf16[256,1664]{0,1:T(8,128)(2,1)}, u32[]{:S(2)}, u32[]{:S(2)}) collective-permute-start(bf16[256,1664]{0,1:T(8,128)(2,1)} %get-tuple-element.443), channel_id=1, source_target_pairs={{0,1},{1,2},{2,3},{3,0},{4,5},{5,6},{6,7},{7,4},{8,9},{9,10},{10,1... | collective-permute-start | bytes 2555912 | tf_op jit(solution)/shard_map/ppermute | solution.py:864
  160.8 30.5 %collective-permute-start.8 = (bf16[256,1664]{0,1:T(8,128)(2,1)}, bf16[256,1664]{0,1:T(8,128)(2,1)S(1)}, u32[]{:S(2)}, u32[]{:S(2)}) collective-permute-start(bf16[256,1664]{0,1:T(8,128)(2,1)} %get-tuple-element.197), channel_id=1, source_target_pairs={{0,1},{1,2},{2,3},{3,0},{4,5},{5,6},{6,7},{7,4},{8,9},{9,10},{10,1... | collective-permute-start | bytes 2555912 | tf_op jit(solution)/shard_map/ppermute | solution.py:864
  173.5 23.4 %collective-permute-start.7 = (bf16[256,1024]{1,0:T(8,128)(2,1)S(1)}, bf16[256,1024]{1,0:T(8,128)(2,1)}, u32[]{:S(2)}, u32[]{:S(2)}) collective-permute-start(bf16[256,1024]{1,0:T(8,128)(2,1)S(1)} %collective-permute-done.6.refs_1_.refs_5_), channel_id=1, source_target_pairs={{0,1},{1,2},{2,3},{4,5},{5,6},{6,7},{8,9},{9,10},{10,11},{12,13},{... | collective-permute-start | bytes 1572872 | tf_op jit(solution)/shard_map/ppermute | solution.py:865
  203.8 140.9 %all-gather.8.cloned.1.call-start = ((), (), s32[]{:S(2)}) async-start(), calls=%async_computation.5 | async-start | bytes 4259840 | tf_op jit(solution)/shard_map/all_gather | solution.py:868
  208.6 28.8 %collective-permute-start.9 = (bf16[256,1024]{1,0:T(8,128)(2,1)}, bf16[256,1024]{1,0:T(8,128)(2,1)}, u32[]{:S(2)}, u32[]{:S(2)}) collective-permute-start(bf16[256,1024]{1,0:T(8,128)(2,1)} %collective-permute-done.7.refs_2_.refs_6_), channel_id=1, source_target_pairs={{0,1},{1,2},{2,3},{4,5},{5,6},{6,7},{8,9},{9,10},{10,11},{12,13},{... | collective-permute-start | bytes 1572872 | tf_op jit(solution)/shard_map/ppermute | solution.py:865
  251.7 158.7 %reduce-scatter.4.cloned.1.call-start = ((), (), s32[]{:S(2)}) async-start(), calls=%async_computation.6 | async-start | bytes 4259840 | tf_op jit(solution)/shard_map/reduce_scatter | solution.py:984
  326.5 226.9 %reduce-scatter.6.cloned.1.call-start = ((), (), s32[]{:S(2)}) async-start(), calls=%async_computation.7 | async-start | bytes 17694720 | tf_op jit(solution)/shard_map/reduce_scatter | solution.py:993
  410.4 234.9 %reduce-scatter.8.cloned.1.call-start = ((), (), s32[]{:S(2)}) async-start(), calls=%async_computation.8 | async-start | bytes 9830400 | tf_op jit(solution)/shard_map/reduce_scatter | solution.py:877
  419.1 29.9 %collective-permute-start.10 = (bf16[256,1664]{1,0:T(8,128)(2,1)S(1)}, bf16[256,1664]{1,0:T(8,128)(2,1)S(1)}, u32[]{:S(2)}, u32[]{:S(2)}) collective-permute-start(bf16[256,1664]{1,0:T(8,128)(2,1)S(1)} %constant_dynamic-slice_fusion.2), channel_id=1, source_target_pairs={{0,1},{1,2},{2,3},{3,0},{4,5},{5,6},{6,7},{7,4},{8,9},{9,10},{10,1... | collective-permute-start | bytes 2555912 | tf_op jit(solution)/shard_map/ppermute | solution.py:864
  449.0 23.7 %collective-permute-start.13 = (bf16[10,768,512]{2,1,0:T(8,128)(2,1)}, bf16[10,768,512]{2,1,0:T(8,128)(2,1)}, u32[]{:S(2)}, u32[]{:S(2)}) collective-permute-start(bf16[10,768,512]{2,1,0:T(8,128)(2,1)} %get-tuple-element.243), channel_id=1, source_target_pairs={{0,4},{4,0},{8,12},{12,8},{16,20},{20,16},{24,28},{28,24},{1,5},{5... | collective-permute-start | bytes 23592968 | tf_op jit(solution)/shard_map/ppermute | solution.py:869
  449.0 24.0 %collective-permute-start.14 = (bf16[10,768,512]{2,1,0:T(8,128)(2,1)}, bf16[10,768,512]{2,1,0:T(8,128)(2,1)}, u32[]{:S(2)}, u32[]{:S(2)}) collective-permute-start(bf16[10,768,512]{2,1,0:T(8,128)(2,1)} %get-tuple-element.244), channel_id=1, source_target_pairs={{0,4},{4,0},{8,12},{12,8},{16,20},{20,16},{24,28},{28,24},{1,5},{5... | collective-permute-start | bytes 23592968 | tf_op jit(solution)/shard_map/ppermute | solution.py:869
  449.8 23.0 %collective-permute-start.12 = (bf16[256,1664]{1,0:T(8,128)(2,1)S(1)}, bf16[256,1664]{1,0:T(8,128)(2,1)S(1)}, u32[]{:S(2)}, u32[]{:S(2)}) collective-permute-start(bf16[256,1664]{1,0:T(8,128)(2,1)S(1)} %add_convert_fusion.4), channel_id=1, source_target_pairs={{0,1},{1,2},{2,3},{3,0},{4,5},{5,6},{6,7},{7,4},{8,9},{9,10},{10,1... | collective-permute-start | bytes 2555912 | tf_op jit(solution)/shard_map/ppermute | solution.py:864
  474.1 33.3 %collective-permute-start.15 = (bf16[256,1664]{1,0:T(8,128)(2,1)}, bf16[256,1664]{1,0:T(8,128)(2,1)}, u32[]{:S(2)}, u32[]{:S(2)}) collective-permute-start(bf16[256,1664]{1,0:T(8,128)(2,1)} %add_convert_fusion.3), channel_id=1, source_target_pairs={{0,1},{1,2},{2,3},{3,0},{4,5},{5,6},{6,7},{7,4},{8,9},{9,10},{10,1... | collective-permute-start | bytes 2555912 | tf_op jit(solution)/shard_map/ppermute | solution.py:864
  507.4 306.1 %all-reduce.3.cloned.1.call-start = ((), (), s32[]{:S(2)}) async-start(), calls=%async_computation.9 | async-start | bytes 3244032 | tf_op jit(solution)/shard_map/psum | solution.py:1081
  507.5 32.4 %collective-permute-start.11 = (bf16[2,256,512]{2,1,0:T(8,128)(2,1)}, bf16[2,256,512]{2,1,0:T(8,128)(2,1)S(1)}, u32[]{:S(2)}, u32[]{:S(2)}) collective-permute-start(bf16[2,256,512]{2,1,0:T(8,128)(2,1)} %get-tuple-element.241), channel_id=1, source_target_pairs={{1,0},{2,1},{3,2},{5,4},{6,5},{7,6},{9,8},{10,9},{11,10},{13,12},{... | collective-permute-start | bytes 1572872 | tf_op jit(solution)/shard_map/ppermute | solution.py:866
  512.2 41.1 %collective-permute-start.17 = (bf16[256,1536]{1,0:T(8,128)(2,1)S(1)}, bf16[256,1536]{1,0:T(8,128)(2,1)}, u32[]{:S(2)}, u32[]{:S(2)}) collective-permute-start(bf16[256,1536]{1,0:T(8,128)(2,1)S(1)} %constant_dynamic-slice_fusion.1), channel_id=1, source_target_pairs={{0,1},{1,2},{2,3},{3,0},{4,5},{5,6},{6,7},{7,4},{8,9},{9,10},{10,1... | collective-permute-start | bytes 2359304 | tf_op jit(solution)/shard_map/ppermute | solution.py:864
  554.8 25.8 %collective-permute-start.19 = (bf16[2,256,512]{2,1,0:T(8,128)(2,1)S(1)}, bf16[2,256,512]{2,1,0:T(8,128)(2,1)S(1)}, u32[]{:S(2)}, u32[]{:S(2)}) collective-permute-start(bf16[2,256,512]{2,1,0:T(8,128)(2,1)S(1)} %add_convert_fusion.18), channel_id=1, source_target_pairs={{1,0},{2,1},{3,2},{5,4},{6,5},{7,6},{9,8},{10,9},{11,10},{13,12},{... | collective-permute-start | bytes 1572872 | tf_op jit(solution)/shard_map/ppermute | solution.py:866
  582.8 59.6 %collective-permute-start.23 = (bf16[5,384,512]{2,1,0:T(8,128)(2,1)}, bf16[5,384,512]{2,1,0:T(8,128)(2,1)}, u32[]{:S(2)}, u32[]{:S(2)}) collective-permute-start(bf16[5,384,512]{2,1,0:T(8,128)(2,1)} %get-tuple-element.307), channel_id=1, source_target_pairs={{0,8},{4,12},{8,0},{12,4},{16,24},{20,28},{24,16},{28,20},{1,9},{5... | collective-permute-start | bytes 5898248 | tf_op jit(solution)/shard_map/ppermute | solution.py:871
  583.8 58.6 %collective-permute-start.24 = (bf16[5,384,512]{2,1,0:T(8,128)(2,1)}, bf16[5,384,512]{2,1,0:T(8,128)(2,1)}, u32[]{:S(2)}, u32[]{:S(2)}) collective-permute-start(bf16[5,384,512]{2,1,0:T(8,128)(2,1)} %get-tuple-element.309), channel_id=1, source_target_pairs={{0,16},{4,20},{8,24},{12,28},{16,0},{20,4},{24,8},{28,12},{1,17},{... | collective-permute-start | bytes 5898248 | tf_op jit(solution)/shard_map/ppermute | solution.py:871
  614.2 28.1 %collective-permute-start.22 = (bf16[256,1536]{1,0:T(8,128)(2,1)}, bf16[256,1536]{1,0:T(8,128)(2,1)}, u32[]{:S(2)}, u32[]{:S(2)}) collective-permute-start(bf16[256,1536]{1,0:T(8,128)(2,1)} %add_convert_fusion.12), channel_id=1, source_target_pairs={{0,1},{1,2},{2,3},{3,0},{4,5},{5,6},{6,7},{7,4},{8,9},{9,10},{10,1... | collective-permute-start | bytes 2359304 | tf_op jit(solution)/shard_map/ppermute | solution.py:864
  644.6 23.2 %collective-permute-start.27 = (bf16[256,1536]{1,0:T(8,128)(2,1)}, bf16[256,1536]{1,0:T(8,128)(2,1)}, u32[]{:S(2)}, u32[]{:S(2)}) collective-permute-start(bf16[256,1536]{1,0:T(8,128)(2,1)} %constant_dynamic-slice_fusion), channel_id=1, source_target_pairs={{0,1},{1,2},{2,3},{3,0},{4,5},{5,6},{6,7},{7,4},{8,9},{9,10},{10,1... | collective-permute-start | bytes 2359304 | tf_op jit(solution)/shard_map/ppermute | solution.py:864
  665.2 41.0 %collective-permute-start.29 = (bf16[1,384,2304]{2,1,0:T(8,128)(2,1)}, bf16[1,384,2304]{2,1,0:T(8,128)(2,1)}, u32[]{:S(2)}, u32[]{:S(2)}) collective-permute-start(bf16[1,384,2304]{2,1,0:T(8,128)(2,1)} %get-tuple-element.328), channel_id=1, source_target_pairs={{0,8},{4,12},{8,0},{12,4},{16,24},{20,28},{24,16},{28,20},{1,9},{5... | collective-permute-start | bytes 5308424 | tf_op jit(solution)/shard_map/ppermute | solution.py:871
  666.5 34.3 %collective-permute-start.30 = (bf16[1,384,1920]{2,1,0:T(8,128)(2,1)}, bf16[1,384,1920]{2,1,0:T(8,128)(2,1)S(1)}, u32[]{:S(2)}, u32[]{:S(2)}) collective-permute-start(bf16[1,384,1920]{2,1,0:T(8,128)(2,1)} %get-tuple-element.330), channel_id=1, source_target_pairs={{0,16},{4,20},{8,24},{12,28},{16,0},{20,4},{24,8},{28,12},{1,17},{... | collective-permute-start | bytes 4423688 | tf_op jit(solution)/shard_map/ppermute | solution.py:871
  670.0 22.6 %collective-permute-start.28 = (bf16[256,1536]{1,0:T(8,128)(2,1)}, bf16[256,1536]{1,0:T(8,128)(2,1)}, u32[]{:S(2)}, u32[]{:S(2)}) collective-permute-start(bf16[256,1536]{1,0:T(8,128)(2,1)} %add_convert_fusion.8), channel_id=1, source_target_pairs={{0,1},{1,2},{2,3},{3,0},{4,5},{5,6},{6,7},{7,4},{8,9},{9,10},{10,1... | collective-permute-start | bytes 2359304 | tf_op jit(solution)/shard_map/ppermute | solution.py:864
  672.8 48.4 %collective-permute-start.25 = (bf16[256,1536]{1,0:T(8,128)(2,1)}, bf16[256,1536]{1,0:T(8,128)(2,1)}, u32[]{:S(2)}, u32[]{:S(2)}) collective-permute-start(bf16[256,1536]{1,0:T(8,128)(2,1)} %add_convert_fusion.11), channel_id=1, source_target_pairs={{0,1},{1,2},{2,3},{3,0},{4,5},{5,6},{6,7},{7,4},{8,9},{9,10},{10,1... | collective-permute-start | bytes 2359304 | tf_op jit(solution)/shard_map/ppermute | solution.py:864
  712.3 22.9 %collective-permute-start.32 = (bf16[1,192,2304]{2,1,0:T(8,128)(2,1)}, bf16[1,192,2304]{2,1,0:T(8,128)(2,1)S(1)}, u32[]{:S(2)}, u32[]{:S(2)}) collective-permute-start(bf16[1,192,2304]{2,1,0:T(8,128)(2,1)} %get-tuple-element.339), channel_id=1, source_target_pairs={{0,16},{4,20},{8,24},{12,28},{16,0},{20,4},{24,8},{28,12},{1,17},{... | collective-permute-start | bytes 2654216 | tf_op jit(solution)/shard_map/ppermute | solution.py:871
  737.4 22.1 %collective-permute-start.34 = (bf16[5,192,512]{2,1,0:T(8,128)(2,1)}, bf16[5,192,512]{2,1,0:T(8,128)(2,1)}, u32[]{:S(2)}, u32[]{:S(2)}) collective-permute-start(bf16[5,192,512]{2,1,0:T(8,128)(2,1)} %get-tuple-element.359), channel_id=1, source_target_pairs={{0,16},{4,20},{8,24},{12,28},{16,0},{20,4},{24,8},{28,12},{1,17},{... | collective-permute-start | bytes 2949128 | tf_op jit(solution)/shard_map/ppermute | solution.py:871
  743.5 21.9 %collective-permute-start.35 = (bf16[5,192,512]{2,1,0:T(8,128)(2,1)}, bf16[5,192,512]{2,1,0:T(8,128)(2,1)S(1)}, u32[]{:S(2)}, u32[]{:S(2)}) collective-permute-start(bf16[5,192,512]{2,1,0:T(8,128)(2,1)} %get-tuple-element.361), channel_id=1, source_target_pairs={{0,8},{4,12},{8,0},{12,4},{16,24},{20,28},{24,16},{28,20},{1,9},{5... | collective-permute-start | bytes 2949128 | tf_op jit(solution)/shard_map/ppermute | solution.py:871
  (56 other events, 697.2 us)
Sparse Core Ops, SparseCore 0:
  13.5 76.4 all-gather.3
  203.9 69.9 all-gather.5
  276.0 68.5 all-gather.7
  347.4 62.9 reduce-scatter.3
  413.7 109.3 reduce-scatter.5
  525.9 106.9 reduce-scatter.7
  743.6 69.8 all-reduce.2
